TPU v7x, 32 devices: a whole 2x2x4 slice. The times are simulated.
32 devices in a mesh: gx: 4 (over y, core), gy: 8 (over z, x).
Axes of the slice: x: 2, y: 2, z: 4, core: 2. Of those that a mesh axis runs over, the one named last changes fastest.
Arguments:
- phase: float32 [32, 64, 256], P('gx', 'gy'), may hold values from -1 to 1
- solute: float32 [32, 64, 256], P('gx', 'gy'), may hold values from 0 to 1
- undercool: float32 [32, 64, 256], P('gx', 'gy'), may hold values from -1 to 1
- lift_weight: float32 [32, 2], replicated, may hold values from -4 to 4
- spectral_weight: float32 [2, 32, 32, 32, 1024], P(None, 'gx', 'gy'), may hold values from -6 to 6
- local_weight: float32 [32, 32], replicated, may hold values from -1 to 1
- local_bias: float32 [32], replicated, may hold values from -4 to 4
- proj_weight: float32 [32], replicated, may hold values from -1 to 1
- cotangent: float32 [32, 64, 256], P('gx', 'gy'), may hold values from -6 to 6
Outputs:
- phase_next: float32 [32, 64, 256], P('gx', 'gy')
- solute_next: float32 [32, 64, 256], P('gx', 'gy')
- predicted: float32 [32, 64, 256], P('gx', 'gy')
- grad_spectral: float32 [2, 32, 32, 32, 1024], P(None, 'gx', 'gy')
- grad_local: float32 [32, 32], replicated
- grad_proj: float32 [32], replicated
All inputs are finite; a program needn't handle non-finite values.
Results may differ from a plain program's by a relative error of at most 0.00029.
Values sent between devices are 32-bit elements; how exact they have to be, the bound alone decides.
No kernel may reach another device: no remote copies, remote signals or barrier semaphores. Data moves between devices by JAX's collectives and lax.ppermute only.
A program may use at most 128 MiB of HBM per device.

v0:
```python
from functools import reduce
import math

import jax
import jax.numpy as jnp
from jax import lax
from jax.sharding import PartitionSpec as P

WIDTH = 32
KX = 32
KY = 32
KZ = 32


TIME_STEP = 0.05
COUPLING = 2.0
SOLID_DIFF = 0.05
LIQUID_DIFF = 1.0
PARTITION = 0.15
TRAP_RATE = 4.0
SOLUTE_MEAN = 0.5


def extended(cells, sides, width):
    for axis, dim in sides:
        count = lax.axis_size(axis)
        head = lax.slice_in_dim(cells, 0, width, axis=dim)
        tail = lax.slice_in_dim(cells, cells.shape[dim] - width, cells.shape[dim], axis=dim)
        cells = jnp.concatenate(
            [
                lax.ppermute(tail, axis, [(i, (i + 1) % count) for i in range(count)]),
                cells,
                lax.ppermute(head, axis, [((i + 1) % count, i) for i in range(count)]),
            ],
            axis=dim,
        )
    return cells


def diffusivity(phase_now):
    return SOLID_DIFF + (LIQUID_DIFF - SOLID_DIFF) * 0.5 * (1.0 - jnp.tanh(phase_now))


def update(phase_now, solute_now, undercool, phase_nb, solute_nb, diff_now, diff_nb):
    lap = reduce(jnp.add, phase_nb) - 6.0 * phase_now
    squares = 1.0 - phase_now * phase_now
    rate = (
        lap
        + phase_now
        - phase_now * phase_now * phase_now
        + COUPLING * squares * squares * (undercool - solute_now)
    )
    fluxes = [
        0.5 * (diff_now + diff_nb[index]) * (solute_nb[index] - solute_now) for index in range(6)
    ]
    divergence = reduce(jnp.add, fluxes)
    speed = TRAP_RATE * jnp.abs(rate)
    keff = (PARTITION + speed) / (1.0 + speed)
    phase_new = phase_now + TIME_STEP * rate
    solute_new = solute_now + TIME_STEP * (divergence + 0.5 * (1.0 - keff) * solute_now * rate)
    return (phase_new, solute_new)


def beside(padded):
    centre = padded[1:-1, 1:-1]
    return [
        padded[2:, 1:-1],
        padded[:-2, 1:-1],
        padded[1:-1, 2:],
        padded[1:-1, :-2],
        jnp.roll(centre, -1, 2),
        jnp.roll(centre, 1, 2),
    ]


def phase_sweep(phase_now, solute_now, undercool):
    padded = extended(jnp.stack([phase_now, solute_now]), (("gx", 1), ("gy", 2)), 1)
    phase_pad = padded[0]
    solute_pad = padded[1]
    diff_pad = diffusivity(phase_pad)
    return update(
        phase_now,
        solute_now,
        undercool,
        beside(phase_pad),
        beside(solute_pad),
        diff_pad[1:-1, 1:-1],
        beside(diff_pad),
    )


def signed_freq(indices, total):
    return jnp.where(indices < total // 2, indices, indices - total)


def wave_tables(freqs, positions, length, factor):
    product = freqs[:, None] * positions[None, :] % length
    angles = product.astype(jnp.float32) * (2.0 * math.pi / length)
    return (jnp.cos(angles) * factor, jnp.sin(angles) * factor)


def complex_mix(cosines, sines, data, pattern, orient):

    def apply(table, values):
        return jnp.einsum(pattern, table, values, precision=lax.Precision.HIGHEST)

    cos_real = apply(cosines, data[0])
    cos_imag = apply(cosines, data[1])
    sin_real = apply(sines, data[0])
    sin_imag = apply(sines, data[1])
    return jnp.stack([cos_real - orient * sin_imag, cos_imag + orient * sin_real])


def x_forward(data, factor):
    portion = lax.all_to_all(data, "gx", split_axis=1, concat_axis=2, tiled=True)
    length = portion.shape[2]
    cosines, sines = wave_tables(
        signed_freq(jnp.arange(KX, dtype=jnp.int32), KX),
        jnp.arange(length, dtype=jnp.int32),
        length,
        factor,
    )
    lines = complex_mix(cosines, sines, portion, "kx,wxyz->wkyz", -1.0)
    return lax.all_to_all(lines, "gx", split_axis=2, concat_axis=1, tiled=True)


def y_forward(data, factor):
    portion = lax.all_to_all(data, "gy", split_axis=1, concat_axis=3, tiled=True)
    length = portion.shape[3]
    cosines, sines = wave_tables(
        signed_freq(jnp.arange(KY, dtype=jnp.int32), KY),
        jnp.arange(length, dtype=jnp.int32),
        length,
        factor,
    )
    lines = complex_mix(cosines, sines, portion, "ky,wayz->wakz", -1.0)
    return lax.all_to_all(lines, "gy", split_axis=3, concat_axis=1, tiled=True)


def contract(weights, values):
    return jnp.einsum("abzoi,iabz->oabz", weights, values, precision=lax.Precision.HIGHEST)


def outer(left, right):
    return jnp.einsum("oabz,iabz->abzoi", left, right, precision=lax.Precision.HIGHEST)


def per_device(
    phase,
    solute,
    undercool,
    lift_weight,
    spectral_weight,
    local_weight,
    local_bias,
    proj_weight,
    cotangent,
):
    phase_mid, solute_mid = phase_sweep(phase, solute, undercool)
    phase_next, solute_next = phase_sweep(phase_mid, solute_mid, undercool)
    cells_x, cells_y, depth = phase.shape
    total_x = cells_x * lax.axis_size("gx")
    total_y = cells_y * lax.axis_size("gy")
    fields = jnp.stack([phase_next, solute_next - SOLUTE_MEAN])
    modes_z = jnp.arange(KZ, dtype=jnp.int32)
    zpos = jnp.arange(depth, dtype=jnp.int32)
    unit_z = jnp.ones((KZ,), jnp.float32)
    weights_z = jnp.where(modes_z == 0, 1.0, 2.0).astype(jnp.float32) / depth

    def z_forward(field, zfactor):
        cosines, sines = wave_tables(modes_z, zpos, depth, zfactor[:, None])
        tables = jnp.stack([cosines, -sines])
        return jnp.einsum("wxyz,rkz->rwxyk", field, tables, precision=lax.Precision.HIGHEST)

    def spectral_forward(field, zfactor, xfactor, yfactor):
        return y_forward(x_forward(z_forward(field, zfactor), xfactor), yfactor)

    lifted = jnp.einsum("wc,cxyz->wxyz", lift_weight, fields, precision=lax.Precision.HIGHEST)
    spectrum = spectral_forward(lifted, unit_z, 1.0, 1.0)
    own_x = spectrum.shape[2]
    own_y = spectrum.shape[3]
    shaped = spectral_weight.reshape(2, own_x, own_y, KZ, WIDTH, WIDTH)
    out_real = contract(shaped[0], spectrum[0]) - contract(shaped[1], spectrum[1])
    out_imag = contract(shaped[0], spectrum[1]) + contract(shaped[1], spectrum[0])
    spectral_out = jnp.stack([out_real, out_imag])
    ypos = lax.axis_index("gy") * cells_y + jnp.arange(cells_y, dtype=jnp.int32)
    portion = lax.all_gather(spectral_out, "gy", axis=3, tiled=True)
    freqs = signed_freq(jnp.arange(portion.shape[3], dtype=jnp.int32), KY)
    cosines, sines = wave_tables(ypos, freqs, total_y, 1.0 / total_y)
    back_y = complex_mix(cosines, sines, portion, "yk,wakz->wayz", 1.0)
    cosines, sines = wave_tables(
        jnp.arange(total_x, dtype=jnp.int32),
        signed_freq(jnp.arange(KX, dtype=jnp.int32), KX),
        total_x,
        1.0 / total_x,
    )
    inverted = complex_mix(
        cosines,
        sines,
        lax.all_to_all(back_y, "gx", split_axis=1, concat_axis=2, tiled=True),
        "xk,wkyz->wxyz",
        1.0,
    )
    back_x = lax.all_to_all(inverted, "gx", split_axis=2, concat_axis=1, tiled=True)
    cos_back, sin_back = wave_tables(modes_z, zpos, depth, weights_z[:, None])
    back_tables = jnp.stack([cos_back, -sin_back])
    spectral_field = jnp.einsum(
        "rwxyk,rkz->wxyz", back_x, back_tables, precision=lax.Precision.HIGHEST
    )
    mixed = jnp.dot(local_weight, lift_weight, precision=lax.Precision.HIGHEST)
    pre_act = (
        spectral_field
        + jnp.einsum("wc,cxyz->wxyz", mixed, fields, precision=lax.Precision.HIGHEST)
        + local_bias[:, None, None, None]
    )
    activated, gelu_back = jax.vjp(jax.nn.gelu, pre_act)
    predicted = jnp.einsum("w,wxyz->xyz", proj_weight, activated, precision=lax.Precision.HIGHEST)
    grad_pre = gelu_back(proj_weight[:, None, None, None] * cotangent[None])[0]
    field_sums = jnp.einsum("wxyz,cxyz->wc", grad_pre, fields, precision=lax.Precision.HIGHEST)
    proj_sums = jnp.einsum("wxyz,xyz->w", activated, cotangent, precision=lax.Precision.HIGHEST)
    field_sums, proj_sums = lax.psum((field_sums, proj_sums), ("gx", "gy"))
    grad_modes = spectral_forward(grad_pre, weights_z, 1.0 / total_x, 1.0 / total_y)
    grad_real = outer(grad_modes[0], spectrum[0]) + outer(grad_modes[1], spectrum[1])
    grad_imag = outer(grad_modes[1], spectrum[0]) - outer(grad_modes[0], spectrum[1])
    grad_spectral = jnp.stack([grad_real, grad_imag]).reshape(2, own_x, own_y, KZ, WIDTH * WIDTH)
    scale = 1.0 / math.sqrt(total_x * total_y * depth)
    grad_local = jnp.dot(field_sums, lift_weight.T, precision=lax.Precision.HIGHEST) * scale
    grad_proj = proj_sums * scale
    return (phase_next, solute_next, predicted, grad_spectral, grad_local, grad_proj)


def solution(mesh):
    return jax.shard_map(
        per_device,
        mesh=mesh,
        in_specs=(
            P("gx", "gy", None),
            P("gx", "gy", None),
            P("gx", "gy", None),
            P(),
            P(None, "gx", "gy", None, None),
            P(),
            P(),
            P(),
            P("gx", "gy", None),
        ),
        out_specs=(
            P("gx", "gy", None),
            P("gx", "gy", None),
            P("gx", "gy", None),
            P(None, "gx", "gy", None, None),
            P(),
            P(),
        ),
        check_vma=False,
    )
```

profile of v0, /device:TPU:0, one launch (start us, length us, event | category | flops | bytes accessed | tf_op | source)
XLA Modules:
  0.0 614.0 jit_solution(5089301524419711944)
XLA Ops:
  15.2 3.1 collective-permute-start.3
  26.4 3.4 collective-permute-start.7
  35.6 6.6 %fusion.28 = f32[2,32,8,8,32]{1,4,3,2,0:T(8,128)} fusion(f32[8,8,256,32]{2,3,1,0:T(8,128)S(1)} %fusion.250, f32[1,32,256]{2,1,0:T(8,128)S(1)} %get-tuple-element.84, f32[1,32,256]{2,1,0:T(8,128)S(1)} %get-tuple-element.83), kind=kOutput, calls=%fused_computation.45 | convolution fusion | flops 402669568 | bytes 2686976 | tf_op jit(solution)/shard_map/wxyz,rkz->rwxyk/dot_general | solution.py:173
  42.1 3.1 copy.140
  46.8 3.6 all-to-all-start
  50.5 8.8 %all-to-all-done = f32[4,1,32768]{2,1,0:T(1,128)S(1)} async-done(((f32[4,1,32768]{2,1,0:T(1,128)}), f32[4,1,32768]{2,1,0:T(1,128)S(1)}, u32[]{:S(2)}, u32[]{:S(2)}) %all-to-all-start) | async-done | bytes 524320 | tf_op jit(solution)/shard_map/all_to_all | solution.py:115
  72.3 3.1 copy.148
  76.3 11.2 %all_to_all.159 = f32[4,1,32768]{2,1,0:T(1,128)S(1)} all-to-all(f32[4,1,32768]{2,1,0:T(1,128)S(1)} %reshape.245), channel_id=1, replica_groups=mesh['gx'=4,'gy'=8] {'gx'}, dimensions={0} | all-to-all | bytes 1048576 | tf_op jit(solution)/shard_map/all_to_all | solution.py:124
  91.9 20.2 %all_to_all.160 = f32[8,1,16384]{2,1,0:T(1,128)S(1)} all-to-all(f32[8,1,16384]{2,1,0:T(1,128)S(1)} %reshape.247), channel_id=1, replica_groups=mesh['gx'=4,'gy'=8] {'gy'}, dimensions={0} | all-to-all | bytes 1048576 | tf_op jit(solution)/shard_map/all_to_all | solution.py:128
  124.7 3.6 all-to-all-start.3
  128.8 8.5 %fusion.375 = (f32[1,8,4,32,1024]{4,3,2,1,0:T(8,128)}, f32[1,8,4,32,1024]{4,3,2,1,0:T(8,128)}) fusion(f32[2,8,4,32,1024]{4,3,2,1,0:T(8,128)} %param.13), kind=kLoop, calls=%fused_computation.466 | loop fusion | bytes 16777216 | tf_op jit(solution)/shard_map/slice | solution.py:183
  137.3 11.6 %squeeze.105 = f32[8,4,32,32,32]{4,3,2,1,0:T(8,128)} reshape(f32[1,8,4,32,1024]{4,3,2,1,0:T(8,128)} %get-tuple-element.22) | data formatting | bytes 8388608 | tf_op jit(solution)/shard_map/squeeze | solution.py:183
  148.9 11.6 %squeeze.107 = f32[8,4,32,32,32]{4,3,2,1,0:T(8,128)} reshape(f32[1,8,4,32,1024]{4,3,2,1,0:T(8,128)} %get-tuple-element.21) | data formatting | bytes 8388608 | tf_op jit(solution)/shard_map/squeeze | solution.py:183
  163.2 21.4 %multiply_reduce_fusion.3 = (f32[8,4,32,32]{3,2,1,0:T(8,128)S(1)}, f32[8,4,32,32]{3,2,1,0:T(8,128)S(1)}, f32[8,4,32,32]{3,2,1,0:T(8,128)S(1)}, f32[8,4,32,32]{3,2,1,0:T(8,128)S(1)}) fusion(f32[8,4,32,32,32]{4,3,2,1,0:T(8,128)} %squeeze.105, f32[8,4,32,32]{3,2,1,0:T(8,128)S(1)} %copy.271, f32[8,4,32,32]{3,2,1,0:T(8,128)S(1)} %copy.272, ...), kind=kLoop, calls=%fused_computation.3 | loop fusion | flops 8257536 | bytes 9175040
  190.8 125.7 %all-gather.2.cloned.1.call-done = f32[2,32,8,32,32]{4,2,1,0,3:T(8,128)} async-done(((f32[2,32,8,4,32]{4,2,1,0,3:T(8,128)}), f32[2,32,8,32,32]{4,2,1,0,3:T(8,128)}) %all-gather.2.cloned.1.call-update) | async-done | bytes 2097168 | tf_op jit(solution)/shard_map/all_gather | solution.py:187
  316.5 4.0 fusion.374
  320.5 4.7 fusion.1
  325.3 4.7 fusion
  329.9 4.9 fusion.32
  334.8 4.7 fusion.34
  341.5 3.9 all-to-all-start.4
  345.4 8.8 %all-to-all-done.4 = f32[4,1,32768]{2,1,0:T(1,128)S(1)} async-done(((f32[4,1,32768]{2,1,0:T(1,128)}), f32[4,1,32768]{2,1,0:T(1,128)S(1)}, u32[]{:S(2)}, u32[]{:S(2)}) %all-to-all-start.4) | async-done | bytes 524320 | tf_op jit(solution)/shard_map/all_to_all | solution.py:200
  354.1 3.0 reduce.12
  370.4 3.1 copy.173
  375.1 3.6 all-to-all-start.5
  379.0 3.2 fusion.370
  382.2 5.3 all-to-all-done.5
  387.5 2.9 reduce.13
  393.8 5.4 fusion.9
  400.6 7.2 %fusion.25 = f32[2,32,8,8,32]{1,4,3,2,0:T(8,128)} fusion(f32[32,8,8,256]{3,2,1,0:T(8,128)S(1)} %get-tuple-element.29, f32[1,32,256]{2,1,0:T(8,128)S(1)} %get-tuple-element.78, f32[1,32,256]{2,1,0:T(8,128)S(1)} %get-tuple-element.77), kind=kOutput, calls=%fused_computation.44 | convolution fusion | flops 402669568 | bytes 2686976 | tf_op jit(solution)/shard_map/wxyz,rkz->rwxyk/dot_general | solution.py:173
  407.8 3.1 copy.178
  412.9 12.3 %all_to_all.161 = f32[4,1,32768]{2,1,0:T(1,128)S(1)} all-to-all(f32[4,1,32768]{2,1,0:T(1,128)} %reshape.255), channel_id=1, replica_groups=mesh['gx'=4,'gy'=8] {'gx'}, dimensions={0} | all-to-all | bytes 1048576 | tf_op jit(solution)/shard_map/all_to_all | solution.py:115
  425.2 3.0 reduce.14
  441.6 3.1 copy.186
  446.3 12.3 %all_to_all.162 = f32[4,1,32768]{2,1,0:T(1,128)S(1)} all-to-all(f32[4,1,32768]{2,1,0:T(1,128)} %reshape.257), channel_id=1, replica_groups=mesh['gx'=4,'gy'=8] {'gx'}, dimensions={0} | all-to-all | bytes 1048576 | tf_op jit(solution)/shard_map/all_to_all | solution.py:124
  458.6 3.0 reduce.15
  465.1 3.3 reshape.259
  468.4 4.3 all-to-all-start.8
  475.5 3.0 fusion.20
  478.5 8.4 %all-to-all-done.8 = f32[8,1,16384]{2,1,0:T(1,128)} async-done(((f32[8,1,16384]{2,1,0:T(1,128)}), f32[8,1,16384]{2,1,0:T(1,128)}, u32[]{:S(2)}, u32[]{:S(2)}) %all-to-all-start.8) | async-done | bytes 524320 | tf_op jit(solution)/shard_map/all_to_all | solution.py:128
  486.9 3.8 reduce.16
  501.5 3.1 copy.197
  507.1 3.6 all-to-all-start.9
  514.1 40.0 %all-reduce = (f32[32,2]{0,1:T(2,128)S(1)}, f32[32]{0:T(128)S(1)}) all-reduce(f32[32,2]{0,1:T(2,128)S(1)} %fusion.53, f32[32]{0:T(128)S(1)} %fusion.56), channel_id=1, replica_groups=mesh['gx'=4,'gy'=8] {'gx','gy'}, use_global_device_ids=true, to_apply=%region_0.1 | all-reduce | flops 96 | bytes 768 | tf_op jit(solution)/shard_map/psum | solution.py:221
  559.5 11.6 %multiply_add_fusion = (f32[8,4,32,32,32]{4,3,2,1,0:T(8,128)}, f32[8,4,32,32,32]{4,3,2,1,0:T(8,128)}) fusion(f32[8,4,32,32]{3,2,1,0:T(8,128)S(1)} %copy.272, f32[8,4,32,32]{3,2,1,0:T(8,128)S(1)} %copy.203, f32[8,4,32,32]{3,2,1,0:T(8,128)S(1)} %copy.271, f32[8,4,32,32]{3,2,1,0:T(8,128)S(1)} %copy.200), kind=kLoop, calls=%fused_computation.5 | loop fusion | flops 6291456 | bytes 8912896 | tf_op jit(solution)/shard_map/add | solution.py:223
  571.1 13.7 %stack.144 = f32[1,8,4,32,1024]{4,3,2,1,0:T(8,128)} reshape(f32[8,4,32,32,32]{4,3,2,1,0:T(8,128)} %get-tuple-element.23) | data formatting | bytes 8388608 | tf_op jit(solution)/shard_map/stack | solution.py:225
  584.8 13.7 %stack.145 = f32[1,8,4,32,1024]{4,3,2,1,0:T(8,128)} reshape(f32[8,4,32,32,32]{4,3,2,1,0:T(8,128)} %get-tuple-element.24) | data formatting | bytes 8388608 | tf_op jit(solution)/shard_map/stack | solution.py:225
  598.4 8.5 %pad_maximum_fusion = f32[2,8,4,32,1024]{4,3,2,1,0:T(8,128)} fusion(f32[1,8,4,32,1024]{4,3,2,1,0:T(8,128)} %stack.145, f32[1,8,4,32,1024]{4,3,2,1,0:T(8,128)} %stack.144), kind=kLoop, calls=%fused_computation.6 | loop fusion | flops 2097152 | bytes 16777216 | tf_op jit(solution)/shard_map/stack | solution.py:225
  (202 shorter events, 130.4 us)
Async XLA Ops:
  7.2 371.7 %copy-start = (f32[32,32]{1,0:T(8,128)S(1)}, f32[32,32]{1,0:T(8,128)}, u32[]{:S(2)}) copy-start(f32[32,32]{1,0:T(8,128)} %param.14) | copy-start | bytes 12292
  7.2 14.2 %copy-start.9 = (f32[8,8,256]{2,1,0:T(8,128)S(1)}, f32[8,8,256]{2,1,0:T(8,128)}, u32[]{:S(2)}) copy-start(f32[8,8,256]{2,1,0:T(8,128)} %param.9) | copy-start | bytes 196612
  7.2 14.2 %copy-start.15 = (f32[8,8,256]{2,1,0:T(8,128)S(1)}, f32[8,8,256]{2,1,0:T(8,128)}, u32[]{:S(2)}) copy-start(f32[8,8,256]{2,1,0:T(8,128)} %param.10) | copy-start | bytes 196612
  7.2 14.2 %copy-start.18 = (f32[8,8,256]{2,1,0:T(8,128)S(1)}, f32[8,8,256]{2,1,0:T(8,128)}, u32[]{:S(2)}) copy-start(f32[8,8,256]{2,1,0:T(8,128)} %param.11) | copy-start | bytes 196612
  8.0 3.8 collective-permute-start
  8.5 3.4 collective-permute-start.1
  12.9 7.1 %collective-permute-start.2 = (f32[2,10,1,256]{3,2,1,0:T(1,128)S(1)}, f32[2,10,1,256]{3,2,1,0:T(1,128)S(1)}, u32[]{:S(2)}, u32[]{:S(2)}) collective-permute-start(f32[2,10,1,256]{3,2,1,0:T(1,128)S(1)} %get-tuple-element.71), channel_id=1, source_target_pairs={{0,1},{1,2},{2,3},{3,4},{4,5},{5,6},{6,7},{7,0},{8,9},{9,10},{10,1... | collective-permute-start | bytes 61448 | tf_op jit(solution)/shard_map/ppermute | solution.py:31
  15.2 4.8 collective-permute-start.3
  21.6 3.2 collective-permute-start.4
  22.4 2.5 collective-permute-start.5
  24.9 6.6 %collective-permute-start.6 = (f32[2,10,1,256]{3,2,1,0:T(1,128)S(1)}, f32[2,10,1,256]{3,2,1,0:T(1,128)S(1)}, u32[]{:S(2)}, u32[]{:S(2)}) collective-permute-start(f32[2,10,1,256]{3,2,1,0:T(1,128)S(1)} %get-tuple-element.57), channel_id=1, source_target_pairs={{0,1},{1,2},{2,3},{3,4},{4,5},{5,6},{6,7},{7,0},{8,9},{9,10},{10,1... | collective-permute-start | bytes 61448 | tf_op jit(solution)/shard_map/ppermute | solution.py:31
  26.4 5.1 collective-permute-start.7
  31.6 2.1 copy-start.20
  33.0 0.6 copy-start.17
  46.8 12.4 %all-to-all-start = ((f32[4,1,32768]{2,1,0:T(1,128)}), f32[4,1,32768]{2,1,0:T(1,128)S(1)}, u32[]{:S(2)}, u32[]{:S(2)}) async-start(f32[4,1,32768]{2,1,0:T(1,128)} %reshape.243), calls=%async_computation | async-start | bytes 1048576 | tf_op jit(solution)/shard_map/all_to_all | solution.py:115
  124.7 35.8 %all-to-all-start.3 = ((f32[8,1,8192]{2,1,0:T(1,128)}), f32[8,1,8192]{2,1,0:T(1,128)S(1)}, u32[]{:S(2)}, u32[]{:S(2)}) async-start(f32[8,1,8192]{2,1,0:T(1,128)} %reshape.249), calls=%async_computation.3 | async-start | bytes 524288 | tf_op jit(solution)/shard_map/all_to_all | solution.py:137
  128.4 188.1 %all-gather.2.cloned.1.call-start = ((), (), s32[]{:S(2)}) async-start(), calls=%async_computation.10 | async-start | bytes 9437184 | tf_op jit(solution)/shard_map/all_gather | solution.py:187
  185.5 3.0 copy-start.10
  186.5 2.0 copy-start.11
  187.5 1.1 copy-start.12
  341.5 12.7 %all-to-all-start.4 = ((f32[4,1,32768]{2,1,0:T(1,128)}), f32[4,1,32768]{2,1,0:T(1,128)S(1)}, u32[]{:S(2)}, u32[]{:S(2)}) async-start(f32[4,1,32768]{2,1,0:T(1,128)} %reshape.251), calls=%async_computation.4 | async-start | bytes 1048576 | tf_op jit(solution)/shard_map/all_to_all | solution.py:200
  360.7 2.0 copy-start.7
  365.4 1.2 copy-start.5
  375.1 12.4 %all-to-all-start.5 = ((f32[4,1,32768]{2,1,0:T(1,128)}), f32[4,1,32768]{2,1,0:T(1,128)S(1)}, u32[]{:S(2)}, u32[]{:S(2)}) async-start(f32[4,1,32768]{2,1,0:T(1,128)} %reshape.253), calls=%async_computation.5 | async-start | bytes 1048576 | tf_op jit(solution)/shard_map/all_to_all | solution.py:204
  392.2 1.6 copy-start.13
  392.2 1.6 copy-start.19
  392.2 1.6 copy-start.22
  392.2 1.6 copy-start.23
  399.2 1.3 copy-start.3
  431.8 2.1 copy-start.8
  436.5 1.2 copy-start.6
  465.1 7.6 %copy-start.2 = (f32[32,8,8,256]{3,2,1,0:T(8,128)S(1)}, f32[32,8,8,256]{3,2,1,0:T(8,128)}, u32[]{:S(2)}) copy-start(f32[32,8,8,256]{3,2,1,0:T(8,128)} %get-tuple-element.30) | copy-start | bytes 6291460
  468.4 18.5 %all-to-all-start.8 = ((f32[8,1,16384]{2,1,0:T(1,128)}), f32[8,1,16384]{2,1,0:T(1,128)}, u32[]{:S(2)}, u32[]{:S(2)}) async-start(f32[8,1,16384]{2,1,0:T(1,128)} %reshape.259), calls=%async_computation.8 | async-start | bytes 1048576 | tf_op jit(solution)/shard_map/all_to_all | solution.py:128
  501.5 9.1 %copy-start.4 = (f32[32,8,8,256]{3,2,1,0:T(8,128)S(1)}, f32[32,8,8,256]{3,2,1,0:T(8,128)}, u32[]{:S(2)}) copy-start(f32[32,8,8,256]{3,2,1,0:T(8,128)} %copy-done.3) | copy-start | bytes 6291460
  504.7 49.9 %copy-start.21 = (f32[32,2]{0,1:T(2,128)S(1)}, f32[32,2]{0,1:T(2,128)}, u32[]{:S(2)}) copy-start(f32[32,2]{0,1:T(2,128)} %param.12) | copy-start | bytes 772
  507.1 48.4 %all-to-all-start.9 = ((f32[8,1,8192]{2,1,0:T(1,128)}), f32[8,1,8192]{2,1,0:T(1,128)S(1)}, u32[]{:S(2)}, u32[]{:S(2)}) async-start(f32[8,1,8192]{2,1,0:T(1,128)} %reshape.261), calls=%async_computation.9 | async-start | bytes 524288 | tf_op jit(solution)/shard_map/all_to_all | solution.py:137
  510.7 2.8 copy-start.16
  558.0 1.0 copy-start.14
  598.4 8.5 %copy-start.1 = (f32[32,32]{1,0:T(8,128)S(1)}, f32[32,32]{1,0:T(8,128)}, u32[]{:S(2)}) copy-start(f32[32,32]{1,0:T(8,128)} %param.14) | copy-start | bytes 12292
Sparse Core Ops, SparseCore 0:
  190.9 125.5 all-gather.1
where the time goes:
time: 623 us; the launch traced here: 614 us
  waiting for transfers between devices  163 us (26%)
  local copies, waits for them, and re-layouts  140 us (22%)
  blocking collectives  96 us (15%)
  matrix products  82.6 us (13%)
  other arithmetic  79.3 us (13%)
  starting transfers between devices  37.7 us (6%)
  between operations  15.2 us (2%)
    all_gather x1, waiting for transfers between devices, per_device(): portion = lax.all_gather(spectral_out, 'gy', axis=3, tiled=True)  126 us
    dot_general x24, matrix products, apply(): return jnp.einsum(pattern, table, values, precision=lax.Precision.HIGHEST)  48.9 us
    psum x1, blocking collectives, per_device(): field_sums, proj_sums = lax.psum((field_sums, proj_sums), ('gx', 'gy'))  40 us
    unnamed x70, local copies, waits for them, and re-layouts  33.7 us
    another operation x2, local copies, waits for them, and re-layouts, per_device(): jnp.stack([grad_real, grad_imag])  27.3 us
    all_to_all x2, blocking collectives, x_forward(): return lax.all_to_all(lines, 'gx', split_axis=2, concat_axis=1, tiled=True)  23.5 us
    unnamed x2, other arithmetic  21.6 us
    all_to_all x1, blocking collectives, y_forward(): lax.all_to_all(data, 'gy', split_axis=1, concat_axis=3, tiled=True)  20.2 us
  transfers between devices with their start and end apart: 15, of which 10 were waited for; matrix products, arithmetic and copies ran while one was open for 7% of the time, Pallas kernels for 0%

commit v1 on v0

--- a/solution.py
+++ b/solution.py
@@ -1,9 +1,14 @@
+import functools
 from functools import reduce
 import math
 
 import jax
 import jax.numpy as jnp
+import ml_dtypes
+import numpy as np
 from jax import lax
+from jax.experimental import pallas as pl
+from jax.experimental.pallas import tpu as pltpu
 from jax.sharding import PartitionSpec as P
 
 WIDTH = 32
@@ -145,7 +150,7 @@
     return jnp.einsum("oabz,iabz->abzoi", left, right, precision=lax.Precision.HIGHEST)
 
 
-def per_device(
+def per_device_plain(
     phase,
     solute,
     undercool,
@@ -227,6 +232,727 @@
     grad_local = jnp.dot(field_sums, lift_weight.T, precision=lax.Precision.HIGHEST) * scale
     grad_proj = proj_sums * scale
     return (phase_next, solute_next, predicted, grad_spectral, grad_local, grad_proj)
+
+
+LANES = 128
+SPREAD = LANES // WIDTH
+NARROW = jnp.bfloat16
+EXACT = lax.Precision.HIGHEST
+
+
+def halves(table):
+    head = table.astype(np.float32).astype(ml_dtypes.bfloat16)
+    rest = (table - head.astype(np.float64)).astype(np.float32).astype(ml_dtypes.bfloat16)
+    return head, rest
+
+
+def left_table(table):
+    head, rest = halves(table)
+    return np.concatenate([head, head, rest], axis=1)
+
+
+def right_table(table):
+    head, rest = halves(table)
+    return np.concatenate([head, head, rest], axis=0)
+
+
+def parts_of(values):
+    head = values.astype(NARROW)
+    return head, (values - head.astype(jnp.float32)).astype(NARROW)
+
+
+def thrice(values, axis):
+    head, rest = parts_of(values)
+    return jnp.concatenate([head, rest, head], axis=axis)
+
+
+def mul(left, right):
+    return jnp.dot(left, right, preferred_element_type=jnp.float32)
+
+
+def mul_rows(left, right):
+    return lax.dot_general(
+        left, right, (((1,), (1,)), ((), ())), preferred_element_type=jnp.float32
+    )
+
+
+def angles(freqs, positions, length):
+    return 2.0 * np.pi * ((freqs[:, None] * positions[None, :]) % length) / length
+
+
+def signed(count):
+    index = np.arange(count)
+    return np.where(index < count // 2, index, index - count)
+
+
+def rotation(theta, orient):
+    cosines, sines = np.cos(theta), orient * np.sin(theta)
+    return np.block([[cosines, -sines], [sines, cosines]])
+
+
+def group_of(shape):
+    return lax.broadcasted_iota(jnp.int32, shape, len(shape) - 1) // WIDTH
+
+
+def pick(groups, choices):
+    result = choices[-1]
+    for index in range(len(choices) - 2, -1, -1):
+        result = jnp.where(groups == index, choices[index], result)
+    return result
+
+
+def turn(values, shift):
+    shift = shift % LANES
+    return values if shift == 0 else pltpu.roll(values, shift, 1)
+
+
+def swap_groups(pieces):
+    groups = group_of(pieces[0].shape)
+    return [
+        pick(groups, [turn(pieces[i], WIDTH * (i - j)) for i in range(SPREAD)])
+        for j in range(SPREAD)
+    ]
+
+
+def contract_kernel(weight_ref, lift_ref, out_ref, mix_ref):
+    _, planes, own_y, modes_z, _ = weight_ref.shape
+    own_x = pl.num_programs(0) * planes
+    step = pl.program_id(0)
+
+    @pl.when(step == 0)
+    def _():
+        shape = (WIDTH, LANES)
+        lane = lax.broadcasted_iota(jnp.int32, shape, 1)
+        base = jnp.where(
+            lane % (2 * WIDTH) < WIDTH,
+            jnp.broadcast_to(lift_ref[:, 0:1], shape),
+            jnp.broadcast_to(lift_ref[:, 1:2], shape),
+        )
+        for channel in range(WIDTH):
+            block = jnp.where(lane % WIDTH == channel, base, 0.0)
+            head, rest = parts_of(block)
+            both = jnp.where(lane < 2 * WIDTH, head.astype(jnp.float32), rest.astype(jnp.float32))
+            mix_ref[channel * WIDTH : (channel + 1) * WIDTH, :] = both.astype(NARROW)
+
+    mixing = mix_ref[...]
+    rows = planes * own_y * modes_z
+    sums = []
+    for part in range(2):
+        head, rest = parts_of(weight_ref[part].reshape(rows, WIDTH * WIDTH))
+        total = mul(head, mixing) + mul(rest, mixing)
+        sums.append(total + pltpu.roll(total, 2 * WIDTH, 1))
+    lane = lax.broadcasted_iota(jnp.int32, (rows, LANES), 1)
+    result = jnp.where(lane < 2 * WIDTH, sums[0], sums[1])
+    for plane in range(planes):
+        for row in range(own_y):
+            first = (plane * own_y + row) * modes_z
+            place = row * own_x + step * planes + plane
+            out_ref[pl.ds(place, modes_z, stride=own_x * own_y), :] = result[
+                first : first + modes_z
+            ]
+
+
+def pack_kernel(phase_ref, solute_ref, cool_ref, before_ref, after_ref, head_ref, tail_ref):
+    cells_x, cells_y, _ = phase_ref.shape
+
+    def put(target, phase, solute, cool):
+        head_ref[target, 0:2] = phase[:, 0:2]
+        head_ref[target, 2:4] = solute[:, 0:2]
+        head_ref[target, 4:5] = cool[:, 0:1]
+        tail_ref[target, 0:2] = phase[:, cells_y - 2 : cells_y]
+        tail_ref[target, 2:4] = solute[:, cells_y - 2 : cells_y]
+        tail_ref[target, 4:5] = cool[:, cells_y - 1 : cells_y]
+
+    put(slice(0, 1), before_ref[1:2], before_ref[3:4], before_ref[4:5])
+    put(slice(1, cells_x + 1), phase_ref[...], solute_ref[...], cool_ref[...])
+    put(slice(cells_x + 1, cells_x + 2), after_ref[0:1], after_ref[2:3], after_ref[4:5])
+
+
+def step_kernel(
+    phase_ref,
+    solute_ref,
+    cool_ref,
+    before_ref,
+    after_ref,
+    low_ref,
+    high_ref,
+    table_ref,
+    phase_out,
+    solute_out,
+    spec_out,
+    phase_ext,
+    solute_ext,
+    cool_ext,
+    diff_ext,
+    lines,
+):
+    cells_x, cells_y, depth = phase_ref.shape
+    base = 8
+    end = base + cells_y
+    for ext, own, first in ((phase_ext, phase_ref, 0), (solute_ext, solute_ref, 2)):
+        ext[2 : cells_x + 2, base:end] = own[...]
+        ext[0:2, base:end] = before_ref[first : first + 2]
+        ext[cells_x + 2 : cells_x + 4, base:end] = after_ref[first : first + 2]
+        ext[1 : cells_x + 3, base - 2 : base] = low_ref[:, first : first + 2]
+        ext[1 : cells_x + 3, end : end + 2] = high_ref[:, first : first + 2]
+    cool_ext[2 : cells_x + 2, base:end] = cool_ref[...]
+    cool_ext[1:2, base:end] = before_ref[4:5]
+    cool_ext[cells_x + 2 : cells_x + 3, base:end] = after_ref[4:5]
+    cool_ext[1 : cells_x + 3, base - 1 : base] = low_ref[:, 4:5]
+    cool_ext[1 : cells_x + 3, end : end + 1] = high_ref[:, 4:5]
+
+    def sweep(reach):
+        diff_ext[...] = diffusivity(phase_ext[...])
+
+        def window(ext, move_x, move_y):
+            return ext[
+                2 - reach + move_x : cells_x + 2 + reach + move_x,
+                base - reach + move_y : end + reach + move_y,
+            ]
+
+        def around(ext, now):
+            return [
+                window(ext, 1, 0),
+                window(ext, -1, 0),
+                window(ext, 0, 1),
+                window(ext, 0, -1),
+                pltpu.roll(now, depth - 1, 2),
+                pltpu.roll(now, 1, 2),
+            ]
+
+        phase_now = window(phase_ext, 0, 0)
+        solute_now = window(solute_ext, 0, 0)
+        diff_now = window(diff_ext, 0, 0)
+        return update(
+            phase_now,
+            solute_now,
+            window(cool_ext, 0, 0),
+            around(phase_ext, phase_now),
+            around(solute_ext, solute_now),
+            diff_now,
+            around(diff_ext, diff_now),
+        )
+
+    phase_mid, solute_mid = sweep(1)
+    phase_ext[1 : cells_x + 3, base - 1 : end + 1] = phase_mid
+    solute_ext[1 : cells_x + 3, base - 1 : end + 1] = solute_mid
+    phase_next, solute_next = sweep(0)
+    phase_out[...] = phase_next
+    solute_out[...] = solute_next
+    tile = cells_x * cells_y
+    both = (phase_next.reshape(tile, depth), solute_next.reshape(tile, depth) - SOLUTE_MEAN)
+    ordered = []
+    for part in range(depth // LANES):
+        for index, values in enumerate(both):
+            lines[part, index * tile : (index + 1) * tile] = values[
+                :, part * LANES : (part + 1) * LANES
+            ]
+        ordered.append(
+            jnp.concatenate(
+                [
+                    lines[part, pl.ds(row, 2 * cells_x, stride=cells_y), :]
+                    for row in range(cells_y)
+                ],
+                axis=0,
+            )
+        )
+    ordered = jnp.concatenate(ordered, axis=1)
+    spec_out[...] = mul_rows(table_ref[...], thrice(ordered, 1))
+
+
+def spectral_kernel(
+    shape,
+    spec_ref,
+    weight_ref,
+    y_in_ref,
+    x_in_ref,
+    y_out_ref,
+    x_out_ref,
+    modes_ref,
+    send_ref,
+    lines_y,
+    lines_x,
+):
+    count_x, count_y, cells_x, cells_y, own_x, own_y = shape
+    modes_x, modes_y = count_x * own_x, count_y * own_y
+    total_x, total_y = count_x * cells_x, count_y * cells_y
+    tile = cells_x * cells_y
+    narrow = 2 * cells_x
+    rows = 2 * count_y
+    lane = lax.broadcasted_iota(jnp.int32, (rows, LANES), 1)
+    blocks = []
+    for row in range(cells_y):
+        block = jnp.zeros((rows, LANES), jnp.float32)
+        for index in range(count_x):
+            piece = turn(spec_ref[index * rows : (index + 1) * rows, :], narrow * (index - row))
+            block = jnp.where(lane // narrow == index, piece, block)
+        blocks.append(block)
+    along_y = mul(y_in_ref[...], thrice(jnp.concatenate(blocks, axis=0), 0))
+    half = lax.broadcasted_iota(jnp.int32, (modes_y, LANES), 1) < LANES // 2
+    joined = jnp.where(half, along_y[0:modes_y], turn(along_y[modes_y:], LANES // 2))
+    modes = mul(thrice(joined, 1), x_in_ref[...])
+    modes_ref[...] = modes
+    groups = group_of((modes_y, LANES))
+    quads_y = total_y // SPREAD
+    for quad in range(modes_x // SPREAD):
+        reals, imags = [], []
+        for index in range(SPREAD):
+            freq = SPREAD * quad + index
+            start = (freq // own_x) * count_y * own_y * own_x + freq % own_x
+            weights = weight_ref[pl.ds(start, modes_y, stride=own_x), :]
+            columns = [
+                jnp.broadcast_to(
+                    modes[:, k * modes_x + freq : k * modes_x + freq + 1], (modes_y, LANES)
+                )
+                for k in range(4)
+            ]
+            first = weights * pick(groups, [columns[0], columns[1], -columns[2], -columns[3]])
+            second = weights * pick(groups, [columns[2], columns[3], columns[0], columns[1]])
+            first = first + turn(first, 2 * WIDTH)
+            second = second + turn(second, 2 * WIDTH)
+            reals.append(first + turn(first, WIDTH))
+            imags.append(second + turn(second, WIDTH))
+        stacked = jnp.concatenate([pick(groups, reals), pick(groups, imags)], axis=0)
+        lines_y[...] = mul(y_out_ref[...], thrice(stacked, 0))
+        for part in range(2):
+            pieces = [
+                lines_y[pl.ds(part * total_y + i, quads_y, stride=SPREAD), :] for i in range(SPREAD)
+            ]
+            for index, piece in enumerate(swap_groups(pieces)):
+                place = part * modes_x + SPREAD * quad + index
+                lines_x[pl.ds(place, quads_y, stride=2 * modes_x), :] = piece
+    per_tile = cells_y // SPREAD
+    for quad in range(quads_y):
+        block = lines_x[quad * 2 * modes_x : (quad + 1) * 2 * modes_x, :]
+        back = mul(x_out_ref[...], thrice(block, 0))
+        for part in range(2):
+            for index in range(count_x):
+                device = index * count_y + quad // per_tile
+                place = (device * 2 + part) * per_tile + quad % per_tile
+                first = part * total_x + index * cells_x
+                send_ref[place * cells_x : (place + 1) * cells_x, :] = back[
+                    first : first + cells_x
+                ]
+
+
+def field_kernel(
+    shape,
+    field_ref,
+    phase_ref,
+    solute_ref,
+    cotangent_ref,
+    vector_ref,
+    back_ref,
+    forth_ref,
+    predicted_ref,
+    send_ref,
+    spread_ref,
+):
+    cells_x, cells_y, modes_z = shape
+    tile = cells_x * cells_y
+    depth = phase_ref.shape[1]
+    wide = cells_y * WIDTH
+    halves_y = cells_y // SPREAD
+    stride = halves_y * cells_x
+    for index, values in enumerate(
+        (phase_ref[...], solute_ref[...] - SOLUTE_MEAN, cotangent_ref[...])
+    ):
+        head, rest = parts_of(values.T)
+        spread_ref[index] = jnp.concatenate([head, rest], axis=1)
+    mix_phase = vector_ref[0:1, :]
+    mix_solute = vector_ref[1:2, :]
+    bias = vector_ref[2:3, :]
+    proj = vector_ref[3:4, :]
+    root = math.sqrt(2.0 / math.pi)
+    curve = 0.044715
+    cell = lax.broadcasted_iota(jnp.int32, (2 * tile, wide), 0) % tile
+    row = lax.broadcasted_iota(jnp.int32, (2 * tile, wide), 1) // WIDTH
+    picker = (
+        lax.broadcasted_iota(jnp.int32, (cells_y, 2 * wide), 0)
+        == lax.broadcasted_iota(jnp.int32, (cells_y, 2 * wide), 1) % wide // WIDTH
+    ).astype(jnp.float32).astype(NARROW)
+
+    def fold(values):
+        return jnp.sum(values.reshape(depth // 8, 8, wide), axis=0)
+
+    def one(plane, sums):
+        spectra = jnp.concatenate(
+            [
+                field_ref[pl.ds(part * cells_x + plane, 2 * modes_z, stride=stride), :]
+                for part in range(halves_y)
+            ],
+            axis=1,
+        )
+        field = mul(back_ref[...], thrice(spectra, 0))
+        chosen = (cell == plane * cells_y + row).astype(jnp.float32).astype(NARROW)
+        phase = mul(spread_ref[0], chosen)
+        solute = mul(spread_ref[1], chosen)
+        cotangent = mul(spread_ref[2], chosen)
+        pre = field + phase * mix_phase + solute * mix_solute + bias
+        square = pre * pre
+        bent = jnp.tanh(root * pre * (1.0 + curve * square))
+        upper = 0.5 * (1.0 + bent)
+        active = pre * upper
+        slope = upper + 0.5 * pre * (1.0 - bent * bent) * (root * (1.0 + 3.0 * curve * square))
+        grad = proj * cotangent * slope
+        weighted = jnp.concatenate(parts_of(proj * active), axis=1)
+        predicted_ref[pl.ds(pl.multiple_of(plane * cells_y, cells_y), cells_y), :] = mul_rows(
+            picker, weighted
+        )
+        spectra = mul(forth_ref[...], thrice(grad, 0))
+        for part in range(halves_y):
+            send_ref[pl.ds(part * cells_x + plane, 2 * modes_z, stride=stride), :] = spectra[
+                :, part * LANES : (part + 1) * LANES
+            ]
+        return (
+            sums[0] + fold(grad * phase),
+            sums[1] + fold(grad * solute),
+            sums[2] + fold(active * cotangent),
+        )
+
+    zero = jnp.zeros((8, wide), jnp.float32)
+    sums = lax.fori_loop(0, cells_x, one, (zero, zero, zero))
+    for index, values in enumerate(sums):
+        line = jnp.sum(values, axis=0, keepdims=True)
+        line = sum(line[:, part * LANES : (part + 1) * LANES] for part in range(halves_y))
+        send_ref[stride + index : stride + index + 1, :] = line
+
+
+def gradient_kernel(
+    shape, spectra_ref, modes_ref, x_in_ref, y_in_ref, send_ref, lines_x, lines_y
+):
+    count_x, count_y, cells_x, cells_y, own_x, own_y = shape
+    modes_x, modes_y = count_x * own_x, count_y * own_y
+    total_x, total_y = count_x * cells_x, count_y * cells_y
+    per_tile = cells_y // SPREAD
+    quads_y = total_y // SPREAD
+    chunk = 2 * per_tile * cells_x
+    first_device = (lax.axis_index("gx") == 0) & (lax.axis_index("gy") == 0)
+    keep = jnp.where(first_device, 0.0, 1.0)
+    for quad in range(quads_y):
+        blocks = []
+        for part in range(2):
+            for index in range(count_x):
+                device = index * count_y + quad // per_tile
+                place = (device * 2 + part) * per_tile + quad % per_tile
+                block = spectra_ref[place * cells_x : (place + 1) * cells_x, :]
+                blocks.append(block * keep if part else block)
+        lines_x[quad * 2 * modes_x : (quad + 1) * 2 * modes_x, :] = mul(
+            x_in_ref[...], thrice(jnp.concatenate(blocks, axis=0), 0)
+        )
+    out_chunk = send_ref.shape[0] // (count_x * count_y)
+    per_own = own_x // SPREAD
+    for quad in range(modes_x // SPREAD):
+        for part in range(2):
+            pieces = [
+                lines_x[
+                    pl.ds(part * modes_x + SPREAD * quad + j, quads_y, stride=2 * modes_x), :
+                ]
+                for j in range(SPREAD)
+            ]
+            for index, piece in enumerate(swap_groups(pieces)):
+                lines_y[pl.ds(part * total_y + index, quads_y, stride=SPREAD), :] = piece
+        modes = mul(y_in_ref[...], thrice(lines_y[...], 0))
+        for part in range(2):
+            for index in range(count_y):
+                device = (quad // per_own) * count_y + index
+                place = device * out_chunk + (part * per_own + quad % per_own) * own_y
+                first = part * modes_y + index * own_y
+                send_ref[place : place + own_y, :] = modes[first : first + own_y]
+    extra = 2 * per_own * own_y
+    totals = []
+    for index in range(3):
+        start = chunk // 2 + index
+        line = jnp.sum(
+            spectra_ref[pl.ds(start, count_x * count_y, stride=chunk), :], axis=0, keepdims=True
+        )
+        line = line + turn(line, 2 * WIDTH)
+        totals.append(line + turn(line, WIDTH))
+    totals.append(jnp.zeros_like(totals[0]))
+    totals = jnp.concatenate(totals, axis=0)
+    for index_x in range(count_x):
+        for index_y in range(count_y):
+            place = (index_x * count_y + index_y) * out_chunk + extra
+            send_ref[place : place + own_y, :] = modes_ref[
+                index_y * own_y : (index_y + 1) * own_y, :
+            ]
+            send_ref[place + own_y : place + own_y + 4, :] = totals
+
+
+def outer_kernel(scale, modes_x, modes_ref, lift_ref, grad_ref, local_ref, proj_ref, mix_ref):
+    _, planes, own_y, modes_z, width = grad_ref.shape
+    own_x = pl.num_programs(0) * planes
+    step = pl.program_id(0)
+    chunk = modes_ref.shape[0] // modes_z
+    per_own = own_x // SPREAD
+    extra = 2 * per_own * own_y
+
+    @pl.when(step == 0)
+    def _():
+        shape = (2 * WIDTH, width)
+        row = lax.broadcasted_iota(jnp.int32, shape, 0)
+        column = lax.broadcasted_iota(jnp.int32, shape, 1)
+        lift = jnp.where(row < WIDTH, lift_ref[0:1, :], lift_ref[1:2, :])
+        head, rest = parts_of(jnp.where(column // WIDTH == row % WIDTH, lift, 0.0))
+        mix_ref[0 : 2 * WIDTH] = head
+        mix_ref[2 * WIDTH : 4 * WIDTH] = head
+        mix_ref[4 * WIDTH : 6 * WIDTH] = rest
+        mix_ref[6 * WIDTH : 8 * WIDTH] = jnp.zeros_like(rest)
+        sums = modes_ref[extra : extra + 8, :]
+        turned = sums.T[0:WIDTH]
+        local_ref[...] = scale * (
+            turned[:, own_y : own_y + 1] * lift_ref[0:1, 0:WIDTH]
+            + turned[:, own_y + 1 : own_y + 2] * lift_ref[1:2, 0:WIDTH]
+        )
+        proj_ref[...] = scale * sums[own_y + 2 : own_y + 3, 0:WIDTH]
+
+    lane = lax.broadcasted_iota(jnp.int32, (modes_z, LANES), 1)
+    even = lane % (2 * WIDTH) < WIDTH
+    low = lane < 2 * WIDTH
+
+    def rows_of(values):
+        head, rest = parts_of(values)
+        both = jnp.where(low, head.astype(jnp.float32), rest.astype(jnp.float32)).astype(NARROW)
+        return jnp.concatenate([both, head], axis=1)
+
+    for plane in range(planes):
+        freq = step * planes + plane
+        reals, imags = [], []
+        for row in range(own_y):
+            modes = modes_ref[pl.ds(extra + row, modes_z, stride=chunk), :]
+            modes = pltpu.roll(modes, LANES - (lax.axis_index("gx") * own_x + freq), 1)
+            columns = [
+                jnp.broadcast_to(modes[:, k * modes_x : k * modes_x + 1], (modes_z, LANES))
+                for k in range(4)
+            ]
+            real = jnp.where(even, columns[0], columns[1])
+            imag = jnp.where(even, columns[2], columns[3])
+            grads = []
+            for part in range(2):
+                place = (part * per_own + freq // SPREAD) * own_y + row
+                grad = modes_ref[pl.ds(place, modes_z, stride=chunk), :]
+                grad = pltpu.roll(grad, (LANES - WIDTH * (freq % SPREAD)) % LANES, 1)
+                grad = jnp.where(lane < WIDTH, grad, 0.0)
+                grad = grad + turn(grad, WIDTH)
+                grads.append(grad + turn(grad, 2 * WIDTH))
+            reals.append(rows_of(grads[0] * real + grads[1] * imag))
+            imags.append(rows_of(grads[1] * real - grads[0] * imag))
+        result = mul(jnp.concatenate(reals + imags, axis=0), mix_ref[...])
+        grad_ref[:, plane] = result.reshape(2, own_y, modes_z, width)
+
+
+def tables(shape, depth, modes_z):
+    count_x, count_y, cells_x, cells_y, own_x, own_y = shape
+    modes_x, modes_y = count_x * own_x, count_y * own_y
+    total_x, total_y = count_x * cells_x, count_y * cells_y
+    theta_z = angles(np.arange(modes_z), np.arange(depth), depth)
+    theta_x = angles(signed(modes_x), np.arange(total_x), total_x)
+    theta_y = angles(signed(modes_y), np.arange(total_y), total_y)
+    forth_z = np.stack([np.cos(theta_z), -np.sin(theta_z)], axis=1).reshape(2 * modes_z, depth)
+    weight = np.where(np.arange(modes_z) == 0, 1.0, 2.0) / (total_x * total_y * depth)
+    weighted_z = np.repeat(weight, 2)[:, None] * forth_z
+    forth_x, back_x = rotation(theta_x, -1.0), rotation(theta_x.T, 1.0)
+    forth_y, back_y = rotation(theta_y, -1.0), rotation(theta_y.T, 1.0)
+    order_y = forth_y.reshape(2 * modes_y, 2, count_y, cells_y)
+    order_y = order_y.transpose(0, 3, 2, 1).reshape(2 * modes_y, 2 * total_y)
+    lines = forth_x.reshape(2, modes_x, 2, count_x, cells_x)
+    both = np.zeros((2, count_x, 2, cells_x, 2, 2, modes_x))
+    for field in range(2):
+        both[:, :, field, :, :, field, :] = lines.transpose(2, 3, 4, 0, 1)
+    both = both.reshape(4 * total_x, 4 * modes_x)
+    return {
+        "z_plain": left_table(forth_z),
+        "z_forth": left_table(weighted_z),
+        "z_back": left_table(weighted_z.T),
+        "y_first": left_table(order_y),
+        "x_first": right_table(both),
+        "y_back": left_table(back_y),
+        "x_back": left_table(back_x),
+        "x_forth": left_table(forth_x),
+        "y_forth": left_table(forth_y),
+    }
+
+
+def fits(count_x, count_y, phase, spectral_weight):
+    cells_x, cells_y, depth = phase.shape
+    _, own_x, own_y, modes_z, width = spectral_weight.shape
+    return (
+        width == WIDTH * WIDTH
+        and modes_z == count_x * count_y
+        and 4 * count_x * cells_x == LANES
+        and 4 * count_x * own_x == LANES
+        and 2 * cells_x * cells_y == LANES
+        and cells_x == 8
+        and cells_y % SPREAD == 0
+        and own_x % SPREAD == 0
+        and own_y == 4
+        and depth % LANES == 0
+    )
+
+
+def call(kernel, outs, scratch, flops, moved, **more):
+    return pl.pallas_call(
+        kernel,
+        out_shape=outs,
+        scratch_shapes=scratch,
+        compiler_params=pltpu.CompilerParams(vmem_limit_bytes=32 * 1024 * 1024),
+        cost_estimate=pl.CostEstimate(flops=flops, bytes_accessed=moved, transcendentals=0),
+        **more,
+    )
+
+
+def exchange(values):
+    return lax.all_to_all(values, ("gx", "gy"), split_axis=0, concat_axis=0, tiled=True)
+
+
+def per_device_fast(
+    phase,
+    solute,
+    undercool,
+    lift_weight,
+    spectral_weight,
+    local_weight,
+    local_bias,
+    proj_weight,
+    cotangent,
+):
+    count_x, count_y = lax.axis_size("gx"), lax.axis_size("gy")
+    cells_x, cells_y, depth = phase.shape
+    _, own_x, own_y, modes_z, width = spectral_weight.shape
+    shape = (count_x, count_y, cells_x, cells_y, own_x, own_y)
+    devices = count_x * count_y
+    tile = cells_x * cells_y
+    modes_x, modes_y = count_x * own_x, count_y * own_y
+    total_x, total_y = count_x * cells_x, count_y * cells_y
+    table = tables(shape, depth, modes_z)
+    real = jnp.float32
+
+    def like(*dims):
+        return jax.ShapeDtypeStruct(dims, real)
+
+    planes = 2
+    mixed_weights = call(
+        contract_kernel,
+        like(modes_z * own_x * own_y, LANES),
+        [pltpu.VMEM((width, LANES), NARROW)],
+        8 * own_x * own_y * modes_z * width * LANES,
+        8 * own_x * own_y * modes_z * width,
+        grid=(own_x // planes,),
+        in_specs=[
+            pl.BlockSpec((2, planes, own_y, modes_z, width), lambda i: (0, i, 0, 0, 0)),
+            pl.BlockSpec(lift_weight.shape, lambda i: (0, 0)),
+        ],
+        out_specs=pl.BlockSpec((modes_z * own_x * own_y, LANES), lambda i: (0, 0)),
+    )(spectral_weight, lift_weight)
+
+    def ring(values, axis, step):
+        count = lax.axis_size(axis)
+        return lax.ppermute(values, axis, [(i, (i + step) % count) for i in range(count)])
+
+    head = jnp.concatenate([phase[:2], solute[:2], undercool[:1]])
+    tail = jnp.concatenate([phase[-2:], solute[-2:], undercool[-1:]])
+    before, after = ring(tail, "gx", 1), ring(head, "gx", -1)
+    head, tail = call(
+        pack_kernel,
+        (like(cells_x + 2, 8, depth), like(cells_x + 2, 8, depth)),
+        [],
+        1000,
+        40 * cells_x * cells_y * depth,
+    )(phase, solute, undercool, before, after)
+    low, high = ring(tail, "gy", 1), ring(head, "gy", -1)
+    extended_shape = pltpu.VMEM((cells_x + 4, cells_y + 16, depth), real)
+    phase_next, solute_next, spectra = call(
+        step_kernel,
+        (like(*phase.shape), like(*phase.shape), like(2 * modes_z, LANES)),
+        [extended_shape] * 4 + [pltpu.VMEM((depth // LANES, 2 * tile, LANES), real)],
+        400 * tile * depth,
+        80 * tile * depth,
+    )(phase, solute, undercool, before, after, low, high, table["z_plain"])
+    gathered_weights = exchange(mixed_weights)
+    gathered = exchange(spectra)
+    modes, fields = call(
+        functools.partial(spectral_kernel, shape),
+        (like(modes_y, LANES), like(devices * 2 * cells_x * (cells_y // SPREAD), LANES)),
+        [
+            pltpu.VMEM((2 * total_y, LANES), real),
+            pltpu.VMEM((2 * modes_x * (total_y // SPREAD), LANES), real),
+        ],
+        100_000_000,
+        2_000_000,
+    )(
+        gathered,
+        gathered_weights,
+        table["y_first"],
+        table["x_first"],
+        table["y_back"],
+        table["x_back"],
+    )
+    fields = exchange(fields)
+    mixed = jnp.dot(local_weight, lift_weight, precision=EXACT)
+    vectors = jnp.tile(
+        jnp.stack([mixed[:, 0], mixed[:, 1], local_bias, proj_weight]), (1, cells_y)
+    )
+    predicted, spectra = call(
+        functools.partial(field_kernel, (cells_x, cells_y, modes_z)),
+        (like(tile, depth), like(*fields.shape)),
+        [pltpu.VMEM((3, depth, 2 * tile), NARROW)],
+        1_000_000_000,
+        2_000_000,
+    )(
+        fields,
+        phase_next.reshape(tile, depth),
+        solute_next.reshape(tile, depth),
+        cotangent.reshape(tile, depth),
+        vectors,
+        table["z_back"],
+        table["z_forth"],
+    )
+    spectra = exchange(spectra)
+    chunk = 2 * own_x * own_y * WIDTH // LANES + 8
+    gradients = call(
+        functools.partial(gradient_kernel, shape),
+        like(devices * chunk, LANES),
+        [
+            pltpu.VMEM((2 * modes_x * (total_y // SPREAD), LANES), real),
+            pltpu.VMEM((2 * total_y, LANES), real),
+        ],
+        100_000_000,
+        2_000_000,
+    )(spectra, modes, table["x_forth"], table["y_forth"])
+    gradients = exchange(gradients)
+    planes = 1
+    grad_spectral, grad_local, grad_proj = call(
+        functools.partial(outer_kernel, 1.0 / math.sqrt(total_x * total_y * depth), modes_x),
+        (like(*spectral_weight.shape), like(WIDTH, WIDTH), like(1, WIDTH)),
+        [pltpu.VMEM((8 * WIDTH, width), NARROW)],
+        4 * own_x * own_y * modes_z * width * 8 * WIDTH,
+        8 * own_x * own_y * modes_z * width,
+        grid=(own_x // planes,),
+        in_specs=[
+            pl.BlockSpec(gradients.shape, lambda i: (0, 0)),
+            pl.BlockSpec((2, width), lambda i: (0, 0)),
+        ],
+        out_specs=(
+            pl.BlockSpec((2, planes, own_y, modes_z, width), lambda i: (0, i, 0, 0, 0)),
+            pl.BlockSpec((WIDTH, WIDTH), lambda i: (0, 0)),
+            pl.BlockSpec((1, WIDTH), lambda i: (0, 0)),
+        ),
+    )(gradients, jnp.tile(lift_weight.T, (1, WIDTH)))
+    return (
+        phase_next,
+        solute_next,
+        predicted.reshape(phase.shape),
+        grad_spectral,
+        grad_local,
+        grad_proj.reshape(WIDTH),
+    )
+
+
+def per_device(*arguments):
+    count_x, count_y = lax.axis_size("gx"), lax.axis_size("gy")
+    if fits(count_x, count_y, arguments[0], arguments[4]):
+        return per_device_fast(*arguments)
+    return per_device_plain(*arguments)
 
 
 def solution(mesh):

time: 623 us -> 133 us (0.21); the launches traced: 614 us -> 132 us
  waiting for transfers between devices: 163 us -> 34.3 us
  local copies, waits for them, and re-layouts: 140 us -> 11.9 us
  matrix products: 82.6 us -> 0.13 us
  other arithmetic: 79.3 us -> 0.02 us
  blocking collectives: 96 us -> 40.3 us
  Pallas kernels: 0 us -> 26.5 us
  starting transfers between devices: 37.7 us -> 18.2 us
  between operations: 15.2 us -> 0.87 us
    all_gather x1 -> x0, waiting for transfers between devices: 126 us -> none  [per_device(): portion = lax.all_gather(spectral_out, 'gy', axis=3, tiled=True)]
    dot_general x34 -> x1, matrix products: 82.6 us -> 0.13 us  [per_device_fast(): mixed = jnp.dot(local_weight, lift_weight, precision=EXACT)]
    another operation x9 -> x5, local copies, waits for them, and re-layouts: 40.6 us -> 0.18 us  [the longest x2 0.09 us: per_device_fast(): jnp.tile(lift_weight.T, (1, WIDTH))]
    psum x1 -> x0, blocking collectives: 40 us -> none  [per_device(): field_sums, proj_sums = lax.psum((field_sums, proj_sums), ('gx', 'gy'))]
    squeeze x12 -> x0, local copies, waits for them, and re-layouts: 28.5 us -> none  [the longest x1 11.6 us: per_device(): shaped[1]]
    pallas_call x0 -> x7, Pallas kernels: none -> 26.5 us  [the longest x1 6.88 us: per_device_fast(): call(functools.partial(outer_kernel, 1.0 / math.sqrt(total_x * total_y *...]
    all_to_all x10 -> x0, other arithmetic: 24.4 us -> none  [the longest x2 5.66 us: y_forward(): lax.all_to_all(data, 'gy', split_axis=1, concat_axis=3, tiled=True)]
    unnamed x70 -> x47, local copies, waits for them, and re-layouts: 33.7 us -> 10.1 us
  transfers between devices with their start and end apart: 15 -> 7, of which waited for: 10 -> 6; matrix products, arithmetic and copies ran while one was open for 7% -> 1% of each run, Pallas kernels for 0% -> 3%
where the time goes in v1:
time: 133 us; the launch traced here: 132 us
  blocking collectives  40.3 us (30%)
  waiting for transfers between devices  34.3 us (26%)
  Pallas kernels  26.5 us (20%)
  starting transfers between devices  18.2 us (14%)
  local copies, waits for them, and re-layouts  11.9 us (9%)
    all_to_all x2, blocking collectives, exchange(): lax.all_to_all(values, ('gx', 'gy'), split_axis=0, concat_axis=0, tiled=T...  40.3 us
    all_to_all x3, waiting for transfers between devices, exchange(): lax.all_to_all(values, ('gx', 'gy'), split_axis=0, concat_axis=0, tiled=T...  29.5 us
    all_to_all x3, starting transfers between devices, exchange(): lax.all_to_all(values, ('gx', 'gy'), split_axis=0, concat_axis=0, tiled=T...  10.5 us
    unnamed x47, local copies, waits for them, and re-layouts  10.1 us
    ppermute x4, starting transfers between devices, ring(): lax.ppermute(values, axis, [(i, (i + step) % count) for i in range(count)])  7.71 us
    pallas_call x1, Pallas kernels, per_device_fast(): call(functools.partial(outer_kernel, 1.0 / math.sqrt(total_x * total_y *...  6.88 us
    pallas_call x1, Pallas kernels, per_device_fast(): call(functools.partial(field_kernel, (cells_x, cells_y, modes_z)), (like(...  6.66 us
    pallas_call x1, Pallas kernels, per_device_fast(): call(functools.partial(spectral_kernel, shape), (like(modes_y, LANES), li...  5.2 us
  transfers between devices with their start and end apart: 7, of which 6 were waited for; matrix products, arithmetic and copies ran while one was open for 1% of the time, Pallas kernels for 3%

profile of v1, /device:TPU:0, one launch (start us, length us, event | category | flops | bytes accessed | tf_op | source)
XLA Modules:
  0.0 132.2 jit_solution(567260959102907432)
XLA Ops:
  0.6 0.0 copy-start
  0.6 0.0 copy-start.14
  0.7 0.0 copy-start.10
  0.7 0.0 copy-start.8
  0.7 0.0 copy-start.12
  0.7 0.0 copy-start.20
  0.7 0.8 fusion.2
  1.5 0.8 fusion
  2.3 0.5 collective-permute-start
  2.8 2.0 %collective-permute-start.1 = (f32[5,8,256]{2,1,0:T(8,128)S(1)}, f32[5,8,256]{2,1,0:T(8,128)S(1)}, u32[]{:S(2)}, u32[]{:S(2)}) collective-permute-start(f32[5,8,256]{2,1,0:T(8,128)S(1)} %pad_maximum_fusion.1), channel_id=1, source_target_pairs={{0,24},{8,0},{16,8},{24,16},{1,25},{9,1},{17,9},{25,17},{2,26},{10... | collective-permute-start | bytes 122888 | tf_op jit(solution)/shard_map/ppermute | solution.py:850
  4.8 1.6 %collective-permute-done.before_ref = f32[5,8,256]{2,1,0:T(8,128)S(1)} collective-permute-done((f32[5,8,256]{2,1,0:T(8,128)S(1)}, f32[5,8,256]{2,1,0:T(8,128)S(1)}, u32[]{:S(2)}, u32[]{:S(2)}) %collective-permute-start) | collective-permute-done | bytes 40992 | tf_op jit(solution)/shard_map/ppermute | solution.py:850
  6.4 0.3 collective-permute-done.1.after_ref
  6.7 0.8 copy-done.2
  7.5 0.8 copy-done.4
  8.4 0.8 copy-done.6
  9.2 2.1 %collective-permute-start.2 = (f32[10,8,256]{2,1,0:T(8,128)S(1)}, f32[10,8,256]{2,1,0:T(8,128)S(1)}, u32[]{:S(2)}, u32[]{:S(2)}) collective-permute-start(f32[10,8,256]{2,1,0:T(8,128)S(1)} %get-tuple-element.18), channel_id=1, source_target_pairs={{0,1},{1,2},{2,3},{3,4},{4,5},{5,6},{6,7},{7,0},{8,9},{9,10},{10,1... | collective-permute-start | bytes 245768 | tf_op jit(solution)/shard_map/ppermute | solution.py:850
  11.3 3.1 %collective-permute-start.3 = (f32[10,8,256]{2,1,0:T(8,128)S(1)}, f32[10,8,256]{2,1,0:T(8,128)S(1)}, u32[]{:S(2)}, u32[]{:S(2)}) collective-permute-start(f32[10,8,256]{2,1,0:T(8,128)S(1)} %get-tuple-element.19), channel_id=1, source_target_pairs={{0,7},{1,0},{2,1},{3,2},{4,3},{5,4},{6,5},{7,6},{8,15},{9,8},{10,9... | collective-permute-start | bytes 245768 | tf_op jit(solution)/shard_map/ppermute | solution.py:850
  14.4 0.8 copy.24.lift_ref
  15.2 1.7 %collective-permute-done.2.low_ref = f32[10,8,256]{2,1,0:T(8,128)S(1)} collective-permute-done((f32[10,8,256]{2,1,0:T(8,128)S(1)}, f32[10,8,256]{2,1,0:T(8,128)S(1)}, u32[]{:S(2)}, u32[]{:S(2)}) %collective-permute-start.2) | collective-permute-done | bytes 81952 | tf_op jit(solution)/shard_map/ppermute | solution.py:850
  16.9 1.2 collective-permute-done.3.high_ref
  18.1 0.8 copy-done.3
  18.9 0.8 copy-done.5
  19.8 0.8 copy-done.7
  20.6 0.9 copy-done.9
  21.5 1.9 %shard_map.218 = (f32[8,8,256]{2,1,0:T(8,128)}, f32[8,8,256]{2,1,0:T(8,128)}, f32[64,128]{1,0:T(8,128)}) custom-call(f32[8,8,256]{2,1,0:T(8,128)S(1)} %copy-done.3, f32[8,8,256]{2,1,0:T(8,128)S(1)} %copy-done.5, f32[8,8,256]{2,1,0:T(8,128)S(1)} %copy-done.7, f32[5,8,256]{2,1,0:T(8,128)S(1)} %collective-permute-done.before_ref, ...), custom_call_target="tpu_custom_call" | custom-call | flops 6553600 | bytes 1310720 | tf_op jit(solution)/shard_map/pallas_call | solution.py:864
  23.4 5.3 %all-to-all-start = ((f32[32,2,128]{2,1,0:T(2,128)}), f32[32,2,128]{2,1,0:T(2,128)S(1)}, u32[]{:S(2)}, u32[]{:S(2)}) async-start(f32[32,2,128]{2,1,0:T(2,128)} %bitcast), calls=%async_computation | async-start | bytes 65536 | tf_op jit(solution)/shard_map/all_to_all | solution.py:805
  28.7 0.0 copy-start.1
  28.7 3.4 %copy-done.1 = f32[2,8,4,32,1024]{4,3,2,1,0:T(8,128)S(1)} copy-done((f32[2,8,4,32,1024]{4,3,2,1,0:T(8,128)S(1)}, f32[2,8,4,32,1024]{4,3,2,1,0:T(8,128)}, u32[]{:S(2)}) %copy-start.1) | copy-done | bytes 8388632
  32.1 4.1 %shard_map.219 = f32[1024,128]{1,0:T(8,128)S(1)} custom-call(f32[2,8,4,32,1024]{4,3,2,1,0:T(8,128)S(1)} %copy-done.1, f32[32,2]{1,0:T(8,128)S(1)} %copy.24.lift_ref), custom_call_target="tpu_custom_call" | custom-call | flops 1073741824 | bytes 8388608 | tf_op jit(solution)/shard_map/pallas_call | solution.py:834
  36.2 0.0 all-to-all-done
  36.2 22.0 %all_to_all.55 = f32[32,32,128]{2,1,0:T(8,128)S(1)} all-to-all(f32[32,32,128]{2,1,0:T(8,128)S(1)} %bitcast.24), channel_id=1, replica_groups=mesh['gx'=4,'gy'=8] {'gx','gy'}, dimensions={0} | all-to-all | bytes 1048576 | tf_op jit(solution)/shard_map/all_to_all | solution.py:805
  58.2 0.0 copy-done.8
  58.2 0.0 copy-done.12
  58.2 5.2 %shard_map.220 = (f32[32,128]{1,0:T(8,128)S(1)}, f32[1024,128]{1,0:T(8,128)}) custom-call(f32[64,128]{1,0:T(8,128)S(1)} %bitcast.30, f32[1024,128]{1,0:T(8,128)S(1)} %bitcast.25, bf16[64,384]{1,0:T(8,128)(2,1)S(1)} %copy-done.12, bf16[384,128]{1,0:T(8,128)(2,1)S(1)} %copy-done.8, bf16[128,192]{1,0:T(8,128)(2,1)S(1)} %copy-done.10, bf16[64,192]{1,0:T(8,128)(2,1)S(1)} %copy-done.14), custom_call_target="tpu_custom_call" | custom-call | flops 100000000 | bytes 2000000 | tf_op jit(solution)/shard_map/pallas_call | solution.py:873
  63.4 2.6 %all-to-all-start.2 = ((f32[32,32,128]{2,1,0:T(8,128)}), f32[32,32,128]{2,1,0:T(8,128)S(1)}, u32[]{:S(2)}, u32[]{:S(2)}) async-start(f32[32,32,128]{2,1,0:T(8,128)} %bitcast.4), calls=%async_computation.2 | async-start | bytes 1048576 | tf_op jit(solution)/shard_map/all_to_all | solution.py:805
  66.1 0.0 copy-done
  66.1 0.0 copy-done.20
  66.1 0.1 fusion.3
  66.2 0.0 copy-done.21
  66.3 0.1 tile.9.vector_ref
  66.4 16.1 %all-to-all-done.2 = f32[32,32,128]{2,1,0:T(8,128)S(1)} async-done(((f32[32,32,128]{2,1,0:T(8,128)}), f32[32,32,128]{2,1,0:T(8,128)S(1)}, u32[]{:S(2)}, u32[]{:S(2)}) %all-to-all-start.2) | async-done | bytes 524320 | tf_op jit(solution)/shard_map/all_to_all | solution.py:805
  82.4 6.7 %shard_map.221 = (f32[64,256]{1,0:T(8,128)}, f32[1024,128]{1,0:T(8,128)S(1)}) custom-call(f32[1024,128]{1,0:T(8,128)S(1)} %bitcast.27, f32[64,256]{1,0:T(8,128)S(1)} %bitcast.32, f32[64,256]{1,0:T(8,128)S(1)} %bitcast.33, f32[64,256]{1,0:T(8,128)S(1)} %bitcast.31, f32[4,256]{1,0:T(4,128)S(1)} %tile.9.vector_ref, bf16[256,192]{1,0:T(8,128)(2,1)S(1)} %copy-done.18, ...), custom_call_target="tpu_custom_call" | custom-call | flops 1000000000 | bytes 2000000 | tf_op jit(solution)/shard_map/pallas_call | solution.py:895
  89.1 18.3 %all_to_all.56 = f32[32,32,128]{2,1,0:T(8,128)S(1)} all-to-all(f32[32,32,128]{2,1,0:T(8,128)S(1)} %bitcast.28), channel_id=1, replica_groups=mesh['gx'=4,'gy'=8] {'gx','gy'}, dimensions={0} | all-to-all | bytes 1048576 | tf_op jit(solution)/shard_map/all_to_all | solution.py:805
  107.4 1.8 %shard_map.222 = f32[768,128]{1,0:T(8,128)} custom-call(f32[1024,128]{1,0:T(8,128)S(1)} %bitcast.26, f32[32,128]{1,0:T(8,128)S(1)} %get-tuple-element.26.modes_ref, bf16[64,192]{1,0:T(8,128)(2,1)S(1)} %copy-done.13, bf16[64,384]{1,0:T(8,128)(2,1)S(1)} %copy-done.11), custom_call_target="tpu_custom_call" | custom-call | flops 100000000 | bytes 2000000 | tf_op jit(solution)/shard_map/pallas_call | solution.py:912
  109.2 2.6 %all-to-all-start.4 = ((f32[32,24,128]{2,1,0:T(8,128)}), f32[32,24,128]{2,1,0:T(8,128)S(1)}, u32[]{:S(2)}, u32[]{:S(2)}) async-start(f32[32,24,128]{2,1,0:T(8,128)} %bitcast.16), calls=%async_computation.4 | async-start | bytes 786432 | tf_op jit(solution)/shard_map/all_to_all | solution.py:805
  111.8 0.1 tile.21.lift_ref
  111.9 13.4 %all-to-all-done.4 = f32[32,24,128]{2,1,0:T(8,128)S(1)} async-done(((f32[32,24,128]{2,1,0:T(8,128)}), f32[32,24,128]{2,1,0:T(8,128)S(1)}, u32[]{:S(2)}, u32[]{:S(2)}) %all-to-all-start.4) | async-done | bytes 393248 | tf_op jit(solution)/shard_map/all_to_all | solution.py:805
  125.3 6.9 %shard_map.223 = (f32[2,8,4,32,1024]{4,3,2,1,0:T(8,128)}, f32[32,32]{1,0:T(8,128)}, f32[1,32]{1,0:T(1,128)}) custom-call(f32[768,128]{1,0:T(8,128)S(1)} %bitcast.29, f32[2,1024]{1,0:T(2,128)S(1)} %tile.21.lift_ref), custom_call_target="tpu_custom_call" | custom-call | flops 1073741824 | bytes 8388608 | tf_op jit(solution)/shard_map/pallas_call | solution.py:924
  (33 shorter events, 0.1 us)
Async XLA Ops:
  0.6 65.4 %copy-start = (f32[32,32]{1,0:T(8,128)S(1)}, f32[32,32]{1,0:T(8,128)}, u32[]{:S(2)}) copy-start(f32[32,32]{1,0:T(8,128)} %param.23) | copy-start | bytes 12292
  0.6 57.6 %copy-start.14 = (bf16[64,192]{1,0:T(8,128)(2,1)S(1)}, bf16[64,192]{1,0:T(8,128)(2,1)}, u32[]{:S(2)}) copy-start(bf16[64,192]{1,0:T(8,128)(2,1)} %constant.22.clone.x_out_ref) | copy-start | bytes 73732
  0.7 57.6 %copy-start.10 = (bf16[128,192]{1,0:T(8,128)(2,1)S(1)}, bf16[128,192]{1,0:T(8,128)(2,1)}, u32[]{:S(2)}) copy-start(bf16[128,192]{1,0:T(8,128)(2,1)} %constant.21.clone.y_out_ref) | copy-start | bytes 147460
  0.7 57.6 %copy-start.8 = (bf16[384,128]{1,0:T(8,128)(2,1)S(1)}, bf16[384,128]{1,0:T(8,128)(2,1)}, u32[]{:S(2)}) copy-start(bf16[384,128]{1,0:T(8,128)(2,1)} %constant.20.clone.x_in_ref) | copy-start | bytes 294916
  0.7 57.5 %copy-start.12 = (bf16[64,384]{1,0:T(8,128)(2,1)S(1)}, bf16[64,384]{1,0:T(8,128)(2,1)}, u32[]{:S(2)}) copy-start(bf16[64,384]{1,0:T(8,128)(2,1)} %constant.19.clone.y_in_ref) | copy-start | bytes 147460
  0.7 65.4 %copy-start.20 = (f32[32,2]{0,1:T(2,128)S(1)}, f32[32,2]{0,1:T(2,128)}, u32[]{:S(2)}) copy-start(f32[32,2]{0,1:T(2,128)} %param.21) | copy-start | bytes 772
  0.7 65.5 %copy-start.21 = (f32[32]{0:T(128)S(1)}, f32[32]{0:T(128)}, u32[]{:S(2)}) copy-start(f32[32]{0:T(128)} %param.25) | copy-start | bytes 388
  0.7 65.5 %copy-start.22 = (f32[32]{0:T(128)S(1)}, f32[32]{0:T(128)}, u32[]{:S(2)}) copy-start(f32[32]{0:T(128)} %param.24) | copy-start | bytes 388
  0.7 81.7 %copy-start.15 = (f32[8,8,256]{2,1,0:T(8,128)S(1)}, f32[8,8,256]{2,1,0:T(8,128)}, u32[]{:S(2)}) copy-start(f32[8,8,256]{2,1,0:T(8,128)} %param.26) | copy-start | bytes 196612
  2.3 4.1 %collective-permute-start = (f32[5,8,256]{2,1,0:T(8,128)S(1)}, f32[5,8,256]{2,1,0:T(8,128)S(1)}, u32[]{:S(2)}, u32[]{:S(2)}) collective-permute-start(f32[5,8,256]{2,1,0:T(8,128)S(1)} %pad_maximum_fusion), channel_id=1, source_target_pairs={{0,8},{8,16},{16,24},{24,0},{1,9},{9,17},{17,25},{25,1},{2,10},{10... | collective-permute-start | bytes 122888 | tf_op jit(solution)/shard_map/ppermute | solution.py:850
  2.8 3.9 %collective-permute-start.1 = (f32[5,8,256]{2,1,0:T(8,128)S(1)}, f32[5,8,256]{2,1,0:T(8,128)S(1)}, u32[]{:S(2)}, u32[]{:S(2)}) collective-permute-start(f32[5,8,256]{2,1,0:T(8,128)S(1)} %pad_maximum_fusion.1), channel_id=1, source_target_pairs={{0,24},{8,0},{16,8},{24,16},{1,25},{9,1},{17,9},{25,17},{2,26},{10... | collective-permute-start | bytes 122888 | tf_op jit(solution)/shard_map/ppermute | solution.py:850
  6.7 0.8 copy-start.2
  7.5 0.8 copy-start.4
  8.4 0.8 copy-start.6
  9.2 73.2 %copy-start.18 = (bf16[256,192]{1,0:T(8,128)(2,1)S(1)}, bf16[256,192]{1,0:T(8,128)(2,1)}, u32[]{:S(2)}) copy-start(bf16[256,192]{1,0:T(8,128)(2,1)} %constant.23.clone.back_ref) | copy-start | bytes 294916
  9.2 73.2 %copy-start.19 = (bf16[64,768]{1,0:T(8,128)(2,1)S(1)}, bf16[64,768]{1,0:T(8,128)(2,1)}, u32[]{:S(2)}) copy-start(bf16[64,768]{1,0:T(8,128)(2,1)} %constant.24.clone.forth_ref) | copy-start | bytes 294916
  9.2 7.6 %collective-permute-start.2 = (f32[10,8,256]{2,1,0:T(8,128)S(1)}, f32[10,8,256]{2,1,0:T(8,128)S(1)}, u32[]{:S(2)}, u32[]{:S(2)}) collective-permute-start(f32[10,8,256]{2,1,0:T(8,128)S(1)} %get-tuple-element.18), channel_id=1, source_target_pairs={{0,1},{1,2},{2,3},{3,4},{4,5},{5,6},{6,7},{7,0},{8,9},{9,10},{10,1... | collective-permute-start | bytes 245768 | tf_op jit(solution)/shard_map/ppermute | solution.py:850
  11.3 6.8 %collective-permute-start.3 = (f32[10,8,256]{2,1,0:T(8,128)S(1)}, f32[10,8,256]{2,1,0:T(8,128)S(1)}, u32[]{:S(2)}, u32[]{:S(2)}) collective-permute-start(f32[10,8,256]{2,1,0:T(8,128)S(1)} %get-tuple-element.19), channel_id=1, source_target_pairs={{0,7},{1,0},{2,1},{3,2},{4,3},{5,4},{6,5},{7,6},{8,15},{9,8},{10,9... | collective-permute-start | bytes 245768 | tf_op jit(solution)/shard_map/ppermute | solution.py:850
  18.1 0.8 copy-start.3
  18.9 0.8 copy-start.5
  19.8 0.8 copy-start.7
  20.6 0.9 copy-start.9
  21.5 85.9 %copy-start.13 = (bf16[64,192]{1,0:T(8,128)(2,1)S(1)}, bf16[64,192]{1,0:T(8,128)(2,1)}, u32[]{:S(2)}) copy-start(bf16[64,192]{1,0:T(8,128)(2,1)} %constant.25.clone.x_in_ref) | copy-start | bytes 73732
  23.4 84.0 %copy-start.11 = (bf16[64,384]{1,0:T(8,128)(2,1)S(1)}, bf16[64,384]{1,0:T(8,128)(2,1)}, u32[]{:S(2)}) copy-start(bf16[64,384]{1,0:T(8,128)(2,1)} %constant.26.clone.y_in_ref) | copy-start | bytes 147460
  23.4 12.8 %all-to-all-start = ((f32[32,2,128]{2,1,0:T(2,128)}), f32[32,2,128]{2,1,0:T(2,128)S(1)}, u32[]{:S(2)}, u32[]{:S(2)}) async-start(f32[32,2,128]{2,1,0:T(2,128)} %bitcast), calls=%async_computation | async-start | bytes 65536 | tf_op jit(solution)/shard_map/all_to_all | solution.py:805
  28.7 3.4 %copy-start.1 = (f32[2,8,4,32,1024]{4,3,2,1,0:T(8,128)S(1)}, f32[2,8,4,32,1024]{4,3,2,1,0:T(8,128)}, u32[]{:S(2)}) copy-start(f32[2,8,4,32,1024]{4,3,2,1,0:T(8,128)} %weight_ref.1) | copy-start | bytes 25165828
  32.1 50.3 %copy-start.16 = (f32[8,8,256]{2,1,0:T(8,128)S(1)}, f32[8,8,256]{2,1,0:T(8,128)}, u32[]{:S(2)}) copy-start(f32[8,8,256]{2,1,0:T(8,128)} %get-tuple-element.12) | copy-start | bytes 196612
  32.1 50.3 %copy-start.17 = (f32[8,8,256]{2,1,0:T(8,128)S(1)}, f32[8,8,256]{2,1,0:T(8,128)}, u32[]{:S(2)}) copy-start(f32[8,8,256]{2,1,0:T(8,128)} %get-tuple-element.13) | copy-start | bytes 196612
  63.4 19.0 %all-to-all-start.2 = ((f32[32,32,128]{2,1,0:T(8,128)}), f32[32,32,128]{2,1,0:T(8,128)S(1)}, u32[]{:S(2)}, u32[]{:S(2)}) async-start(f32[32,32,128]{2,1,0:T(8,128)} %bitcast.4), calls=%async_computation.2 | async-start | bytes 1048576 | tf_op jit(solution)/shard_map/all_to_all | solution.py:805
  109.2 16.1 %all-to-all-start.4 = ((f32[32,24,128]{2,1,0:T(8,128)}), f32[32,24,128]{2,1,0:T(8,128)S(1)}, u32[]{:S(2)}, u32[]{:S(2)}) async-start(f32[32,24,128]{2,1,0:T(8,128)} %bitcast.16), calls=%async_computation.4 | async-start | bytes 786432 | tf_op jit(solution)/shard_map/all_to_all | solution.py:805

commit v2 on v1

--- a/solution.py
+++ b/solution.py
@@ -235,6 +235,9 @@
 
 
 LANES = 128
+SMALL_VMEM = 24 * 1024 * 1024
+LARGE_VMEM = 56 * 1024 * 1024
+PACK_COST = 50_000_000_000
 SPREAD = LANES // WIDTH
 NARROW = jnp.bfloat16
 EXACT = lax.Precision.HIGHEST
@@ -264,6 +267,10 @@
 def thrice(values, axis):
     head, rest = parts_of(values)
     return jnp.concatenate([head, rest, head], axis=axis)
+
+
+def one_where(mask):
+    return mask.astype(jnp.float32).astype(NARROW)
 
 
 def mul(left, right):
@@ -314,46 +321,64 @@
     ]
 
 
-def contract_kernel(weight_ref, lift_ref, out_ref, mix_ref):
-    _, planes, own_y, modes_z, _ = weight_ref.shape
-    own_x = pl.num_programs(0) * planes
-    step = pl.program_id(0)
-
-    @pl.when(step == 0)
-    def _():
-        shape = (WIDTH, LANES)
-        lane = lax.broadcasted_iota(jnp.int32, shape, 1)
-        base = jnp.where(
-            lane % (2 * WIDTH) < WIDTH,
-            jnp.broadcast_to(lift_ref[:, 0:1], shape),
-            jnp.broadcast_to(lift_ref[:, 1:2], shape),
-        )
-        for channel in range(WIDTH):
-            block = jnp.where(lane % WIDTH == channel, base, 0.0)
-            head, rest = parts_of(block)
-            both = jnp.where(lane < 2 * WIDTH, head.astype(jnp.float32), rest.astype(jnp.float32))
-            mix_ref[channel * WIDTH : (channel + 1) * WIDTH, :] = both.astype(NARROW)
-
-    mixing = mix_ref[...]
+def contract_kernel(planes, lift_ref, weight_ref, out_ref, held, arrived):
+    _, own_x, own_y, modes_z, width = weight_ref.shape
+    chunk = out_ref.shape[0] // modes_z
+    steps = own_x // planes
+
+    def fetch(step):
+        block = pl.ds(step * planes, planes)
+        return pltpu.make_async_copy(
+            weight_ref.at[:, block], held.at[:, block], arrived.at[step]
+        )
+
+    for step in range(steps):
+        fetch(step).start()
+    square = (WIDTH, WIDTH)
+    diagonal = lax.broadcasted_iota(jnp.int32, square, 0) == lax.broadcasted_iota(
+        jnp.int32, square, 1
+    )
+    columns = [
+        jnp.sum(
+            jnp.where(diagonal, jnp.broadcast_to(lift_ref[k : k + 1, :], square), 0.0),
+            axis=1,
+            keepdims=True,
+        )
+        for k in range(2)
+    ]
+    lane = lax.broadcasted_iota(jnp.int32, (WIDTH, LANES), 1)
+    base = jnp.where(
+        lane % (2 * WIDTH) < WIDTH,
+        jnp.broadcast_to(columns[0], lane.shape),
+        jnp.broadcast_to(columns[1], lane.shape),
+    )
+    head, rest = parts_of(base)
+    base = jnp.where(lane < 2 * WIDTH, head.astype(jnp.float32), rest.astype(jnp.float32))
+    mixing = jnp.concatenate(
+        [jnp.where(lane % WIDTH == channel, base, 0.0) for channel in range(WIDTH)], axis=0
+    ).astype(NARROW)
     rows = planes * own_y * modes_z
-    sums = []
-    for part in range(2):
-        head, rest = parts_of(weight_ref[part].reshape(rows, WIDTH * WIDTH))
-        total = mul(head, mixing) + mul(rest, mixing)
-        sums.append(total + pltpu.roll(total, 2 * WIDTH, 1))
-    lane = lax.broadcasted_iota(jnp.int32, (rows, LANES), 1)
-    result = jnp.where(lane < 2 * WIDTH, sums[0], sums[1])
-    for plane in range(planes):
-        for row in range(own_y):
-            first = (plane * own_y + row) * modes_z
-            place = row * own_x + step * planes + plane
-            out_ref[pl.ds(place, modes_z, stride=own_x * own_y), :] = result[
-                first : first + modes_z
-            ]
-
-
-def pack_kernel(phase_ref, solute_ref, cool_ref, before_ref, after_ref, head_ref, tail_ref):
-    cells_x, cells_y, _ = phase_ref.shape
+    low = lax.broadcasted_iota(jnp.int32, (rows, LANES), 1) < 2 * WIDTH
+    for step in range(steps):
+        fetch(step).wait()
+        sums = []
+        for part in range(2):
+            block = held[part, step * planes : (step + 1) * planes]
+            head, rest = parts_of(block.reshape(rows, width))
+            total = mul(head, mixing) + mul(rest, mixing)
+            sums.append(total + turn(total, 2 * WIDTH))
+        result = jnp.where(low, sums[0], sums[1])
+        for plane in range(planes):
+            for row in range(own_y):
+                first = (plane * own_y + row) * modes_z
+                place = row * own_x + step * planes + plane
+                out_ref[pl.ds(place, modes_z, stride=chunk), :] = result[
+                    first : first + modes_z
+                ]
+
+
+def pack_kernel(held_ref, before_ref, after_ref, head_ref, tail_ref):
+    _, cells_x, cells_y, _ = held_ref.shape
 
     def put(target, phase, solute, cool):
         head_ref[target, 0:2] = phase[:, 0:2]
@@ -364,38 +389,38 @@
         tail_ref[target, 4:5] = cool[:, cells_y - 1 : cells_y]
 
     put(slice(0, 1), before_ref[1:2], before_ref[3:4], before_ref[4:5])
-    put(slice(1, cells_x + 1), phase_ref[...], solute_ref[...], cool_ref[...])
+    put(slice(1, cells_x + 1), held_ref[0], held_ref[1], held_ref[2])
     put(slice(cells_x + 1, cells_x + 2), after_ref[0:1], after_ref[2:3], after_ref[4:5])
 
 
 def step_kernel(
-    phase_ref,
-    solute_ref,
-    cool_ref,
+    held_ref,
     before_ref,
     after_ref,
     low_ref,
     high_ref,
     table_ref,
+    mixed_ref,
     phase_out,
     solute_out,
-    spec_out,
+    send_ref,
     phase_ext,
     solute_ext,
     cool_ext,
     diff_ext,
     lines,
 ):
-    cells_x, cells_y, depth = phase_ref.shape
+    _, cells_x, cells_y, depth = held_ref.shape
     base = 8
     end = base + cells_y
-    for ext, own, first in ((phase_ext, phase_ref, 0), (solute_ext, solute_ref, 2)):
-        ext[2 : cells_x + 2, base:end] = own[...]
+    for index, ext in enumerate((phase_ext, solute_ext)):
+        first = 2 * index
+        ext[2 : cells_x + 2, base:end] = held_ref[index]
         ext[0:2, base:end] = before_ref[first : first + 2]
         ext[cells_x + 2 : cells_x + 4, base:end] = after_ref[first : first + 2]
         ext[1 : cells_x + 3, base - 2 : base] = low_ref[:, first : first + 2]
         ext[1 : cells_x + 3, end : end + 2] = high_ref[:, first : first + 2]
-    cool_ext[2 : cells_x + 2, base:end] = cool_ref[...]
+    cool_ext[2 : cells_x + 2, base:end] = held_ref[2]
     cool_ext[1:2, base:end] = before_ref[4:5]
     cool_ext[cells_x + 2 : cells_x + 3, base:end] = after_ref[4:5]
     cool_ext[1 : cells_x + 3, base - 1 : base] = low_ref[:, 4:5]
@@ -457,13 +482,37 @@
             )
         )
     ordered = jnp.concatenate(ordered, axis=1)
-    spec_out[...] = mul_rows(table_ref[...], thrice(ordered, 1))
+    spectra = mul_rows(table_ref[...], thrice(ordered, 1))
+    send_ref[...] = mixed_ref[...]
+    modes_z = spectra.shape[0] // 2
+    chunk = send_ref.shape[0] // modes_z
+    for part in range(2):
+        send_ref[pl.ds(chunk - 2 + part, modes_z, stride=chunk), :] = spectra[
+            part * modes_z : (part + 1) * modes_z
+        ]
+
+
+def pack_modes(shape, modes, modes_ref, rows_ref):
+    count_x, count_y, _, _, own_x, own_y = shape
+    modes_x, modes_y = count_x * own_x, count_y * own_y
+    lane = lax.broadcasted_iota(jnp.int32, (modes_y, LANES), 1)
+    for index in range(count_x):
+        block = modes
+        for k in range(4):
+            shift = k * own_x - k * modes_x - index * own_x
+            block = jnp.where(lane // own_x == k, turn(modes, shift), block)
+        rows_ref[index] = block
+        line = rows_ref[index, pl.ds(0, count_y, stride=own_y), :]
+        groups = group_of(line.shape)
+        for row in range(1, own_y):
+            piece = rows_ref[index, pl.ds(row, count_y, stride=own_y), :]
+            line = jnp.where(groups == row, turn(piece, row * WIDTH), line)
+        modes_ref[index * count_y : (index + 1) * count_y] = line
 
 
 def spectral_kernel(
     shape,
-    spec_ref,
-    weight_ref,
+    mixed_ref,
     y_in_ref,
     x_in_ref,
     y_out_ref,
@@ -472,6 +521,8 @@
     send_ref,
     lines_y,
     lines_x,
+    rows_ref,
+    weight_ref,
 ):
     count_x, count_y, cells_x, cells_y, own_x, own_y = shape
     modes_x, modes_y = count_x * own_x, count_y * own_y
@@ -479,139 +530,190 @@
     tile = cells_x * cells_y
     narrow = 2 * cells_x
     rows = 2 * count_y
+    devices = count_x * count_y
+    own = own_x * own_y
+    chunk = mixed_ref.shape[0] // devices
+    spectra = [mixed_ref[pl.ds(own + part, devices, stride=chunk), :] for part in range(2)]
+    for index in range(devices):
+        weight_ref[index * own : (index + 1) * own, :] = mixed_ref[
+            index * chunk : index * chunk + own, :
+        ]
     lane = lax.broadcasted_iota(jnp.int32, (rows, LANES), 1)
     blocks = []
     for row in range(cells_y):
         block = jnp.zeros((rows, LANES), jnp.float32)
         for index in range(count_x):
-            piece = turn(spec_ref[index * rows : (index + 1) * rows, :], narrow * (index - row))
+            piece = jnp.concatenate(
+                [values[index * count_y : (index + 1) * count_y] for values in spectra], axis=0
+            )
+            piece = turn(piece, narrow * (index - row))
             block = jnp.where(lane // narrow == index, piece, block)
         blocks.append(block)
     along_y = mul(y_in_ref[...], thrice(jnp.concatenate(blocks, axis=0), 0))
     half = lax.broadcasted_iota(jnp.int32, (modes_y, LANES), 1) < LANES // 2
     joined = jnp.where(half, along_y[0:modes_y], turn(along_y[modes_y:], LANES // 2))
     modes = mul(thrice(joined, 1), x_in_ref[...])
-    modes_ref[...] = modes
-    groups = group_of((modes_y, LANES))
     quads_y = total_y // SPREAD
-    for quad in range(modes_x // SPREAD):
-        reals, imags = [], []
+    quads_x = modes_x // SPREAD
+    lane = lax.broadcasted_iota(jnp.int32, (modes_y, LANES), 1) % modes_x
+    chosen = jnp.concatenate(
+        [jnp.where(lane == freq, modes, 0.0) for freq in range(modes_x)], axis=0
+    )
+    place = lax.broadcasted_iota(jnp.int32, (2 * LANES, 2 * LANES), 0) % LANES // modes_x
+    group = lax.broadcasted_iota(jnp.int32, (2 * LANES, 2 * LANES), 1) // WIDTH
+    same = jnp.where(group < 4, group, (group + 2) % 4)
+    signed_one = jnp.where((group == 2) | (group == 3), -1.0, 1.0)
+    spread = jnp.where(place == same, signed_one, 0.0).astype(NARROW)
+    columns = mul(jnp.concatenate(parts_of(chosen), axis=1), spread)
+    products = [[], []]
+    for quad in range(quads_x):
+        lines = [[], []]
         for index in range(SPREAD):
             freq = SPREAD * quad + index
             start = (freq // own_x) * count_y * own_y * own_x + freq % own_x
             weights = weight_ref[pl.ds(start, modes_y, stride=own_x), :]
-            columns = [
-                jnp.broadcast_to(
-                    modes[:, k * modes_x + freq : k * modes_x + freq + 1], (modes_y, LANES)
-                )
-                for k in range(4)
-            ]
-            first = weights * pick(groups, [columns[0], columns[1], -columns[2], -columns[3]])
-            second = weights * pick(groups, [columns[2], columns[3], columns[0], columns[1]])
-            first = first + turn(first, 2 * WIDTH)
-            second = second + turn(second, 2 * WIDTH)
-            reals.append(first + turn(first, WIDTH))
-            imags.append(second + turn(second, WIDTH))
-        stacked = jnp.concatenate([pick(groups, reals), pick(groups, imags)], axis=0)
-        lines_y[...] = mul(y_out_ref[...], thrice(stacked, 0))
+            for part in range(2):
+                column = columns[
+                    freq * modes_y : (freq + 1) * modes_y, part * LANES : (part + 1) * LANES
+                ]
+                lines[part].append(weights * column)
+        for part in range(2):
+            products[part].append(jnp.concatenate(lines[part], axis=1))
+    products = jnp.concatenate(products[0] + products[1], axis=0)
+    gather = lax.broadcasted_iota(jnp.int32, (2 * SPREAD * LANES, LANES), 0) % (SPREAD * LANES)
+    column = lax.broadcasted_iota(jnp.int32, (2 * SPREAD * LANES, LANES), 1)
+    gather = one_where(gather // LANES * WIDTH + gather % WIDTH == column)
+    products = mul(jnp.concatenate(parts_of(products), axis=1), gather)
+    stacked = [
+        jnp.concatenate(
+            [
+                products[(part * quads_x + quad) * modes_y : (part * quads_x + quad + 1) * modes_y]
+                for part in range(2)
+            ],
+            axis=0,
+        )
+        for quad in range(quads_x)
+    ]
+    back = mul(y_out_ref[...], thrice(jnp.concatenate(stacked, axis=1), 0))
+    for quad in range(quads_x):
+        lines_y[quad] = back[:, quad * LANES : (quad + 1) * LANES]
+    for quad in range(quads_x):
         for part in range(2):
             pieces = [
-                lines_y[pl.ds(part * total_y + i, quads_y, stride=SPREAD), :] for i in range(SPREAD)
+                lines_y[quad, pl.ds(part * total_y + i, quads_y, stride=SPREAD), :]
+                for i in range(SPREAD)
             ]
             for index, piece in enumerate(swap_groups(pieces)):
                 place = part * modes_x + SPREAD * quad + index
                 lines_x[pl.ds(place, quads_y, stride=2 * modes_x), :] = piece
     per_tile = cells_y // SPREAD
+    blocks = [
+        lines_x[quad * 2 * modes_x : (quad + 1) * 2 * modes_x, :] for quad in range(quads_y)
+    ]
+    back = mul(x_out_ref[...], thrice(jnp.concatenate(blocks, axis=1), 0))
     for quad in range(quads_y):
-        block = lines_x[quad * 2 * modes_x : (quad + 1) * 2 * modes_x, :]
-        back = mul(x_out_ref[...], thrice(block, 0))
         for part in range(2):
             for index in range(count_x):
                 device = index * count_y + quad // per_tile
                 place = (device * 2 + part) * per_tile + quad % per_tile
                 first = part * total_x + index * cells_x
                 send_ref[place * cells_x : (place + 1) * cells_x, :] = back[
-                    first : first + cells_x
+                    first : first + cells_x, quad * LANES : (quad + 1) * LANES
                 ]
+    pack_modes(shape, modes, modes_ref, rows_ref)
+
+
+def prepare_kernel(
+    phase_ref, solute_ref, cotangent_ref, vector_ref, base_ref, spread_ref, table_ref
+):
+    planes, depth, wide = base_ref.shape
+    tile = phase_ref.shape[0]
+    cells_y = tile // planes
+    fields = (phase_ref[...], solute_ref[...] - SOLUTE_MEAN)
+    spread = jnp.concatenate(
+        [jnp.concatenate(parts_of(values.T), axis=1) for values in fields], axis=0
+    )
+    spread_ref[...] = jnp.concatenate(parts_of(cotangent_ref[...].T), axis=1)
+    cell = lax.broadcasted_iota(jnp.int32, (2 * tile, wide), 0) % tile
+    row = lax.broadcasted_iota(jnp.int32, (2 * tile, wide), 1) // WIDTH
+    for plane in range(planes):
+        values = mul(spread, one_where(cell == plane * cells_y + row))
+        base_ref[plane] = (
+            values[0:depth] * vector_ref[0:1, :]
+            + values[depth:] * vector_ref[1:2, :]
+            + vector_ref[2:3, :]
+        )
+        lines = [values[plane * cells_y : (plane + 1) * cells_y] for values in fields]
+        head, rest = parts_of(jnp.concatenate(lines, axis=0))
+        table_ref[plane] = jnp.concatenate([head, head, rest], axis=1)
 
 
 def field_kernel(
-    shape,
+    cells_y,
     field_ref,
-    phase_ref,
-    solute_ref,
-    cotangent_ref,
+    base_ref,
+    spread_ref,
+    table_ref,
     vector_ref,
     back_ref,
     forth_ref,
     predicted_ref,
     send_ref,
-    spread_ref,
 ):
-    cells_x, cells_y, modes_z = shape
-    tile = cells_x * cells_y
-    depth = phase_ref.shape[1]
-    wide = cells_y * WIDTH
+    planes, depth, wide = base_ref.shape
+    rows = back_ref.shape[1] // 3
     halves_y = cells_y // SPREAD
-    stride = halves_y * cells_x
-    for index, values in enumerate(
-        (phase_ref[...], solute_ref[...] - SOLUTE_MEAN, cotangent_ref[...])
-    ):
-        head, rest = parts_of(values.T)
-        spread_ref[index] = jnp.concatenate([head, rest], axis=1)
-    mix_phase = vector_ref[0:1, :]
-    mix_solute = vector_ref[1:2, :]
-    bias = vector_ref[2:3, :]
+    stride = halves_y * planes
     proj = vector_ref[3:4, :]
     root = math.sqrt(2.0 / math.pi)
     curve = 0.044715
-    cell = lax.broadcasted_iota(jnp.int32, (2 * tile, wide), 0) % tile
-    row = lax.broadcasted_iota(jnp.int32, (2 * tile, wide), 1) // WIDTH
-    picker = (
+    picker = one_where(
         lax.broadcasted_iota(jnp.int32, (cells_y, 2 * wide), 0)
         == lax.broadcasted_iota(jnp.int32, (cells_y, 2 * wide), 1) % wide // WIDTH
-    ).astype(jnp.float32).astype(NARROW)
-
-    def fold(values):
-        return jnp.sum(values.reshape(depth // 8, 8, wide), axis=0)
-
-    def one(plane, sums):
+    )
+    cell = lax.broadcasted_iota(jnp.int32, (2 * planes * cells_y, wide), 0) % (planes * cells_y)
+    cell = cell - lax.broadcasted_iota(jnp.int32, cell.shape, 1) // WIDTH
+    line_sums = jnp.zeros((2 * cells_y, wide), jnp.float32)
+    proj_sums = jnp.zeros((8, wide), jnp.float32)
+    for plane in range(planes):
         spectra = jnp.concatenate(
             [
-                field_ref[pl.ds(part * cells_x + plane, 2 * modes_z, stride=stride), :]
+                field_ref[pl.ds(part * planes + plane, rows, stride=stride), :]
                 for part in range(halves_y)
             ],
             axis=1,
         )
-        field = mul(back_ref[...], thrice(spectra, 0))
-        chosen = (cell == plane * cells_y + row).astype(jnp.float32).astype(NARROW)
-        phase = mul(spread_ref[0], chosen)
-        solute = mul(spread_ref[1], chosen)
-        cotangent = mul(spread_ref[2], chosen)
-        pre = field + phase * mix_phase + solute * mix_solute + bias
+        pre = mul(back_ref[...], thrice(spectra, 0)) + base_ref[plane]
         square = pre * pre
-        bent = jnp.tanh(root * pre * (1.0 + curve * square))
-        upper = 0.5 * (1.0 + bent)
+        bent = jnp.tanh(pre * (root + (root * curve) * square))
+        upper = 0.5 + 0.5 * bent
         active = pre * upper
-        slope = upper + 0.5 * pre * (1.0 - bent * bent) * (root * (1.0 + 3.0 * curve * square))
-        grad = proj * cotangent * slope
-        weighted = jnp.concatenate(parts_of(proj * active), axis=1)
-        predicted_ref[pl.ds(pl.multiple_of(plane * cells_y, cells_y), cells_y), :] = mul_rows(
-            picker, weighted
-        )
-        spectra = mul(forth_ref[...], thrice(grad, 0))
+        slope = upper + (active - active * bent) * (root + (3.0 * root * curve) * square)
+        cotangent = mul(spread_ref[...], one_where(cell == plane * cells_y))
+        weighted = proj * cotangent
+        grad = weighted * slope
+        predicted_ref[plane * cells_y : (plane + 1) * cells_y, :] = mul_rows(
+            picker, jnp.concatenate(parts_of(proj * active), axis=1)
+        )
+        table = jnp.concatenate([forth_ref[...], table_ref[plane]], axis=0)
+        spectra = mul(table, thrice(grad, 0))
         for part in range(halves_y):
-            send_ref[pl.ds(part * cells_x + plane, 2 * modes_z, stride=stride), :] = spectra[
-                :, part * LANES : (part + 1) * LANES
+            send_ref[pl.ds(part * planes + plane, rows, stride=stride), :] = spectra[
+                0:rows, part * LANES : (part + 1) * LANES
             ]
-        return (
-            sums[0] + fold(grad * phase),
-            sums[1] + fold(grad * solute),
-            sums[2] + fold(active * cotangent),
-        )
-
-    zero = jnp.zeros((8, wide), jnp.float32)
-    sums = lax.fori_loop(0, cells_x, one, (zero, zero, zero))
+        line_sums = line_sums + spectra[rows:]
+        proj_sums = proj_sums + jnp.sum(
+            (active * cotangent).reshape(depth // 8, 8, wide), axis=0
+        )
+    shape = (cells_y, wide)
+    own = lax.broadcasted_iota(jnp.int32, shape, 0) == (
+        lax.broadcasted_iota(jnp.int32, shape, 1) // WIDTH
+    )
+    sums = [
+        jnp.where(own, line_sums[0:cells_y], 0.0),
+        jnp.where(own, line_sums[cells_y:], 0.0),
+        proj_sums,
+    ]
     for index, values in enumerate(sums):
         line = jnp.sum(values, axis=0, keepdims=True)
         line = sum(line[:, part * LANES : (part + 1) * LANES] for part in range(halves_y))
@@ -629,20 +731,26 @@
     chunk = 2 * per_tile * cells_x
     first_device = (lax.axis_index("gx") == 0) & (lax.axis_index("gy") == 0)
     keep = jnp.where(first_device, 0.0, 1.0)
+    blocks = []
     for quad in range(quads_y):
-        blocks = []
+        block = []
         for part in range(2):
             for index in range(count_x):
                 device = index * count_y + quad // per_tile
                 place = (device * 2 + part) * per_tile + quad % per_tile
-                block = spectra_ref[place * cells_x : (place + 1) * cells_x, :]
-                blocks.append(block * keep if part else block)
-        lines_x[quad * 2 * modes_x : (quad + 1) * 2 * modes_x, :] = mul(
-            x_in_ref[...], thrice(jnp.concatenate(blocks, axis=0), 0)
-        )
-    out_chunk = send_ref.shape[0] // (count_x * count_y)
+                piece = spectra_ref[place * cells_x : (place + 1) * cells_x, :]
+                block.append(piece * keep if part else piece)
+        blocks.append(jnp.concatenate(block, axis=0))
+    forth = mul(x_in_ref[...], thrice(jnp.concatenate(blocks, axis=1), 0))
+    for quad in range(quads_y):
+        lines_x[quad * 2 * modes_x : (quad + 1) * 2 * modes_x, :] = forth[
+            :, quad * LANES : (quad + 1) * LANES
+        ]
+    devices = count_x * count_y
+    out_chunk = send_ref.shape[0] // devices
     per_own = own_x // SPREAD
-    for quad in range(modes_x // SPREAD):
+    quads_x = modes_x // SPREAD
+    for quad in range(quads_x):
         for part in range(2):
             pieces = [
                 lines_x[
@@ -651,63 +759,49 @@
                 for j in range(SPREAD)
             ]
             for index, piece in enumerate(swap_groups(pieces)):
-                lines_y[pl.ds(part * total_y + index, quads_y, stride=SPREAD), :] = piece
-        modes = mul(y_in_ref[...], thrice(lines_y[...], 0))
+                lines_y[quad, pl.ds(part * total_y + index, quads_y, stride=SPREAD), :] = piece
+    lines = jnp.concatenate([lines_y[quad] for quad in range(quads_x)], axis=1)
+    modes = mul(y_in_ref[...], thrice(lines, 0))
+    for quad in range(quads_x):
         for part in range(2):
             for index in range(count_y):
                 device = (quad // per_own) * count_y + index
                 place = device * out_chunk + (part * per_own + quad % per_own) * own_y
                 first = part * modes_y + index * own_y
-                send_ref[place : place + own_y, :] = modes[first : first + own_y]
+                send_ref[place : place + own_y, :] = modes[
+                    first : first + own_y, quad * LANES : (quad + 1) * LANES
+                ]
     extra = 2 * per_own * own_y
-    totals = []
+    send_ref[pl.ds(extra, devices, stride=out_chunk), :] = modes_ref[...]
+    groups = group_of((1, LANES))
+    total = jnp.zeros((1, LANES), jnp.float32)
     for index in range(3):
         start = chunk // 2 + index
         line = jnp.sum(
-            spectra_ref[pl.ds(start, count_x * count_y, stride=chunk), :], axis=0, keepdims=True
+            spectra_ref[pl.ds(start, devices, stride=chunk), :], axis=0, keepdims=True
         )
         line = line + turn(line, 2 * WIDTH)
-        totals.append(line + turn(line, WIDTH))
-    totals.append(jnp.zeros_like(totals[0]))
-    totals = jnp.concatenate(totals, axis=0)
-    for index_x in range(count_x):
-        for index_y in range(count_y):
-            place = (index_x * count_y + index_y) * out_chunk + extra
-            send_ref[place : place + own_y, :] = modes_ref[
-                index_y * own_y : (index_y + 1) * own_y, :
-            ]
-            send_ref[place + own_y : place + own_y + 4, :] = totals
-
-
-def outer_kernel(scale, modes_x, modes_ref, lift_ref, grad_ref, local_ref, proj_ref, mix_ref):
-    _, planes, own_y, modes_z, width = grad_ref.shape
-    own_x = pl.num_programs(0) * planes
-    step = pl.program_id(0)
+        total = jnp.where(groups == index, line + turn(line, WIDTH), total)
+    send_ref[pl.ds(extra + 1, devices, stride=out_chunk), :] = jnp.broadcast_to(
+        total, (devices, LANES)
+    )
+
+
+def outer_kernel(scale, modes_ref, lift_ref, local_ref, proj_ref, grad_ref, mix_ref, held, sent):
+    _, own_x, own_y, modes_z, width = held.shape
     chunk = modes_ref.shape[0] // modes_z
     per_own = own_x // SPREAD
     extra = 2 * per_own * own_y
-
-    @pl.when(step == 0)
-    def _():
-        shape = (2 * WIDTH, width)
-        row = lax.broadcasted_iota(jnp.int32, shape, 0)
-        column = lax.broadcasted_iota(jnp.int32, shape, 1)
-        lift = jnp.where(row < WIDTH, lift_ref[0:1, :], lift_ref[1:2, :])
-        head, rest = parts_of(jnp.where(column // WIDTH == row % WIDTH, lift, 0.0))
-        mix_ref[0 : 2 * WIDTH] = head
-        mix_ref[2 * WIDTH : 4 * WIDTH] = head
-        mix_ref[4 * WIDTH : 6 * WIDTH] = rest
-        mix_ref[6 * WIDTH : 8 * WIDTH] = jnp.zeros_like(rest)
-        sums = modes_ref[extra : extra + 8, :]
-        turned = sums.T[0:WIDTH]
-        local_ref[...] = scale * (
-            turned[:, own_y : own_y + 1] * lift_ref[0:1, 0:WIDTH]
-            + turned[:, own_y + 1 : own_y + 2] * lift_ref[1:2, 0:WIDTH]
-        )
-        proj_ref[...] = scale * sums[own_y + 2 : own_y + 3, 0:WIDTH]
-
+    shape = (2 * WIDTH, width)
+    row = lax.broadcasted_iota(jnp.int32, shape, 0)
+    column = lax.broadcasted_iota(jnp.int32, shape, 1)
+    lift = jnp.where(row < WIDTH, lift_ref[0:1, :], lift_ref[1:2, :])
+    head, rest = parts_of(jnp.where(column // WIDTH == row % WIDTH, lift, 0.0))
+    mix_ref[0 : 2 * WIDTH] = head
+    mix_ref[2 * WIDTH : 4 * WIDTH] = head
+    mix_ref[4 * WIDTH : 6 * WIDTH] = rest
+    mix_ref[6 * WIDTH : 8 * WIDTH] = jnp.zeros_like(rest)
     lane = lax.broadcasted_iota(jnp.int32, (modes_z, LANES), 1)
-    even = lane % (2 * WIDTH) < WIDTH
     low = lane < 2 * WIDTH
 
     def rows_of(values):
@@ -715,30 +809,55 @@
         both = jnp.where(low, head.astype(jnp.float32), rest.astype(jnp.float32)).astype(NARROW)
         return jnp.concatenate([both, head], axis=1)
 
-    for plane in range(planes):
-        freq = step * planes + plane
+    grads = jnp.concatenate(
+        [modes_ref[pl.ds(place, modes_z, stride=chunk), :] for place in range(extra)], axis=0
+    )
+    repeat = lax.broadcasted_iota(jnp.int32, (2 * LANES, SPREAD * LANES), 0) % LANES
+    column = lax.broadcasted_iota(jnp.int32, (2 * LANES, SPREAD * LANES), 1)
+    repeat = one_where(repeat == column // LANES * WIDTH + column % WIDTH)
+    grads = mul(jnp.concatenate(parts_of(grads), axis=1), repeat)
+    modes = modes_ref[pl.ds(extra, modes_z, stride=chunk), :]
+    place = lax.broadcasted_iota(jnp.int32, (2 * LANES, 2 * LANES), 0) % LANES // own_x % 4
+    column = lax.broadcasted_iota(jnp.int32, (2 * LANES, 2 * LANES), 1) // WIDTH
+    spread = one_where(place == column // 4 * 2 + column % 2)
+    own = lane // (4 * own_x) * own_x + lane % own_x
+    copies = []
+    for plane in range(own_x):
+        chosen = jnp.concatenate(
+            [jnp.where(own == row * own_x + plane, modes, 0.0) for row in range(own_y)], axis=0
+        )
+        columns = mul(jnp.concatenate(parts_of(chosen), axis=1), spread)
         reals, imags = [], []
         for row in range(own_y):
-            modes = modes_ref[pl.ds(extra + row, modes_z, stride=chunk), :]
-            modes = pltpu.roll(modes, LANES - (lax.axis_index("gx") * own_x + freq), 1)
-            columns = [
-                jnp.broadcast_to(modes[:, k * modes_x : k * modes_x + 1], (modes_z, LANES))
-                for k in range(4)
-            ]
-            real = jnp.where(even, columns[0], columns[1])
-            imag = jnp.where(even, columns[2], columns[3])
-            grads = []
+            real = columns[row * modes_z : (row + 1) * modes_z, 0:LANES]
+            imag = columns[row * modes_z : (row + 1) * modes_z, LANES:]
+            pair = []
             for part in range(2):
-                place = (part * per_own + freq // SPREAD) * own_y + row
-                grad = modes_ref[pl.ds(place, modes_z, stride=chunk), :]
-                grad = pltpu.roll(grad, (LANES - WIDTH * (freq % SPREAD)) % LANES, 1)
-                grad = jnp.where(lane < WIDTH, grad, 0.0)
-                grad = grad + turn(grad, WIDTH)
-                grads.append(grad + turn(grad, 2 * WIDTH))
-            reals.append(rows_of(grads[0] * real + grads[1] * imag))
-            imags.append(rows_of(grads[1] * real - grads[0] * imag))
+                first = ((part * per_own + plane // SPREAD) * own_y + row) * modes_z
+                group = plane % SPREAD * LANES
+                pair.append(grads[first : first + modes_z, group : group + LANES])
+            reals.append(rows_of(pair[0] * real + pair[1] * imag))
+            imags.append(rows_of(pair[1] * real - pair[0] * imag))
         result = mul(jnp.concatenate(reals + imags, axis=0), mix_ref[...])
-        grad_ref[:, plane] = result.reshape(2, own_y, modes_z, width)
+        held[:, plane] = result.reshape(2, own_y, modes_z, width)
+        copies.append(
+            pltpu.make_async_copy(held.at[:, plane], grad_ref.at[:, plane], sent.at[plane])
+        )
+        copies[-1].start()
+    line = modes_ref[extra + 1 : extra + 2, :]
+    square = (WIDTH, WIDTH)
+    diagonal = lax.broadcasted_iota(jnp.int32, square, 0) == lax.broadcasted_iota(
+        jnp.int32, square, 1
+    )
+    local = jnp.zeros(square, jnp.float32)
+    for k in range(2):
+        sums = jnp.broadcast_to(line[:, k * WIDTH : (k + 1) * WIDTH], square)
+        sums = jnp.sum(jnp.where(diagonal, sums, 0.0), axis=1, keepdims=True)
+        local = local + sums * lift_ref[k : k + 1, 0:WIDTH]
+    local_ref[...] = scale * local
+    proj_ref[...] = scale * line[:, 2 * WIDTH : 3 * WIDTH]
+    for copy in copies:
+        copy.wait()
 
 
 def tables(shape, depth, modes_z):
@@ -748,20 +867,21 @@
     theta_z = angles(np.arange(modes_z), np.arange(depth), depth)
     theta_x = angles(signed(modes_x), np.arange(total_x), total_x)
     theta_y = angles(signed(modes_y), np.arange(total_y), total_y)
-    forth_z = np.stack([np.cos(theta_z), -np.sin(theta_z)], axis=1).reshape(2 * modes_z, depth)
+    plain_z = np.concatenate([np.cos(theta_z), -np.sin(theta_z)], axis=0)
+    forth_z = plain_z.reshape(2, modes_z, depth).transpose(1, 0, 2).reshape(2 * modes_z, depth)
     weight = np.where(np.arange(modes_z) == 0, 1.0, 2.0) / (total_x * total_y * depth)
     weighted_z = np.repeat(weight, 2)[:, None] * forth_z
     forth_x, back_x = rotation(theta_x, -1.0), rotation(theta_x.T, 1.0)
     forth_y, back_y = rotation(theta_y, -1.0), rotation(theta_y.T, 1.0)
     order_y = forth_y.reshape(2 * modes_y, 2, count_y, cells_y)
-    order_y = order_y.transpose(0, 3, 2, 1).reshape(2 * modes_y, 2 * total_y)
+    order_y = order_y.transpose(0, 3, 1, 2).reshape(2 * modes_y, 2 * total_y)
     lines = forth_x.reshape(2, modes_x, 2, count_x, cells_x)
     both = np.zeros((2, count_x, 2, cells_x, 2, 2, modes_x))
     for field in range(2):
         both[:, :, field, :, :, field, :] = lines.transpose(2, 3, 4, 0, 1)
     both = both.reshape(4 * total_x, 4 * modes_x)
     return {
-        "z_plain": left_table(forth_z),
+        "z_plain": left_table(plain_z),
         "z_forth": left_table(weighted_z),
         "z_back": left_table(weighted_z.T),
         "y_first": left_table(order_y),
@@ -785,17 +905,19 @@
         and cells_x == 8
         and cells_y % SPREAD == 0
         and own_x % SPREAD == 0
-        and own_y == 4
+        and own_y * 4 * own_x == LANES
+        and 3 * WIDTH <= LANES
+        and cells_y == 8
         and depth % LANES == 0
     )
 
 
-def call(kernel, outs, scratch, flops, moved, **more):
+def call(kernel, outs, scratch, flops, moved, limit=SMALL_VMEM, **more):
     return pl.pallas_call(
         kernel,
         out_shape=outs,
         scratch_shapes=scratch,
-        compiler_params=pltpu.CompilerParams(vmem_limit_bytes=32 * 1024 * 1024),
+        compiler_params=pltpu.CompilerParams(vmem_limit_bytes=limit),
         cost_estimate=pl.CostEstimate(flops=flops, bytes_accessed=moved, transcendentals=0),
         **more,
     )
@@ -830,58 +952,62 @@
     def like(*dims):
         return jax.ShapeDtypeStruct(dims, real)
 
-    planes = 2
-    mixed_weights = call(
-        contract_kernel,
-        like(modes_z * own_x * own_y, LANES),
-        [pltpu.VMEM((width, LANES), NARROW)],
-        8 * own_x * own_y * modes_z * width * LANES,
-        8 * own_x * own_y * modes_z * width,
-        grid=(own_x // planes,),
-        in_specs=[
-            pl.BlockSpec((2, planes, own_y, modes_z, width), lambda i: (0, i, 0, 0, 0)),
-            pl.BlockSpec(lift_weight.shape, lambda i: (0, 0)),
-        ],
-        out_specs=pl.BlockSpec((modes_z * own_x * own_y, LANES), lambda i: (0, 0)),
-    )(spectral_weight, lift_weight)
+    far = pl.BlockSpec(memory_space=pltpu.HBM)
+    near = pl.BlockSpec(memory_space=pltpu.VMEM)
+    weight_bytes = 8 * own_x * own_y * modes_z * width
+    head = jnp.concatenate([phase[:2], solute[:2], undercool[:1]])
+    tail = jnp.concatenate([phase[-2:], solute[-2:], undercool[-1:]])
+    held = jnp.stack([phase, solute, undercool])
 
     def ring(values, axis, step):
         count = lax.axis_size(axis)
         return lax.ppermute(values, axis, [(i, (i + step) % count) for i in range(count)])
 
-    head = jnp.concatenate([phase[:2], solute[:2], undercool[:1]])
-    tail = jnp.concatenate([phase[-2:], solute[-2:], undercool[-1:]])
+    head, tail, lift = lax.optimization_barrier((head, tail, lift_weight.T))
     before, after = ring(tail, "gx", 1), ring(head, "gx", -1)
+    planes = 2
+    mixed_weights = call(
+        functools.partial(contract_kernel, planes),
+        like(modes_z * (own_x * own_y + 2), LANES),
+        [
+            pltpu.VMEM(spectral_weight.shape, real),
+            pltpu.SemaphoreType.DMA((own_x // planes,)),
+        ],
+        weight_bytes * LANES,
+        weight_bytes,
+        limit=LARGE_VMEM,
+        in_specs=[near, far],
+    )(lift, spectral_weight)
     head, tail = call(
         pack_kernel,
         (like(cells_x + 2, 8, depth), like(cells_x + 2, 8, depth)),
         [],
-        1000,
-        40 * cells_x * cells_y * depth,
-    )(phase, solute, undercool, before, after)
+        PACK_COST,
+        40 * tile * depth,
+    )(held, before, after)
     low, high = ring(tail, "gy", 1), ring(head, "gy", -1)
     extended_shape = pltpu.VMEM((cells_x + 4, cells_y + 16, depth), real)
     phase_next, solute_next, spectra = call(
         step_kernel,
-        (like(*phase.shape), like(*phase.shape), like(2 * modes_z, LANES)),
+        (like(*phase.shape), like(*phase.shape), like(*mixed_weights.shape)),
         [extended_shape] * 4 + [pltpu.VMEM((depth // LANES, 2 * tile, LANES), real)],
         400 * tile * depth,
         80 * tile * depth,
-    )(phase, solute, undercool, before, after, low, high, table["z_plain"])
-    gathered_weights = exchange(mixed_weights)
-    gathered = exchange(spectra)
+    )(held, before, after, low, high, table["z_plain"], mixed_weights)
+    gathered = exchange(spectra.reshape(-1, 2, LANES)).reshape(spectra.shape)
     modes, fields = call(
         functools.partial(spectral_kernel, shape),
-        (like(modes_y, LANES), like(devices * 2 * cells_x * (cells_y // SPREAD), LANES)),
+        (like(devices, LANES), like(devices * 2 * cells_x * (cells_y // SPREAD), LANES)),
         [
-            pltpu.VMEM((2 * total_y, LANES), real),
+            pltpu.VMEM((modes_x // SPREAD, 2 * total_y, LANES), real),
             pltpu.VMEM((2 * modes_x * (total_y // SPREAD), LANES), real),
+            pltpu.VMEM((count_x, modes_y, LANES), real),
+            pltpu.VMEM((devices * own_x * own_y, LANES), real),
         ],
         100_000_000,
         2_000_000,
     )(
         gathered,
-        gathered_weights,
         table["y_first"],
         table["x_first"],
         table["y_back"],
@@ -892,51 +1018,55 @@
     vectors = jnp.tile(
         jnp.stack([mixed[:, 0], mixed[:, 1], local_bias, proj_weight]), (1, cells_y)
     )
-    predicted, spectra = call(
-        functools.partial(field_kernel, (cells_x, cells_y, modes_z)),
-        (like(tile, depth), like(*fields.shape)),
-        [pltpu.VMEM((3, depth, 2 * tile), NARROW)],
-        1_000_000_000,
-        2_000_000,
+    spread_shape = (cells_x, depth, cells_y * WIDTH)
+    base, spread, lines = call(
+        prepare_kernel,
+        (
+            like(*spread_shape),
+            jax.ShapeDtypeStruct((depth, 2 * tile), NARROW),
+            jax.ShapeDtypeStruct((cells_x, 2 * cells_y, 3 * depth), NARROW),
+        ),
+        [],
+        100_000_000,
+        5_000_000,
     )(
-        fields,
         phase_next.reshape(tile, depth),
         solute_next.reshape(tile, depth),
         cotangent.reshape(tile, depth),
         vectors,
-        table["z_back"],
-        table["z_forth"],
-    )
+    )
+    predicted, spectra = call(
+        functools.partial(field_kernel, cells_y),
+        (like(tile, depth), like(*fields.shape)),
+        [],
+        1_000_000_000,
+        2_000_000,
+    )(fields, base, spread, lines, vectors, table["z_back"], table["z_forth"])
     spectra = exchange(spectra)
-    chunk = 2 * own_x * own_y * WIDTH // LANES + 8
+    chunk = 2 * own_x * own_y * WIDTH // LANES + 2
     gradients = call(
         functools.partial(gradient_kernel, shape),
         like(devices * chunk, LANES),
         [
             pltpu.VMEM((2 * modes_x * (total_y // SPREAD), LANES), real),
-            pltpu.VMEM((2 * total_y, LANES), real),
+            pltpu.VMEM((modes_x // SPREAD, 2 * total_y, LANES), real),
         ],
         100_000_000,
         2_000_000,
     )(spectra, modes, table["x_forth"], table["y_forth"])
-    gradients = exchange(gradients)
-    planes = 1
-    grad_spectral, grad_local, grad_proj = call(
-        functools.partial(outer_kernel, 1.0 / math.sqrt(total_x * total_y * depth), modes_x),
-        (like(*spectral_weight.shape), like(WIDTH, WIDTH), like(1, WIDTH)),
-        [pltpu.VMEM((8 * WIDTH, width), NARROW)],
-        4 * own_x * own_y * modes_z * width * 8 * WIDTH,
-        8 * own_x * own_y * modes_z * width,
-        grid=(own_x // planes,),
-        in_specs=[
-            pl.BlockSpec(gradients.shape, lambda i: (0, 0)),
-            pl.BlockSpec((2, width), lambda i: (0, 0)),
+    gradients = exchange(gradients.reshape(-1, 2, LANES)).reshape(gradients.shape)
+    grad_local, grad_proj, grad_spectral = call(
+        functools.partial(outer_kernel, 1.0 / math.sqrt(total_x * total_y * depth)),
+        (like(WIDTH, WIDTH), like(1, WIDTH), like(*spectral_weight.shape)),
+        [
+            pltpu.VMEM((8 * WIDTH, width), NARROW),
+            pltpu.VMEM(spectral_weight.shape, real),
+            pltpu.SemaphoreType.DMA((own_x,)),
         ],
-        out_specs=(
-            pl.BlockSpec((2, planes, own_y, modes_z, width), lambda i: (0, i, 0, 0, 0)),
-            pl.BlockSpec((WIDTH, WIDTH), lambda i: (0, 0)),
-            pl.BlockSpec((1, WIDTH), lambda i: (0, 0)),
-        ),
+        weight_bytes * 4 * WIDTH,
+        weight_bytes,
+        limit=SMALL_VMEM,
+        out_specs=(near, near, far),
     )(gradients, jnp.tile(lift_weight.T, (1, WIDTH)))
     return (
         phase_next,

time: 133 us -> 107 us (0.80)
  waiting for transfers between devices: 34.3 us -> 25.7 us
  local copies, waits for them, and re-layouts: 11.9 us -> 5.2 us
  starting transfers between devices: 18.2 us -> 12.9 us
  Pallas kernels: 26.5 us -> 22.4 us
  blocking collectives: 40.3 us -> 38.4 us
    unnamed x47 -> x34, local copies, waits for them, and re-layouts: 10.1 us -> 2.83 us
    all_to_all x3 -> x2, starting transfers between devices: 10.5 us -> 5.19 us  [exchange(): lax.all_to_all(values, ('gx', 'gy'), split_axis=0, concat_axis=0, tiled=T...]
    all_to_all x3 -> x2, waiting for transfers between devices: 29.5 us -> 24.7 us  [exchange(): lax.all_to_all(values, ('gx', 'gy'), split_axis=0, concat_axis=0, tiled=T...]
    ppermute x4, waiting for transfers between devices: 4.77 us -> 0.97 us  [ring(): lax.ppermute(values, axis, [(i, (i + step) % count) for i in range(count)])]
    pallas_call x1, Pallas kernels: 6.88 us -> 4.56 us  [per_device_fast(): call(functools.partial(outer_kernel, 1.0 / math.sqrt(total_x * total_y *...]
    all_to_all x2, blocking collectives: 40.3 us -> 38.4 us  [exchange(): lax.all_to_all(values, ('gx', 'gy'), split_axis=0, concat_axis=0, tiled=T...]
    pallas_call x4 -> x5, Pallas kernels: 17.8 us -> 16.2 us  [the longest x1 6.24 us: per_device_fast(): call(functools.partial(contract_kernel, planes), like(modes_z * (own_x *...]
  transfers between devices with their start and end apart: 7 -> 6, of which waited for: 6 -> 4; matrix products, arithmetic and copies ran while one was open for 1% -> 1% of each run, Pallas kernels for 3% -> 7%
where the time goes in v2:
time: 107 us
  blocking collectives  38.4 us (36%)
  waiting for transfers between devices  25.7 us (24%)
  Pallas kernels  22.4 us (21%)
  starting transfers between devices  12.9 us (12%)
  local copies, waits for them, and re-layouts  5.2 us (5%)
    all_to_all x2, blocking collectives, exchange(): lax.all_to_all(values, ('gx', 'gy'), split_axis=0, concat_axis=0, tiled=T...  38.4 us
    all_to_all x2, waiting for transfers between devices, exchange(): lax.all_to_all(values, ('gx', 'gy'), split_axis=0, concat_axis=0, tiled=T...  24.7 us
    ppermute x4, starting transfers between devices, ring(): lax.ppermute(values, axis, [(i, (i + step) % count) for i in range(count)])  7.72 us
    pallas_call x1, Pallas kernels, per_device_fast(): call(functools.partial(contract_kernel, planes), like(modes_z * (own_x *...  6.24 us
    all_to_all x2, starting transfers between devices, exchange(): lax.all_to_all(values, ('gx', 'gy'), split_axis=0, concat_axis=0, tiled=T...  5.19 us
    pallas_call x1, Pallas kernels, per_device_fast(): call(functools.partial(outer_kernel, 1.0 / math.sqrt(total_x * total_y *...  4.56 us
    pallas_call x1, Pallas kernels, per_device_fast(): call(functools.partial(field_kernel, cells_y), (like(tile, depth), like(*...  4.12 us
    pallas_call x1, Pallas kernels, per_device_fast(): call(functools.partial(spectral_kernel, shape), (like(devices, LANES), li...  3.07 us
  transfers between devices with their start and end apart: 6, of which 4 were waited for; matrix products, arithmetic and copies ran while one was open for 1% of the time, Pallas kernels for 7%

profile of v2, /device:TPU:0, one launch (start us, length us, event | category | flops | bytes accessed | tf_op | source)
XLA Modules:
  0.0 106.6 jit_solution(15280878065209409806)
XLA Ops:
  0.6 0.0 copy-start
  0.6 0.7 fusion.2
  1.4 0.7 fusion
  2.1 0.7 fusion.1
  2.9 0.5 collective-permute-start
  3.4 2.0 %collective-permute-start.1 = (f32[5,8,256]{2,1,0:T(8,128)S(1)}, f32[5,8,256]{2,1,0:T(8,128)S(1)}, u32[]{:S(2)}, u32[]{:S(2)}) collective-permute-start(f32[5,8,256]{2,1,0:T(8,128)S(1)} %get-tuple-element.25), channel_id=1, source_target_pairs={{0,24},{8,0},{16,8},{24,16},{1,25},{9,1},{17,9},{25,17},{2,26},{10... | collective-permute-start | bytes 122888 | tf_op jit(solution)/shard_map/ppermute | solution.py:964
  5.4 0.9 pad_maximum_fusion.held_ref
  6.3 0.7 collective-permute-done.before_ref
  7.0 0.3 collective-permute-done.1.after_ref
  7.3 0.0 copy-start.3
  7.3 0.0 copy-start.2
  7.3 0.0 copy-start.4
  7.3 0.0 copy-start.6
  7.3 0.0 copy-start.8
  7.4 0.0 copy-start.14
  7.4 0.0 copy-start.15
  7.4 0.0 copy-start.16
  7.4 0.0 copy-start.9
  7.4 0.0 copy-start.12
  7.4 0.0 copy-start.13
  7.4 2.1 %collective-permute-start.2 = (f32[10,8,256]{2,1,0:T(8,128)S(1)}, f32[10,8,256]{2,1,0:T(8,128)S(1)}, u32[]{:S(2)}, u32[]{:S(2)}) collective-permute-start(f32[10,8,256]{2,1,0:T(8,128)S(1)} %get-tuple-element.26), channel_id=1, source_target_pairs={{0,1},{1,2},{2,3},{3,4},{4,5},{5,6},{6,7},{7,0},{8,9},{9,10},{10,1... | collective-permute-start | bytes 245768 | tf_op jit(solution)/shard_map/ppermute | solution.py:964
  9.5 3.1 %collective-permute-start.3 = (f32[10,8,256]{2,1,0:T(8,128)S(1)}, f32[10,8,256]{2,1,0:T(8,128)S(1)}, u32[]{:S(2)}, u32[]{:S(2)}) collective-permute-start(f32[10,8,256]{2,1,0:T(8,128)S(1)} %get-tuple-element.27), channel_id=1, source_target_pairs={{0,7},{1,0},{2,1},{3,2},{4,3},{5,4},{6,5},{7,6},{8,15},{9,8},{10,9... | collective-permute-start | bytes 245768 | tf_op jit(solution)/shard_map/ppermute | solution.py:964
  12.6 6.2 %shard_map.218.mixed_ref = f32[1088,128]{1,0:T(8,128)} custom-call(f32[2,32]{1,0:T(2,128)} %bitcast.37, f32[2,8,4,32,1024]{4,3,2,1,0:T(8,128)} %weight_ref.1), custom_call_target="tpu_custom_call" | custom-call | flops 1073741824 | bytes 8388608 | tf_op jit(solution)/shard_map/pallas_call | solution.py:969
  18.9 0.0 collective-permute-done.2.low_ref
  18.9 0.0 collective-permute-done.3.high_ref
  18.9 0.0 copy-start.1
  18.9 1.0 copy-done.1
  20.0 1.8 %shard_map.219 = (f32[8,8,256]{2,1,0:T(8,128)}, f32[8,8,256]{2,1,0:T(8,128)}, f32[1088,128]{1,0:T(8,128)S(1)}) custom-call(f32[3,8,8,256]{3,2,1,0:T(8,128)S(1)} %pad_maximum_fusion.held_ref, f32[5,8,256]{2,1,0:T(8,128)S(1)} %collective-permute-done.before_ref, f32[5,8,256]{2,1,0:T(8,128)S(1)} %collective-permute-done.1.after_ref, ...), custom_call_target="tpu_custom_call" | custom-call | flops 6553600 | bytes 1310720 | tf_op jit(solution)/shard_map/pallas_call | solution.py:990
  21.8 20.1 %all_to_all.32 = f32[544,2,128]{2,1,0:T(2,128)S(1)} all-to-all(f32[544,2,128]{2,1,0:T(2,128)S(1)} %bitcast.27), channel_id=1, replica_groups=mesh['gx'=4,'gy'=8] {'gx','gy'}, dimensions={0} | all-to-all | bytes 1114112 | tf_op jit(solution)/shard_map/all_to_all | solution.py:927
  41.9 0.0 copy-done.2
  41.9 3.1 %shard_map.220 = (f32[32,128]{1,0:T(8,128)S(1)}, f32[1024,128]{1,0:T(8,128)}) custom-call(f32[1088,128]{1,0:T(8,128)S(1)} %bitcast.25, bf16[64,384]{1,0:T(8,128)(2,1)S(1)} %copy-done.6, bf16[384,128]{1,0:T(8,128)(2,1)S(1)} %copy-done.2, bf16[128,192]{1,0:T(8,128)(2,1)S(1)} %copy-done.4, bf16[64,192]{1,0:T(8,128)(2,1)S(1)} %copy-done.8), custom_call_target="tpu_custom_call" | custom-call | flops 100000000 | bytes 2000000 | tf_op jit(solution)/shard_map/pallas_call | solution.py:998
  45.0 2.6 %all-to-all-start.1 = ((f32[32,32,128]{2,1,0:T(8,128)}), f32[32,32,128]{2,1,0:T(8,128)S(1)}, u32[]{:S(2)}, u32[]{:S(2)}) async-start(f32[32,32,128]{2,1,0:T(8,128)} %bitcast.6), calls=%async_computation.1 | async-start | bytes 1048576 | tf_op jit(solution)/shard_map/all_to_all | solution.py:927
  47.6 0.1 fusion.3
  47.8 0.0 copy-done.15
  47.8 0.1 tile.9.vector_ref
  47.9 0.8 copy-done.10
  48.7 0.8 copy-done.11
  49.6 1.0 shard_map.221
  50.6 13.4 %all-to-all-done.1 = f32[32,32,128]{2,1,0:T(8,128)S(1)} async-done(((f32[32,32,128]{2,1,0:T(8,128)}), f32[32,32,128]{2,1,0:T(8,128)S(1)}, u32[]{:S(2)}, u32[]{:S(2)}) %all-to-all-start.1) | async-done | bytes 524320 | tf_op jit(solution)/shard_map/all_to_all | solution.py:927
  63.9 0.0 copy-done.12
  64.0 4.1 %shard_map.222 = (f32[64,256]{1,0:T(8,128)}, f32[1024,128]{1,0:T(8,128)S(1)}) custom-call(f32[1024,128]{1,0:T(8,128)S(1)} %bitcast.28, f32[8,256,256]{2,1,0:T(8,128)S(1)} %get-tuple-element.33.base_ref, bf16[256,128]{1,0:T(8,128)(2,1)S(1)} %get-tuple-element.34.spread_ref, bf16[8,16,768]{2,1,0:T(8,128)(2,1)S(1)} %get-tuple-element.35.table_ref, ...), custom_call_target="tpu_custom_call" | custom-call | flops 1000000000 | bytes 2000000 | tf_op jit(solution)/shard_map/pallas_call | solution.py:1038
  68.1 18.3 %all_to_all.33 = f32[32,32,128]{2,1,0:T(8,128)S(1)} all-to-all(f32[32,32,128]{2,1,0:T(8,128)S(1)} %bitcast.29), channel_id=1, replica_groups=mesh['gx'=4,'gy'=8] {'gx','gy'}, dimensions={0} | all-to-all | bytes 1048576 | tf_op jit(solution)/shard_map/all_to_all | solution.py:927
  86.4 0.0 copy-done.5
  86.4 1.6 %shard_map.223 = f32[576,128]{1,0:T(8,128)} custom-call(f32[1024,128]{1,0:T(8,128)S(1)} %bitcast.26, f32[32,128]{1,0:T(8,128)S(1)} %get-tuple-element.38.modes_ref, bf16[64,192]{1,0:T(8,128)(2,1)S(1)} %copy-done.7, bf16[64,384]{1,0:T(8,128)(2,1)S(1)} %copy-done.5), custom_call_target="tpu_custom_call" | custom-call | flops 100000000 | bytes 2000000 | tf_op jit(solution)/shard_map/pallas_call | solution.py:1047
  88.0 2.6 %all-to-all-start.3 = ((f32[288,2,128]{2,1,0:T(2,128)}), f32[288,2,128]{2,1,0:T(2,128)S(1)}, u32[]{:S(2)}, u32[]{:S(2)}) async-start(f32[288,2,128]{2,1,0:T(2,128)} %bitcast.18), calls=%async_computation.3 | async-start | bytes 589824 | tf_op jit(solution)/shard_map/all_to_all | solution.py:927
  90.6 0.1 tile.21.lift_ref
  90.7 11.3 %all-to-all-done.3 = f32[288,2,128]{2,1,0:T(2,128)S(1)} async-done(((f32[288,2,128]{2,1,0:T(2,128)}), f32[288,2,128]{2,1,0:T(2,128)S(1)}, u32[]{:S(2)}, u32[]{:S(2)}) %all-to-all-start.3) | async-done | bytes 294944 | tf_op jit(solution)/shard_map/all_to_all | solution.py:927
  102.1 4.6 %shard_map.224 = (f32[32,32]{1,0:T(8,128)}, f32[1,32]{1,0:T(1,128)}, f32[2,8,4,32,1024]{4,3,2,1,0:T(8,128)}) custom-call(f32[576,128]{1,0:T(8,128)S(1)} %bitcast.30, f32[2,1024]{1,0:T(2,128)S(1)} %tile.21.lift_ref), custom_call_target="tpu_custom_call" | custom-call | flops 1073741824 | bytes 8388608 | tf_op jit(solution)/shard_map/pallas_call | solution.py:1058
  (20 shorter events, 0.1 us)
Async XLA Ops:
  0.6 47.0 %copy-start = (f32[32,32]{1,0:T(8,128)S(1)}, f32[32,32]{1,0:T(8,128)}, u32[]{:S(2)}) copy-start(f32[32,32]{1,0:T(8,128)} %param.23) | copy-start | bytes 12292
  2.9 4.1 %collective-permute-start = (f32[5,8,256]{2,1,0:T(8,128)S(1)}, f32[5,8,256]{2,1,0:T(8,128)S(1)}, u32[]{:S(2)}, u32[]{:S(2)}) collective-permute-start(f32[5,8,256]{2,1,0:T(8,128)S(1)} %get-tuple-element.24), channel_id=1, source_target_pairs={{0,8},{8,16},{16,24},{24,0},{1,9},{9,17},{17,25},{25,1},{2,10},{10... | collective-permute-start | bytes 122888 | tf_op jit(solution)/shard_map/ppermute | solution.py:964
  3.4 3.9 %collective-permute-start.1 = (f32[5,8,256]{2,1,0:T(8,128)S(1)}, f32[5,8,256]{2,1,0:T(8,128)S(1)}, u32[]{:S(2)}, u32[]{:S(2)}) collective-permute-start(f32[5,8,256]{2,1,0:T(8,128)S(1)} %get-tuple-element.25), channel_id=1, source_target_pairs={{0,24},{8,0},{16,8},{24,16},{1,25},{9,1},{17,9},{25,17},{2,26},{10... | collective-permute-start | bytes 122888 | tf_op jit(solution)/shard_map/ppermute | solution.py:964
  7.3 11.6 %copy-start.3 = (bf16[64,768]{1,0:T(8,128)(2,1)S(1)}, bf16[64,768]{1,0:T(8,128)(2,1)}, u32[]{:S(2)}) copy-start(bf16[64,768]{1,0:T(8,128)(2,1)} %constant.18.clone.table_ref) | copy-start | bytes 294916
  7.3 34.6 %copy-start.2 = (bf16[384,128]{1,0:T(8,128)(2,1)S(1)}, bf16[384,128]{1,0:T(8,128)(2,1)}, u32[]{:S(2)}) copy-start(bf16[384,128]{1,0:T(8,128)(2,1)} %constant.20.clone.x_in_ref) | copy-start | bytes 294916
  7.3 34.6 %copy-start.4 = (bf16[128,192]{1,0:T(8,128)(2,1)S(1)}, bf16[128,192]{1,0:T(8,128)(2,1)}, u32[]{:S(2)}) copy-start(bf16[128,192]{1,0:T(8,128)(2,1)} %constant.21.clone.y_out_ref) | copy-start | bytes 147460
  7.3 34.6 %copy-start.6 = (bf16[64,384]{1,0:T(8,128)(2,1)S(1)}, bf16[64,384]{1,0:T(8,128)(2,1)}, u32[]{:S(2)}) copy-start(bf16[64,384]{1,0:T(8,128)(2,1)} %constant.19.clone.y_in_ref) | copy-start | bytes 147460
  7.3 34.6 %copy-start.8 = (bf16[64,192]{1,0:T(8,128)(2,1)S(1)}, bf16[64,192]{1,0:T(8,128)(2,1)}, u32[]{:S(2)}) copy-start(bf16[64,192]{1,0:T(8,128)(2,1)} %constant.22.clone.x_out_ref) | copy-start | bytes 73732
  7.4 40.2 %copy-start.14 = (f32[32,2]{0,1:T(2,128)S(1)}, f32[32,2]{0,1:T(2,128)}, u32[]{:S(2)}) copy-start(f32[32,2]{0,1:T(2,128)} %param.21) | copy-start | bytes 772
  7.4 40.4 %copy-start.15 = (f32[32]{0:T(128)S(1)}, f32[32]{0:T(128)}, u32[]{:S(2)}) copy-start(f32[32]{0:T(128)} %param.25) | copy-start | bytes 388
  7.4 40.4 %copy-start.16 = (f32[32]{0:T(128)S(1)}, f32[32]{0:T(128)}, u32[]{:S(2)}) copy-start(f32[32]{0:T(128)} %param.24) | copy-start | bytes 388
  7.4 40.5 %copy-start.9 = (f32[8,8,256]{2,1,0:T(8,128)S(1)}, f32[8,8,256]{2,1,0:T(8,128)}, u32[]{:S(2)}) copy-start(f32[8,8,256]{2,1,0:T(8,128)} %param.26) | copy-start | bytes 196612
  7.4 56.5 %copy-start.12 = (bf16[256,192]{1,0:T(8,128)(2,1)S(1)}, bf16[256,192]{1,0:T(8,128)(2,1)}, u32[]{:S(2)}) copy-start(bf16[256,192]{1,0:T(8,128)(2,1)} %constant.23.clone.back_ref) | copy-start | bytes 294916
  7.4 56.5 %copy-start.13 = (bf16[64,768]{1,0:T(8,128)(2,1)S(1)}, bf16[64,768]{1,0:T(8,128)(2,1)}, u32[]{:S(2)}) copy-start(bf16[64,768]{1,0:T(8,128)(2,1)} %constant.24.clone.forth_ref) | copy-start | bytes 294916
  7.4 11.4 %collective-permute-start.2 = (f32[10,8,256]{2,1,0:T(8,128)S(1)}, f32[10,8,256]{2,1,0:T(8,128)S(1)}, u32[]{:S(2)}, u32[]{:S(2)}) collective-permute-start(f32[10,8,256]{2,1,0:T(8,128)S(1)} %get-tuple-element.26), channel_id=1, source_target_pairs={{0,1},{1,2},{2,3},{3,4},{4,5},{5,6},{6,7},{7,0},{8,9},{9,10},{10,1... | collective-permute-start | bytes 245768 | tf_op jit(solution)/shard_map/ppermute | solution.py:964
  9.5 76.9 %copy-start.5 = (bf16[64,384]{1,0:T(8,128)(2,1)S(1)}, bf16[64,384]{1,0:T(8,128)(2,1)}, u32[]{:S(2)}) copy-start(bf16[64,384]{1,0:T(8,128)(2,1)} %constant.26.clone.y_in_ref) | copy-start | bytes 147460
  9.5 76.9 %copy-start.7 = (bf16[64,192]{1,0:T(8,128)(2,1)S(1)}, bf16[64,192]{1,0:T(8,128)(2,1)}, u32[]{:S(2)}) copy-start(bf16[64,192]{1,0:T(8,128)(2,1)} %constant.25.clone.x_in_ref) | copy-start | bytes 73732
  9.5 9.4 %collective-permute-start.3 = (f32[10,8,256]{2,1,0:T(8,128)S(1)}, f32[10,8,256]{2,1,0:T(8,128)S(1)}, u32[]{:S(2)}, u32[]{:S(2)}) collective-permute-start(f32[10,8,256]{2,1,0:T(8,128)S(1)} %get-tuple-element.27), channel_id=1, source_target_pairs={{0,7},{1,0},{2,1},{3,2},{4,3},{5,4},{6,5},{7,6},{8,15},{9,8},{10,9... | collective-permute-start | bytes 245768 | tf_op jit(solution)/shard_map/ppermute | solution.py:964
  18.9 1.1 copy-start.1
  45.0 19.0 %all-to-all-start.1 = ((f32[32,32,128]{2,1,0:T(8,128)}), f32[32,32,128]{2,1,0:T(8,128)S(1)}, u32[]{:S(2)}, u32[]{:S(2)}) async-start(f32[32,32,128]{2,1,0:T(8,128)} %bitcast.6), calls=%async_computation.1 | async-start | bytes 1048576 | tf_op jit(solution)/shard_map/all_to_all | solution.py:927
  47.9 0.8 copy-start.10
  48.7 0.8 copy-start.11
  88.0 14.0 %all-to-all-start.3 = ((f32[288,2,128]{2,1,0:T(2,128)}), f32[288,2,128]{2,1,0:T(2,128)S(1)}, u32[]{:S(2)}, u32[]{:S(2)}) async-start(f32[288,2,128]{2,1,0:T(2,128)} %bitcast.18), calls=%async_computation.3 | async-start | bytes 589824 | tf_op jit(solution)/shard_map/all_to_all | solution.py:927

commit v3 on v2

--- a/solution.py
+++ b/solution.py
@@ -236,7 +236,7 @@
 
 LANES = 128
 SMALL_VMEM = 24 * 1024 * 1024
-LARGE_VMEM = 56 * 1024 * 1024
+LARGE_VMEM = 50 * 1024 * 1024
 PACK_COST = 50_000_000_000
 SPREAD = LANES // WIDTH
 NARROW = jnp.bfloat16
@@ -377,6 +377,13 @@
                 ]
 
 
+def edge_kernel(held_ref, head_ref, tail_ref):
+    cells_x = held_ref.shape[1]
+    for index, reach in enumerate((2, 2, 1)):
+        head_ref[2 * index : 2 * index + reach] = held_ref[index, 0:reach]
+        tail_ref[2 * index : 2 * index + reach] = held_ref[index, cells_x - reach : cells_x]
+
+
 def pack_kernel(held_ref, before_ref, after_ref, head_ref, tail_ref):
     _, cells_x, cells_y, _ = held_ref.shape
 
@@ -401,8 +408,7 @@
     high_ref,
     table_ref,
     mixed_ref,
-    phase_out,
-    solute_out,
+    fields_ref,
     send_ref,
     phase_ext,
     solute_ext,
@@ -462,8 +468,8 @@
     phase_ext[1 : cells_x + 3, base - 1 : end + 1] = phase_mid
     solute_ext[1 : cells_x + 3, base - 1 : end + 1] = solute_mid
     phase_next, solute_next = sweep(0)
-    phase_out[...] = phase_next
-    solute_out[...] = solute_next
+    fields_ref[0] = phase_next
+    fields_ref[1] = solute_next
     tile = cells_x * cells_y
     both = (phase_next.reshape(tile, depth), solute_next.reshape(tile, depth) - SOLUTE_MEAN)
     ordered = []
@@ -517,8 +523,18 @@
     x_in_ref,
     y_out_ref,
     x_out_ref,
+    fields_ref,
+    cotangent_ref,
+    lift_ref,
+    local_ref,
+    bias_ref,
+    proj_ref,
     modes_ref,
     send_ref,
+    vector_ref,
+    base_ref,
+    spread_ref,
+    table_ref,
     lines_y,
     lines_x,
     rows_ref,
@@ -621,38 +637,70 @@
                     first : first + cells_x, quad * LANES : (quad + 1) * LANES
                 ]
     pack_modes(shape, modes, modes_ref, rows_ref)
-
-
-def prepare_kernel(
-    phase_ref, solute_ref, cotangent_ref, vector_ref, base_ref, spread_ref, table_ref
+    prepare(
+        fields_ref,
+        cotangent_ref,
+        lift_ref,
+        local_ref,
+        bias_ref,
+        proj_ref,
+        vector_ref,
+        base_ref,
+        spread_ref,
+        table_ref,
+    )
+
+
+def prepare(
+    fields_ref,
+    cotangent_ref,
+    lift_ref,
+    local_ref,
+    bias_ref,
+    proj_ref,
+    vector_ref,
+    base_ref,
+    weight_ref,
+    table_ref,
 ):
     planes, depth, wide = base_ref.shape
-    tile = phase_ref.shape[0]
+    tile = cotangent_ref.shape[0]
     cells_y = tile // planes
-    fields = (phase_ref[...], solute_ref[...] - SOLUTE_MEAN)
+    lift, lift_rest = parts_of(lift_ref[...])
+    local, local_rest = parts_of(local_ref[...])
+    mixed = mul_rows(lift, local) + mul_rows(lift_rest, local) + mul_rows(lift, local_rest)
+    for index in range(wide // WIDTH):
+        place = slice(index * WIDTH, (index + 1) * WIDTH)
+        vector_ref[0:2, place] = mixed
+        vector_ref[2:3, place] = bias_ref[...]
+        vector_ref[3:4, place] = proj_ref[...]
+    fields = (
+        fields_ref[0].reshape(tile, depth),
+        fields_ref[1].reshape(tile, depth) - SOLUTE_MEAN,
+        cotangent_ref[...],
+    )
     spread = jnp.concatenate(
         [jnp.concatenate(parts_of(values.T), axis=1) for values in fields], axis=0
     )
-    spread_ref[...] = jnp.concatenate(parts_of(cotangent_ref[...].T), axis=1)
     cell = lax.broadcasted_iota(jnp.int32, (2 * tile, wide), 0) % tile
     row = lax.broadcasted_iota(jnp.int32, (2 * tile, wide), 1) // WIDTH
     for plane in range(planes):
         values = mul(spread, one_where(cell == plane * cells_y + row))
         base_ref[plane] = (
             values[0:depth] * vector_ref[0:1, :]
-            + values[depth:] * vector_ref[1:2, :]
+            + values[depth : 2 * depth] * vector_ref[1:2, :]
             + vector_ref[2:3, :]
         )
-        lines = [values[plane * cells_y : (plane + 1) * cells_y] for values in fields]
-        head, rest = parts_of(jnp.concatenate(lines, axis=0))
-        table_ref[plane] = jnp.concatenate([head, head, rest], axis=1)
+        weight_ref[plane] = values[2 * depth :]
+        lines = [values[plane * cells_y : (plane + 1) * cells_y] for values in fields[:2]]
+        table_ref[plane] = jnp.concatenate(parts_of(jnp.concatenate(lines, axis=0)), axis=0)
 
 
 def field_kernel(
     cells_y,
     field_ref,
     base_ref,
-    spread_ref,
+    weight_ref,
     table_ref,
     vector_ref,
     back_ref,
@@ -671,8 +719,6 @@
         lax.broadcasted_iota(jnp.int32, (cells_y, 2 * wide), 0)
         == lax.broadcasted_iota(jnp.int32, (cells_y, 2 * wide), 1) % wide // WIDTH
     )
-    cell = lax.broadcasted_iota(jnp.int32, (2 * planes * cells_y, wide), 0) % (planes * cells_y)
-    cell = cell - lax.broadcasted_iota(jnp.int32, cell.shape, 1) // WIDTH
     line_sums = jnp.zeros((2 * cells_y, wide), jnp.float32)
     proj_sums = jnp.zeros((8, wide), jnp.float32)
     for plane in range(planes):
@@ -689,14 +735,18 @@
         upper = 0.5 + 0.5 * bent
         active = pre * upper
         slope = upper + (active - active * bent) * (root + (3.0 * root * curve) * square)
-        cotangent = mul(spread_ref[...], one_where(cell == plane * cells_y))
+        cotangent = weight_ref[plane]
         weighted = proj * cotangent
         grad = weighted * slope
         predicted_ref[plane * cells_y : (plane + 1) * cells_y, :] = mul_rows(
             picker, jnp.concatenate(parts_of(proj * active), axis=1)
         )
-        table = jnp.concatenate([forth_ref[...], table_ref[plane]], axis=0)
-        spectra = mul(table, thrice(grad, 0))
+        head, rest = parts_of(grad)
+        lines = table_ref[plane]
+        top = jnp.concatenate([forth_ref[0:rows], lines[0 : 2 * cells_y]], axis=0)
+        low = jnp.concatenate([forth_ref[rows:], lines[2 * cells_y :]], axis=0)
+        spectra = mul(jnp.concatenate([top, low], axis=0), head)
+        spectra = spectra[0 : rows + 2 * cells_y] + spectra[rows + 2 * cells_y :] + mul(top, rest)
         for part in range(halves_y):
             send_ref[pl.ds(part * planes + plane, rows, stride=stride), :] = spectra[
                 0:rows, part * LANES : (part + 1) * LANES
@@ -787,11 +837,40 @@
     )
 
 
-def outer_kernel(scale, modes_ref, lift_ref, local_ref, proj_ref, grad_ref, mix_ref, held, sent):
+def outer_kernel(
+    scale,
+    modes_ref,
+    narrow_ref,
+    predicted_ref,
+    fields_ref,
+    local_out,
+    proj_out,
+    predicted_out,
+    phase_out,
+    solute_out,
+    grad_ref,
+    mix_ref,
+    local_ref,
+    proj_ref,
+    lift_ref,
+    held,
+    sent,
+):
     _, own_x, own_y, modes_z, width = held.shape
     chunk = modes_ref.shape[0] // modes_z
     per_own = own_x // SPREAD
     extra = 2 * per_own * own_y
+    copies = [
+        pltpu.make_async_copy(predicted_ref, predicted_out, sent.at[own_x]),
+        pltpu.make_async_copy(fields_ref.at[0], phase_out, sent.at[own_x + 1]),
+        pltpu.make_async_copy(fields_ref.at[1], solute_out, sent.at[own_x + 2]),
+    ]
+    for copy in copies:
+        copy.start()
+    for index in range(SPREAD):
+        lift_ref[:, index * WIDTH : (index + 1) * WIDTH] = narrow_ref[...]
+    for index in range(1, width // LANES):
+        lift_ref[:, index * LANES : (index + 1) * LANES] = lift_ref[:, 0:LANES]
     shape = (2 * WIDTH, width)
     row = lax.broadcasted_iota(jnp.int32, shape, 0)
     column = lax.broadcasted_iota(jnp.int32, shape, 1)
@@ -809,6 +888,22 @@
         both = jnp.where(low, head.astype(jnp.float32), rest.astype(jnp.float32)).astype(NARROW)
         return jnp.concatenate([both, head], axis=1)
 
+    line = modes_ref[extra + 1 : extra + 2, :]
+    square = (WIDTH, WIDTH)
+    diagonal = lax.broadcasted_iota(jnp.int32, square, 0) == lax.broadcasted_iota(
+        jnp.int32, square, 1
+    )
+    local = jnp.zeros(square, jnp.float32)
+    for k in range(2):
+        sums = jnp.broadcast_to(line[:, k * WIDTH : (k + 1) * WIDTH], square)
+        sums = jnp.sum(jnp.where(diagonal, sums, 0.0), axis=1, keepdims=True)
+        local = local + sums * narrow_ref[k : k + 1, :]
+    local_ref[...] = scale * local
+    proj_ref[...] = scale * line[:, 2 * WIDTH : 3 * WIDTH]
+    copies.append(pltpu.make_async_copy(local_ref, local_out, sent.at[own_x + 3]))
+    copies.append(pltpu.make_async_copy(proj_ref, proj_out, sent.at[own_x + 4]))
+    copies[3].start()
+    copies[4].start()
     grads = jnp.concatenate(
         [modes_ref[pl.ds(place, modes_z, stride=chunk), :] for place in range(extra)], axis=0
     )
@@ -821,7 +916,6 @@
     column = lax.broadcasted_iota(jnp.int32, (2 * LANES, 2 * LANES), 1) // WIDTH
     spread = one_where(place == column // 4 * 2 + column % 2)
     own = lane // (4 * own_x) * own_x + lane % own_x
-    copies = []
     for plane in range(own_x):
         chosen = jnp.concatenate(
             [jnp.where(own == row * own_x + plane, modes, 0.0) for row in range(own_y)], axis=0
@@ -844,18 +938,6 @@
             pltpu.make_async_copy(held.at[:, plane], grad_ref.at[:, plane], sent.at[plane])
         )
         copies[-1].start()
-    line = modes_ref[extra + 1 : extra + 2, :]
-    square = (WIDTH, WIDTH)
-    diagonal = lax.broadcasted_iota(jnp.int32, square, 0) == lax.broadcasted_iota(
-        jnp.int32, square, 1
-    )
-    local = jnp.zeros(square, jnp.float32)
-    for k in range(2):
-        sums = jnp.broadcast_to(line[:, k * WIDTH : (k + 1) * WIDTH], square)
-        sums = jnp.sum(jnp.where(diagonal, sums, 0.0), axis=1, keepdims=True)
-        local = local + sums * lift_ref[k : k + 1, 0:WIDTH]
-    local_ref[...] = scale * local
-    proj_ref[...] = scale * line[:, 2 * WIDTH : 3 * WIDTH]
     for copy in copies:
         copy.wait()
 
@@ -882,7 +964,7 @@
     both = both.reshape(4 * total_x, 4 * modes_x)
     return {
         "z_plain": left_table(plain_z),
-        "z_forth": left_table(weighted_z),
+        "z_forth": np.concatenate(halves(weighted_z), axis=0),
         "z_back": left_table(weighted_z.T),
         "y_first": left_table(order_y),
         "x_first": right_table(both),
@@ -955,9 +1037,14 @@
     far = pl.BlockSpec(memory_space=pltpu.HBM)
     near = pl.BlockSpec(memory_space=pltpu.VMEM)
     weight_bytes = 8 * own_x * own_y * modes_z * width
-    head = jnp.concatenate([phase[:2], solute[:2], undercool[:1]])
-    tail = jnp.concatenate([phase[-2:], solute[-2:], undercool[-1:]])
     held = jnp.stack([phase, solute, undercool])
+    head, tail = call(
+        edge_kernel,
+        (like(5, cells_y, depth), like(5, cells_y, depth)),
+        [],
+        1000,
+        40 * tile * depth,
+    )(held)
 
     def ring(values, axis, step):
         count = lax.axis_size(axis)
@@ -987,17 +1074,25 @@
     )(held, before, after)
     low, high = ring(tail, "gy", 1), ring(head, "gy", -1)
     extended_shape = pltpu.VMEM((cells_x + 4, cells_y + 16, depth), real)
-    phase_next, solute_next, spectra = call(
+    stepped, spectra = call(
         step_kernel,
-        (like(*phase.shape), like(*phase.shape), like(*mixed_weights.shape)),
+        (like(2, *phase.shape), like(*mixed_weights.shape)),
         [extended_shape] * 4 + [pltpu.VMEM((depth // LANES, 2 * tile, LANES), real)],
         400 * tile * depth,
         80 * tile * depth,
     )(held, before, after, low, high, table["z_plain"], mixed_weights)
     gathered = exchange(spectra.reshape(-1, 2, LANES)).reshape(spectra.shape)
-    modes, fields = call(
+    spread_shape = (cells_x, depth, cells_y * WIDTH)
+    modes, fields, vectors, base, weight, lines = call(
         functools.partial(spectral_kernel, shape),
-        (like(devices, LANES), like(devices * 2 * cells_x * (cells_y // SPREAD), LANES)),
+        (
+            like(devices, LANES),
+            like(devices * 2 * cells_x * (cells_y // SPREAD), LANES),
+            like(4, cells_y * WIDTH),
+            like(*spread_shape),
+            like(*spread_shape),
+            jax.ShapeDtypeStruct((cells_x, 4 * cells_y, depth), NARROW),
+        ),
         [
             pltpu.VMEM((modes_x // SPREAD, 2 * total_y, LANES), real),
             pltpu.VMEM((2 * modes_x * (total_y // SPREAD), LANES), real),
@@ -1012,36 +1107,21 @@
         table["x_first"],
         table["y_back"],
         table["x_back"],
+        stepped,
+        cotangent.reshape(tile, depth),
+        lift,
+        local_weight,
+        local_bias.reshape(1, WIDTH),
+        proj_weight.reshape(1, WIDTH),
     )
     fields = exchange(fields)
-    mixed = jnp.dot(local_weight, lift_weight, precision=EXACT)
-    vectors = jnp.tile(
-        jnp.stack([mixed[:, 0], mixed[:, 1], local_bias, proj_weight]), (1, cells_y)
-    )
-    spread_shape = (cells_x, depth, cells_y * WIDTH)
-    base, spread, lines = call(
-        prepare_kernel,
-        (
-            like(*spread_shape),
-            jax.ShapeDtypeStruct((depth, 2 * tile), NARROW),
-            jax.ShapeDtypeStruct((cells_x, 2 * cells_y, 3 * depth), NARROW),
-        ),
-        [],
-        100_000_000,
-        5_000_000,
-    )(
-        phase_next.reshape(tile, depth),
-        solute_next.reshape(tile, depth),
-        cotangent.reshape(tile, depth),
-        vectors,
-    )
     predicted, spectra = call(
         functools.partial(field_kernel, cells_y),
         (like(tile, depth), like(*fields.shape)),
         [],
         1_000_000_000,
         2_000_000,
-    )(fields, base, spread, lines, vectors, table["z_back"], table["z_forth"])
+    )(fields, base, weight, lines, vectors, table["z_back"], table["z_forth"])
     spectra = exchange(spectra)
     chunk = 2 * own_x * own_y * WIDTH // LANES + 2
     gradients = call(
@@ -1055,19 +1135,28 @@
         2_000_000,
     )(spectra, modes, table["x_forth"], table["y_forth"])
     gradients = exchange(gradients.reshape(-1, 2, LANES)).reshape(gradients.shape)
-    grad_local, grad_proj, grad_spectral = call(
+    grad_local, grad_proj, predicted, phase_next, solute_next, grad_spectral = call(
         functools.partial(outer_kernel, 1.0 / math.sqrt(total_x * total_y * depth)),
-        (like(WIDTH, WIDTH), like(1, WIDTH), like(*spectral_weight.shape)),
+        (
+            like(WIDTH, WIDTH),
+            like(1, WIDTH),
+            like(*predicted.shape),
+            like(*phase.shape),
+            like(*phase.shape),
+            like(*spectral_weight.shape),
+        ),
         [
             pltpu.VMEM((8 * WIDTH, width), NARROW),
+            pltpu.VMEM((WIDTH, WIDTH), real),
+            pltpu.VMEM((1, WIDTH), real),
+            pltpu.VMEM((2, width), real),
             pltpu.VMEM(spectral_weight.shape, real),
-            pltpu.SemaphoreType.DMA((own_x,)),
+            pltpu.SemaphoreType.DMA((own_x + 5,)),
         ],
         weight_bytes * 4 * WIDTH,
         weight_bytes,
-        limit=SMALL_VMEM,
-        out_specs=(near, near, far),
-    )(gradients, jnp.tile(lift_weight.T, (1, WIDTH)))
+        out_specs=(far,) * 6,
+    )(gradients, lift, predicted, stepped)
     return (
         phase_next,
         solute_next,

time: 107 us -> 101 us (0.944)
  blocking collectives: 38.4 us -> 71.4 us
  waiting for transfers between devices: 25.7 us -> 1.88 us
  starting transfers between devices: 12.9 us -> 7.72 us
  local copies, waits for them, and re-layouts: 5.2 us -> 0.09 us
  Pallas kernels: 22.4 us -> 17.9 us
    all_to_all x2 -> x4, blocking collectives: 38.4 us -> 71.4 us  [exchange(): lax.all_to_all(values, ('gx', 'gy'), split_axis=0, concat_axis=0, tiled=T...]
    all_to_all x2 -> x0, waiting for transfers between devices: 24.7 us -> none  [exchange(): lax.all_to_all(values, ('gx', 'gy'), split_axis=0, concat_axis=0, tiled=T...]
    all_to_all x2 -> x0, starting transfers between devices: 5.19 us -> none  [exchange(): lax.all_to_all(values, ('gx', 'gy'), split_axis=0, concat_axis=0, tiled=T...]
    unnamed x34 -> x28, local copies, waits for them, and re-layouts: 2.83 us -> 0.09 us
    slice x3 -> x0, local copies, waits for them, and re-layouts: 2.2 us -> none  [per_device_fast(): tail = jnp.concatenate([phase[-2:], solute[-2:], undercool[-1:]])]
    pallas_call x2, Pallas kernels: 2.79 us -> 1.26 us  [the longest x1 1.25 us: per_device_fast(): call(step_kernel, (like(2, *phase.shape), like(*mixed_weights.shape)), [e...]
    pallas_call x1, Pallas kernels: 6.24 us -> 4.75 us  [per_device_fast(): call(functools.partial(contract_kernel, planes), like(modes_z * (own_x *...]
  transfers between devices with their start and end apart: 6 -> 4, of which waited for: 4 -> 2; matrix products, arithmetic and copies ran while one was open for 1% -> 0% of each run, Pallas kernels for 7% -> 5%
where the time goes in v3:
time: 101 us
  blocking collectives  71.4 us (71%)
  Pallas kernels  17.9 us (18%)
  starting transfers between devices  7.72 us (8%)
  waiting for transfers between devices  1.88 us (2%)
    all_to_all x4, blocking collectives, exchange(): lax.all_to_all(values, ('gx', 'gy'), split_axis=0, concat_axis=0, tiled=T...  71.4 us
    ppermute x4, starting transfers between devices, ring(): lax.ppermute(values, axis, [(i, (i + step) % count) for i in range(count)])  7.72 us
    pallas_call x1, Pallas kernels, per_device_fast(): call(functools.partial(contract_kernel, planes), like(modes_z * (own_x *...  4.75 us
    pallas_call x1, Pallas kernels, per_device_fast(): call(functools.partial(outer_kernel, 1.0 / math.sqrt(total_x * total_y *...  4.08 us
    pallas_call x1, Pallas kernels, per_device_fast(): call(functools.partial(spectral_kernel, shape), (like(devices, LANES), li...  3.56 us
    pallas_call x1, Pallas kernels, per_device_fast(): call(functools.partial(field_kernel, cells_y), (like(tile, depth), like(*...  3.28 us
  transfers between devices with their start and end apart: 4, of which 2 were waited for; matrix products, arithmetic and copies ran while one was open for 0% of the time, Pallas kernels for 5%

profile of v3, /device:TPU:0, one launch (start us, length us, event | category | flops | bytes accessed | tf_op | source)
XLA Modules:
  0.0 100.8 jit_solution(11758440788001978564)
XLA Ops:
  0.6 0.9 pad_maximum_fusion.held_ref
  1.6 0.0 copy-start.11
  1.6 0.5 collective-permute-start
  2.1 2.0 %collective-permute-start.1 = (f32[5,8,256]{2,1,0:T(8,128)S(1)}, f32[5,8,256]{2,1,0:T(8,128)S(1)}, u32[]{:S(2)}, u32[]{:S(2)}) collective-permute-start(f32[5,8,256]{2,1,0:T(8,128)S(1)} %get-tuple-element.32), channel_id=1, source_target_pairs={{0,24},{8,0},{16,8},{24,16},{1,25},{9,1},{17,9},{25,17},{2,26},{10... | collective-permute-start | bytes 122888 | tf_op jit(solution)/shard_map/ppermute | solution.py:1051
  4.1 1.6 %collective-permute-done.before_ref = f32[5,8,256]{2,1,0:T(8,128)S(1)} collective-permute-done((f32[5,8,256]{2,1,0:T(8,128)S(1)}, f32[5,8,256]{2,1,0:T(8,128)S(1)}, u32[]{:S(2)}, u32[]{:S(2)}) %collective-permute-start) | collective-permute-done | bytes 40992 | tf_op jit(solution)/shard_map/ppermute | solution.py:1051
  5.7 0.3 collective-permute-done.1.after_ref
  6.0 0.0 copy-start.1
  6.0 0.0 copy-start.2
  6.0 0.0 copy-start.4
  6.1 0.0 copy-start.5
  6.1 0.0 copy-start.7
  6.1 0.0 copy-start.9
  6.1 0.0 copy-start.10
  6.1 0.0 copy-start.12
  6.1 0.0 copy-start.13
  6.1 0.0 copy-start
  6.1 0.0 copy-start.3
  6.2 2.1 %collective-permute-start.2 = (f32[10,8,256]{2,1,0:T(8,128)S(1)}, f32[10,8,256]{2,1,0:T(8,128)S(1)}, u32[]{:S(2)}, u32[]{:S(2)}) collective-permute-start(f32[10,8,256]{2,1,0:T(8,128)S(1)} %get-tuple-element.33), channel_id=1, source_target_pairs={{0,1},{1,2},{2,3},{3,4},{4,5},{5,6},{6,7},{7,0},{8,9},{9,10},{10,1... | collective-permute-start | bytes 245768 | tf_op jit(solution)/shard_map/ppermute | solution.py:1051
  8.2 0.0 copy-start.6
  8.2 0.0 copy-start.8
  8.2 3.1 %collective-permute-start.3 = (f32[10,8,256]{2,1,0:T(8,128)S(1)}, f32[10,8,256]{2,1,0:T(8,128)S(1)}, u32[]{:S(2)}, u32[]{:S(2)}) collective-permute-start(f32[10,8,256]{2,1,0:T(8,128)S(1)} %get-tuple-element.34), channel_id=1, source_target_pairs={{0,7},{1,0},{2,1},{3,2},{4,3},{5,4},{6,5},{7,6},{8,15},{9,8},{10,9... | collective-permute-start | bytes 245768 | tf_op jit(solution)/shard_map/ppermute | solution.py:1051
  11.4 0.0 copy-done.11
  11.4 4.8 %shard_map.219.mixed_ref = f32[1088,128]{1,0:T(8,128)S(1)} custom-call(f32[2,32]{1,0:T(2,128)S(1)} %bitcast.26, f32[2,8,4,32,1024]{4,3,2,1,0:T(8,128)} %weight_ref.1), custom_call_target="tpu_custom_call" | custom-call | flops 1073741824 | bytes 8388608 | tf_op jit(solution)/shard_map/pallas_call | solution.py:1056
  16.1 0.0 collective-permute-done.2.low_ref
  16.1 0.0 collective-permute-done.3.high_ref
  16.1 0.0 copy-done.1
  16.2 1.3 %shard_map.220 = (f32[2,8,8,256]{3,2,1,0:T(8,128)S(1)}, f32[1088,128]{1,0:T(8,128)S(1)}) custom-call(f32[3,8,8,256]{3,2,1,0:T(8,128)S(1)} %pad_maximum_fusion.held_ref, f32[5,8,256]{2,1,0:T(8,128)S(1)} %collective-permute-done.before_ref, f32[5,8,256]{2,1,0:T(8,128)S(1)} %collective-permute-done.1.after_ref, ...), custom_call_target="tpu_custom_call" | custom-call | flops 6553600 | bytes 1310720 | tf_op jit(solution)/shard_map/pallas_call | solution.py:1077
  17.4 21.1 %all_to_all.32 = f32[544,2,128]{2,1,0:T(2,128)S(1)} all-to-all(f32[544,2,128]{2,1,0:T(2,128)S(1)} %bitcast.21), channel_id=1, replica_groups=mesh['gx'=4,'gy'=8] {'gx','gy'}, dimensions={0} | all-to-all | bytes 1114112 | tf_op jit(solution)/shard_map/all_to_all | solution.py:1009
  38.5 0.0 copy-done.2
  38.5 0.0 copy-done.4
  38.5 0.0 copy-done.5
  38.5 0.0 copy-done.7
  38.5 0.0 copy-done.9
  38.5 0.0 copy-done.10
  38.5 0.0 copy-done.12
  38.5 0.0 copy-done.13
  38.5 3.6 %shard_map.221 = (f32[32,128]{1,0:T(8,128)S(1)}, f32[1024,128]{1,0:T(8,128)S(1)}, f32[4,256]{1,0:T(4,128)S(1)}, f32[8,256,256]{2,1,0:T(8,128)S(1)}, f32[8,256,25...) custom-call(f32[1088,128]{1,0:T(8,128)S(1)} %bitcast.17, bf16[64,384]{1,0:T(8,128)(2,1)S(1)} %copy-done.7, ...), custom_call_target="tpu_custom_call" | custom-call | flops 100000000 | bytes 2000000 | tf_op jit(solution)/shard_map/pallas_call | solution.py:1086
  42.1 18.4 %all_to_all.33 = f32[32,32,128]{2,1,0:T(8,128)S(1)} all-to-all(f32[32,32,128]{2,1,0:T(8,128)S(1)} %bitcast.22), channel_id=1, replica_groups=mesh['gx'=4,'gy'=8] {'gx','gy'}, dimensions={0} | all-to-all | bytes 1048576 | tf_op jit(solution)/shard_map/all_to_all | solution.py:1009
  60.5 0.0 copy-done
  60.5 0.0 copy-done.3
  60.5 3.3 %shard_map.222 = (f32[64,256]{1,0:T(8,128)S(1)}, f32[1024,128]{1,0:T(8,128)S(1)}) custom-call(f32[1024,128]{1,0:T(8,128)S(1)} %bitcast.19, f32[8,256,256]{2,1,0:T(8,128)S(1)} %get-tuple-element.39.base_ref, f32[8,256,256]{2,1,0:T(8,128)S(1)} %get-tuple-element.40.weight_ref, bf16[8,32,256]{2,1,0:T(8,128)(2,1)S(1)} %get-tuple-element.41.table_ref, ...), custom_call_target="tpu_custom_call" | custom-call | flops 1000000000 | bytes 2000000 | tf_op jit(solution)/shard_map/pallas_call | solution.py:1118
  63.8 18.4 %all_to_all.34 = f32[32,32,128]{2,1,0:T(8,128)S(1)} all-to-all(f32[32,32,128]{2,1,0:T(8,128)S(1)} %bitcast.23), channel_id=1, replica_groups=mesh['gx'=4,'gy'=8] {'gx','gy'}, dimensions={0} | all-to-all | bytes 1048576 | tf_op jit(solution)/shard_map/all_to_all | solution.py:1009
  82.3 0.0 copy-done.6
  82.3 0.0 copy-done.8
  82.3 0.9 shard_map.223
  83.2 13.5 %all_to_all.35 = f32[288,2,128]{2,1,0:T(2,128)S(1)} all-to-all(f32[288,2,128]{2,1,0:T(2,128)S(1)} %bitcast.20), channel_id=1, replica_groups=mesh['gx'=4,'gy'=8] {'gx','gy'}, dimensions={0} | all-to-all | bytes 589824 | tf_op jit(solution)/shard_map/all_to_all | solution.py:1009
  96.7 4.1 %shard_map.224 = (f32[32,32]{1,0:T(8,128)}, f32[1,32]{1,0:T(1,128)}, f32[64,256]{1,0:T(8,128)}, f32[8,8,256]{2,1,0:T(8,128)}, f32[8,8,256]{2,1,0:T(8,128)}, /*index=5*/f32[2,8,4,32,1024]{4,3,2,1,0:T(8,128)}) custom-call(f32[576,128]{1,0:T(8,128)S(1)} %bitcast.24, f32[2,32]{1,0:T(2,128)S(1)} %bitcast.28, f32[64,256]{1,0:T(8,128)S(1)} %get-tuple-element.45.predicted_ref, ...), custom_call_target="tpu_custom_call" | custom-call | flops 1073741824 | bytes 8388608 | tf_op jit(solution)/shard_map/pallas_call | solution.py:1138
  (2 shorter events, 0.0 us)
Async XLA Ops:
  1.6 9.8 %copy-start.11 = (f32[32,2]{0,1:T(2,128)S(1)}, f32[32,2]{0,1:T(2,128)}, u32[]{:S(2)}) copy-start(f32[32,2]{0,1:T(2,128)} %param.21) | copy-start | bytes 772
  1.6 4.1 %collective-permute-start = (f32[5,8,256]{2,1,0:T(8,128)S(1)}, f32[5,8,256]{2,1,0:T(8,128)S(1)}, u32[]{:S(2)}, u32[]{:S(2)}) collective-permute-start(f32[5,8,256]{2,1,0:T(8,128)S(1)} %get-tuple-element.31), channel_id=1, source_target_pairs={{0,8},{8,16},{16,24},{24,0},{1,9},{9,17},{17,25},{25,1},{2,10},{10... | collective-permute-start | bytes 122888 | tf_op jit(solution)/shard_map/ppermute | solution.py:1051
  2.1 3.9 %collective-permute-start.1 = (f32[5,8,256]{2,1,0:T(8,128)S(1)}, f32[5,8,256]{2,1,0:T(8,128)S(1)}, u32[]{:S(2)}, u32[]{:S(2)}) collective-permute-start(f32[5,8,256]{2,1,0:T(8,128)S(1)} %get-tuple-element.32), channel_id=1, source_target_pairs={{0,24},{8,0},{16,8},{24,16},{1,25},{9,1},{17,9},{25,17},{2,26},{10... | collective-permute-start | bytes 122888 | tf_op jit(solution)/shard_map/ppermute | solution.py:1051
  6.0 10.1 %copy-start.1 = (bf16[64,768]{1,0:T(8,128)(2,1)S(1)}, bf16[64,768]{1,0:T(8,128)(2,1)}, u32[]{:S(2)}) copy-start(bf16[64,768]{1,0:T(8,128)(2,1)} %constant.18.clone.table_ref) | copy-start | bytes 294916
  6.0 32.4 %copy-start.2 = (bf16[384,128]{1,0:T(8,128)(2,1)S(1)}, bf16[384,128]{1,0:T(8,128)(2,1)}, u32[]{:S(2)}) copy-start(bf16[384,128]{1,0:T(8,128)(2,1)} %constant.20.clone.x_in_ref) | copy-start | bytes 294916
  6.0 32.4 %copy-start.4 = (f32[8,8,256]{2,1,0:T(8,128)S(1)}, f32[8,8,256]{2,1,0:T(8,128)}, u32[]{:S(2)}) copy-start(f32[8,8,256]{2,1,0:T(8,128)} %param.26) | copy-start | bytes 196612
  6.1 32.4 %copy-start.5 = (bf16[128,192]{1,0:T(8,128)(2,1)S(1)}, bf16[128,192]{1,0:T(8,128)(2,1)}, u32[]{:S(2)}) copy-start(bf16[128,192]{1,0:T(8,128)(2,1)} %constant.21.clone.y_out_ref) | copy-start | bytes 147460
  6.1 32.4 %copy-start.7 = (bf16[64,384]{1,0:T(8,128)(2,1)S(1)}, bf16[64,384]{1,0:T(8,128)(2,1)}, u32[]{:S(2)}) copy-start(bf16[64,384]{1,0:T(8,128)(2,1)} %constant.19.clone.y_in_ref) | copy-start | bytes 147460
  6.1 32.4 %copy-start.9 = (bf16[64,192]{1,0:T(8,128)(2,1)S(1)}, bf16[64,192]{1,0:T(8,128)(2,1)}, u32[]{:S(2)}) copy-start(bf16[64,192]{1,0:T(8,128)(2,1)} %constant.22.clone.x_out_ref) | copy-start | bytes 73732
  6.1 32.4 %copy-start.10 = (f32[32,32]{1,0:T(8,128)S(1)}, f32[32,32]{1,0:T(8,128)}, u32[]{:S(2)}) copy-start(f32[32,32]{1,0:T(8,128)} %local_ref.1) | copy-start | bytes 12292
  6.1 32.4 %copy-start.12 = (f32[32]{0:T(128)S(1)}, f32[32]{0:T(128)}, u32[]{:S(2)}) copy-start(f32[32]{0:T(128)} %param.24) | copy-start | bytes 388
  6.1 32.4 %copy-start.13 = (f32[32]{0:T(128)S(1)}, f32[32]{0:T(128)}, u32[]{:S(2)}) copy-start(f32[32]{0:T(128)} %param.25) | copy-start | bytes 388
  6.1 54.4 %copy-start = (bf16[256,192]{1,0:T(8,128)(2,1)S(1)}, bf16[256,192]{1,0:T(8,128)(2,1)}, u32[]{:S(2)}) copy-start(bf16[256,192]{1,0:T(8,128)(2,1)} %constant.23.clone.back_ref) | copy-start | bytes 294916
  6.1 54.4 %copy-start.3 = (bf16[128,256]{1,0:T(8,128)(2,1)S(1)}, bf16[128,256]{1,0:T(8,128)(2,1)}, u32[]{:S(2)}) copy-start(bf16[128,256]{1,0:T(8,128)(2,1)} %constant.24.clone.forth_ref) | copy-start | bytes 196612
  6.2 10.0 %collective-permute-start.2 = (f32[10,8,256]{2,1,0:T(8,128)S(1)}, f32[10,8,256]{2,1,0:T(8,128)S(1)}, u32[]{:S(2)}, u32[]{:S(2)}) collective-permute-start(f32[10,8,256]{2,1,0:T(8,128)S(1)} %get-tuple-element.33), channel_id=1, source_target_pairs={{0,1},{1,2},{2,3},{3,4},{4,5},{5,6},{6,7},{7,0},{8,9},{9,10},{10,1... | collective-permute-start | bytes 245768 | tf_op jit(solution)/shard_map/ppermute | solution.py:1051
  8.2 74.0 %copy-start.6 = (bf16[64,384]{1,0:T(8,128)(2,1)S(1)}, bf16[64,384]{1,0:T(8,128)(2,1)}, u32[]{:S(2)}) copy-start(bf16[64,384]{1,0:T(8,128)(2,1)} %constant.26.clone.y_in_ref) | copy-start | bytes 147460
  8.2 74.0 %copy-start.8 = (bf16[64,192]{1,0:T(8,128)(2,1)S(1)}, bf16[64,192]{1,0:T(8,128)(2,1)}, u32[]{:S(2)}) copy-start(bf16[64,192]{1,0:T(8,128)(2,1)} %constant.25.clone.x_in_ref) | copy-start | bytes 73732
  8.2 7.9 %collective-permute-start.3 = (f32[10,8,256]{2,1,0:T(8,128)S(1)}, f32[10,8,256]{2,1,0:T(8,128)S(1)}, u32[]{:S(2)}, u32[]{:S(2)}) collective-permute-start(f32[10,8,256]{2,1,0:T(8,128)S(1)} %get-tuple-element.34), channel_id=1, source_target_pairs={{0,7},{1,0},{2,1},{3,2},{4,3},{5,4},{6,5},{7,6},{8,15},{9,8},{10,9... | collective-permute-start | bytes 245768 | tf_op jit(solution)/shard_map/ppermute | solution.py:1051

commit v4 on v3

--- a/solution.py
+++ b/solution.py
@@ -236,7 +236,6 @@
 
 LANES = 128
 SMALL_VMEM = 24 * 1024 * 1024
-LARGE_VMEM = 50 * 1024 * 1024
 PACK_COST = 50_000_000_000
 SPREAD = LANES // WIDTH
 NARROW = jnp.bfloat16
@@ -321,19 +320,54 @@
     ]
 
 
-def contract_kernel(planes, lift_ref, weight_ref, out_ref, held, arrived):
+def spread_cells(
+    lift_ref, local_ref, bias_ref, proj_ref, cotangent_ref, vector_ref, mix_ref, spread_ref
+):
+    planes, depth, wide = spread_ref.shape
+    tile = cotangent_ref.shape[0]
+    cells_y = tile // planes
+    lift, lift_rest = parts_of(lift_ref[...])
+    local, local_rest = parts_of(local_ref[...])
+    mixed = mul_rows(lift, local) + mul_rows(lift_rest, local) + mul_rows(lift, local_rest)
+    for index in range(wide // WIDTH):
+        place = slice(index * WIDTH, (index + 1) * WIDTH)
+        vector_ref[0:2, place] = mixed
+        vector_ref[2:3, place] = bias_ref[...]
+        vector_ref[3:4, place] = proj_ref[...]
+    head, rest = parts_of(vector_ref[...])
+    row = lax.broadcasted_iota(jnp.int32, (cells_y, wide), 0)
+    own = row == lax.broadcasted_iota(jnp.int32, (cells_y, wide), 1) // WIDTH
+
+    def diagonal(line):
+        return jnp.where(own, line.astype(jnp.float32), 0.0)
+
+    mixing = [diagonal(part[k : k + 1]) for k in range(2) for part in (head, head, rest)]
+    blank = jnp.zeros((2 * cells_y, wide), jnp.float32)
+    mix_ref[...] = jnp.concatenate(mixing + [blank], axis=0).astype(NARROW)
+    spread = jnp.concatenate(parts_of(cotangent_ref[...].T), axis=1)
+    cell = lax.broadcasted_iota(jnp.int32, (2 * tile, wide), 0) % tile
+    row = lax.broadcasted_iota(jnp.int32, (2 * tile, wide), 1) // WIDTH
+    for plane in range(planes):
+        spread_ref[plane] = mul(spread, one_where(cell == plane * cells_y + row))
+
+
+def contract_kernel(
+    planes,
+    lift_ref,
+    weight_ref,
+    local_ref,
+    bias_ref,
+    proj_ref,
+    cotangent_ref,
+    out_ref,
+    vector_ref,
+    mix_ref,
+    spread_ref,
+):
     _, own_x, own_y, modes_z, width = weight_ref.shape
     chunk = out_ref.shape[0] // modes_z
     steps = own_x // planes
 
-    def fetch(step):
-        block = pl.ds(step * planes, planes)
-        return pltpu.make_async_copy(
-            weight_ref.at[:, block], held.at[:, block], arrived.at[step]
-        )
-
-    for step in range(steps):
-        fetch(step).start()
     square = (WIDTH, WIDTH)
     diagonal = lax.broadcasted_iota(jnp.int32, square, 0) == lax.broadcasted_iota(
         jnp.int32, square, 1
@@ -360,10 +394,9 @@
     rows = planes * own_y * modes_z
     low = lax.broadcasted_iota(jnp.int32, (rows, LANES), 1) < 2 * WIDTH
     for step in range(steps):
-        fetch(step).wait()
         sums = []
         for part in range(2):
-            block = held[part, step * planes : (step + 1) * planes]
+            block = weight_ref[part, step * planes : (step + 1) * planes]
             head, rest = parts_of(block.reshape(rows, width))
             total = mul(head, mixing) + mul(rest, mixing)
             sums.append(total + turn(total, 2 * WIDTH))
@@ -375,6 +408,16 @@
                 out_ref[pl.ds(place, modes_z, stride=chunk), :] = result[
                     first : first + modes_z
                 ]
+    spread_cells(
+        lift_ref,
+        local_ref,
+        bias_ref,
+        proj_ref,
+        cotangent_ref,
+        vector_ref,
+        mix_ref,
+        spread_ref,
+    )
 
 
 def edge_kernel(held_ref, head_ref, tail_ref):
@@ -386,18 +429,16 @@
 
 def pack_kernel(held_ref, before_ref, after_ref, head_ref, tail_ref):
     _, cells_x, cells_y, _ = held_ref.shape
-
-    def put(target, phase, solute, cool):
-        head_ref[target, 0:2] = phase[:, 0:2]
-        head_ref[target, 2:4] = solute[:, 0:2]
-        head_ref[target, 4:5] = cool[:, 0:1]
-        tail_ref[target, 0:2] = phase[:, cells_y - 2 : cells_y]
-        tail_ref[target, 2:4] = solute[:, cells_y - 2 : cells_y]
-        tail_ref[target, 4:5] = cool[:, cells_y - 1 : cells_y]
-
-    put(slice(0, 1), before_ref[1:2], before_ref[3:4], before_ref[4:5])
-    put(slice(1, cells_x + 1), held_ref[0], held_ref[1], held_ref[2])
-    put(slice(cells_x + 1, cells_x + 2), after_ref[0:1], after_ref[2:3], after_ref[4:5])
+    for out, near, far in ((head_ref, 0, 1), (tail_ref, cells_y - 1, cells_y - 2)):
+        for plane in range(cells_x):
+            line = slice(plane, plane + 1)
+            for index in range(2):
+                out[2 * index, line] = held_ref[index, plane, near : near + 1]
+                out[2 * index + 1, line] = held_ref[index, plane, far : far + 1]
+            out[4, line] = held_ref[2, plane, near : near + 1]
+        for index in range(2):
+            out[5, 2 * index : 2 * index + 1] = before_ref[2 * index + 1, near : near + 1]
+            out[5, 2 * index + 1 : 2 * index + 2] = after_ref[2 * index, near : near + 1]
 
 
 def step_kernel(
@@ -424,13 +465,20 @@
         ext[2 : cells_x + 2, base:end] = held_ref[index]
         ext[0:2, base:end] = before_ref[first : first + 2]
         ext[cells_x + 2 : cells_x + 4, base:end] = after_ref[first : first + 2]
-        ext[1 : cells_x + 3, base - 2 : base] = low_ref[:, first : first + 2]
-        ext[1 : cells_x + 3, end : end + 2] = high_ref[:, first : first + 2]
+        for source, near, far in ((low_ref, base - 1, base - 2), (high_ref, end, end + 1)):
+            for plane in range(cells_x):
+                line = slice(plane, plane + 1)
+                ext[plane + 2, near : near + 1] = source[first, line]
+                ext[plane + 2, far : far + 1] = source[first + 1, line]
+            ext[1, near : near + 1] = source[5, first : first + 1]
+            ext[cells_x + 2, near : near + 1] = source[5, first + 1 : first + 2]
     cool_ext[2 : cells_x + 2, base:end] = held_ref[2]
     cool_ext[1:2, base:end] = before_ref[4:5]
     cool_ext[cells_x + 2 : cells_x + 3, base:end] = after_ref[4:5]
-    cool_ext[1 : cells_x + 3, base - 1 : base] = low_ref[:, 4:5]
-    cool_ext[1 : cells_x + 3, end : end + 1] = high_ref[:, 4:5]
+    for plane in range(cells_x):
+        line = slice(plane, plane + 1)
+        cool_ext[plane + 2, base - 1 : base] = low_ref[4, line]
+        cool_ext[plane + 2, end : end + 1] = high_ref[4, line]
 
     def sweep(reach):
         diff_ext[...] = diffusivity(phase_ext[...])
@@ -524,17 +572,13 @@
     y_out_ref,
     x_out_ref,
     fields_ref,
-    cotangent_ref,
-    lift_ref,
-    local_ref,
-    bias_ref,
-    proj_ref,
+    forth_ref,
+    chosen_ref,
+    gather_ref,
     modes_ref,
     send_ref,
-    vector_ref,
-    base_ref,
-    spread_ref,
     table_ref,
+    line_ref,
     lines_y,
     lines_x,
     rows_ref,
@@ -575,12 +619,8 @@
     chosen = jnp.concatenate(
         [jnp.where(lane == freq, modes, 0.0) for freq in range(modes_x)], axis=0
     )
-    place = lax.broadcasted_iota(jnp.int32, (2 * LANES, 2 * LANES), 0) % LANES // modes_x
-    group = lax.broadcasted_iota(jnp.int32, (2 * LANES, 2 * LANES), 1) // WIDTH
-    same = jnp.where(group < 4, group, (group + 2) % 4)
-    signed_one = jnp.where((group == 2) | (group == 3), -1.0, 1.0)
-    spread = jnp.where(place == same, signed_one, 0.0).astype(NARROW)
-    columns = mul(jnp.concatenate(parts_of(chosen), axis=1), spread)
+    columns = mul(jnp.concatenate(parts_of(chosen), axis=1), chosen_ref[...])
+    low = lax.broadcasted_iota(jnp.int32, (modes_y, LANES), 1) < 2 * WIDTH
     products = [[], []]
     for quad in range(quads_x):
         lines = [[], []]
@@ -592,14 +632,16 @@
                 column = columns[
                     freq * modes_y : (freq + 1) * modes_y, part * LANES : (part + 1) * LANES
                 ]
-                lines[part].append(weights * column)
+                line = weights * column
+                lines[part].append(line + turn(line, 2 * WIDTH))
         for part in range(2):
-            products[part].append(jnp.concatenate(lines[part], axis=1))
+            pairs = [
+                jnp.where(low, lines[part][index], lines[part][index + 1])
+                for index in range(0, SPREAD, 2)
+            ]
+            products[part].append(jnp.concatenate(pairs, axis=1))
     products = jnp.concatenate(products[0] + products[1], axis=0)
-    gather = lax.broadcasted_iota(jnp.int32, (2 * SPREAD * LANES, LANES), 0) % (SPREAD * LANES)
-    column = lax.broadcasted_iota(jnp.int32, (2 * SPREAD * LANES, LANES), 1)
-    gather = one_where(gather // LANES * WIDTH + gather % WIDTH == column)
-    products = mul(jnp.concatenate(parts_of(products), axis=1), gather)
+    products = mul(jnp.concatenate(parts_of(products), axis=1), gather_ref[...])
     stacked = [
         jnp.concatenate(
             [
@@ -637,87 +679,75 @@
                     first : first + cells_x, quad * LANES : (quad + 1) * LANES
                 ]
     pack_modes(shape, modes, modes_ref, rows_ref)
-    prepare(
-        fields_ref,
-        cotangent_ref,
-        lift_ref,
-        local_ref,
-        bias_ref,
-        proj_ref,
-        vector_ref,
-        base_ref,
-        spread_ref,
-        table_ref,
-    )
-
-
-def prepare(
-    fields_ref,
-    cotangent_ref,
-    lift_ref,
-    local_ref,
-    bias_ref,
-    proj_ref,
-    vector_ref,
-    base_ref,
-    weight_ref,
-    table_ref,
-):
-    planes, depth, wide = base_ref.shape
-    tile = cotangent_ref.shape[0]
-    cells_y = tile // planes
-    lift, lift_rest = parts_of(lift_ref[...])
-    local, local_rest = parts_of(local_ref[...])
-    mixed = mul_rows(lift, local) + mul_rows(lift_rest, local) + mul_rows(lift, local_rest)
-    for index in range(wide // WIDTH):
-        place = slice(index * WIDTH, (index + 1) * WIDTH)
-        vector_ref[0:2, place] = mixed
-        vector_ref[2:3, place] = bias_ref[...]
-        vector_ref[3:4, place] = proj_ref[...]
-    fields = (
-        fields_ref[0].reshape(tile, depth),
-        fields_ref[1].reshape(tile, depth) - SOLUTE_MEAN,
-        cotangent_ref[...],
-    )
-    spread = jnp.concatenate(
-        [jnp.concatenate(parts_of(values.T), axis=1) for values in fields], axis=0
-    )
-    cell = lax.broadcasted_iota(jnp.int32, (2 * tile, wide), 0) % tile
-    row = lax.broadcasted_iota(jnp.int32, (2 * tile, wide), 1) // WIDTH
+    prepare(fields_ref, forth_ref, table_ref, line_ref)
+
+
+def prepare(fields_ref, forth_ref, table_ref, line_ref):
+    planes, depth, _ = table_ref.shape
+    cells_y = fields_ref.shape[2]
+    tile = planes * cells_y
+    rows = forth_ref.shape[0] // 2
+    fields = (fields_ref[0].reshape(tile, depth), fields_ref[1].reshape(tile, depth) - SOLUTE_MEAN)
+    blank = jnp.zeros((2 * cells_y, depth), jnp.float32)
+    table = forth_ref[rows:].astype(jnp.float32)
     for plane in range(planes):
-        values = mul(spread, one_where(cell == plane * cells_y + row))
-        base_ref[plane] = (
-            values[0:depth] * vector_ref[0:1, :]
-            + values[depth : 2 * depth] * vector_ref[1:2, :]
-            + vector_ref[2:3, :]
-        )
-        weight_ref[plane] = values[2 * depth :]
-        lines = [values[plane * cells_y : (plane + 1) * cells_y] for values in fields[:2]]
-        table_ref[plane] = jnp.concatenate(parts_of(jnp.concatenate(lines, axis=0)), axis=0)
+        lines = [values[plane * cells_y : (plane + 1) * cells_y] for values in fields]
+        pieces = [[part.astype(jnp.float32) for part in parts_of(values)] for values in lines]
+        both = [piece for head, rest in pieces for piece in (head, rest, head)]
+        both = jnp.concatenate([table] + both + [blank], axis=0)
+        table_ref[plane] = both.T.astype(NARROW)
+        pieces = [piece for pair in zip(*pieces) for piece in pair]
+        line_ref[plane] = jnp.concatenate(pieces, axis=0).astype(NARROW)
+
+
+def fold_channels(values):
+    quarter = values.shape[0] // SPREAD
+    parts = []
+    for first in range(0, values.shape[1], LANES):
+        pieces = [
+            values[index * quarter : (index + 1) * quarter, first : first + LANES]
+            for index in range(SPREAD)
+        ]
+        channel = lax.broadcasted_iota(jnp.int32, pieces[0].shape, 1) % WIDTH
+        span = WIDTH // 2
+        while len(pieces) > 1:
+            low = channel % (2 * span) < span
+            pieces = [
+                jnp.where(low, left + turn(left, -span), right + turn(right, span))
+                for left, right in zip(pieces[: len(pieces) // 2], pieces[len(pieces) // 2 :])
+            ]
+            span //= 2
+        parts.append(pieces[0])
+    return jnp.concatenate(parts, axis=1)
 
 
 def field_kernel(
     cells_y,
     field_ref,
-    base_ref,
+    table_ref,
+    mix_ref,
     weight_ref,
-    table_ref,
+    line_ref,
     vector_ref,
     back_ref,
     forth_ref,
     predicted_ref,
     send_ref,
+    shares_ref,
 ):
-    planes, depth, wide = base_ref.shape
-    rows = back_ref.shape[1] // 3
+    planes, depth, wide = weight_ref.shape
+    rows = forth_ref.shape[0] // 2
     halves_y = cells_y // SPREAD
     stride = halves_y * planes
+    bias = vector_ref[2:3, :]
     proj = vector_ref[3:4, :]
     root = math.sqrt(2.0 / math.pi)
     curve = 0.044715
     picker = one_where(
-        lax.broadcasted_iota(jnp.int32, (cells_y, 2 * wide), 0)
-        == lax.broadcasted_iota(jnp.int32, (cells_y, 2 * wide), 1) % wide // WIDTH
+        lax.broadcasted_iota(jnp.int32, (SPREAD * cells_y, 2 * wide), 0)
+        == lax.broadcasted_iota(jnp.int32, (SPREAD * cells_y, 2 * wide), 1)
+        % wide
+        // (WIDTH // SPREAD)
     )
     line_sums = jnp.zeros((2 * cells_y, wide), jnp.float32)
     proj_sums = jnp.zeros((8, wide), jnp.float32)
@@ -729,7 +759,9 @@
             ],
             axis=1,
         )
-        pre = mul(back_ref[...], thrice(spectra, 0)) + base_ref[plane]
+        spectra = jnp.concatenate([thrice(spectra, 0), mix_ref[...]], axis=0)
+        back = jnp.concatenate([back_ref[...], table_ref[plane]], axis=1)
+        pre = mul(back, spectra) + bias
         square = pre * pre
         bent = jnp.tanh(pre * (root + (root * curve) * square))
         upper = 0.5 + 0.5 * bent
@@ -738,11 +770,17 @@
         cotangent = weight_ref[plane]
         weighted = proj * cotangent
         grad = weighted * slope
-        predicted_ref[plane * cells_y : (plane + 1) * cells_y, :] = mul_rows(
-            picker, jnp.concatenate(parts_of(proj * active), axis=1)
+        share = mul_rows(
+            picker, jnp.concatenate(parts_of(fold_channels(proj * active)), axis=1)
         )
+        shares_ref[plane, :, 0 : depth // SPREAD] = share
+        for index in range(SPREAD):
+            predicted_ref[
+                plane * cells_y : (plane + 1) * cells_y,
+                index * (depth // SPREAD) : (index + 1) * (depth // SPREAD),
+            ] = shares_ref[plane, pl.ds(index, cells_y, stride=SPREAD), 0 : depth // SPREAD]
         head, rest = parts_of(grad)
-        lines = table_ref[plane]
+        lines = line_ref[plane]
         top = jnp.concatenate([forth_ref[0:rows], lines[0 : 2 * cells_y]], axis=0)
         low = jnp.concatenate([forth_ref[rows:], lines[2 * cells_y :]], axis=0)
         spectra = mul(jnp.concatenate([top, low], axis=0), head)
@@ -843,6 +881,8 @@
     narrow_ref,
     predicted_ref,
     fields_ref,
+    repeat_ref,
+    spread_ref,
     local_out,
     proj_out,
     predicted_out,
@@ -907,20 +947,14 @@
     grads = jnp.concatenate(
         [modes_ref[pl.ds(place, modes_z, stride=chunk), :] for place in range(extra)], axis=0
     )
-    repeat = lax.broadcasted_iota(jnp.int32, (2 * LANES, SPREAD * LANES), 0) % LANES
-    column = lax.broadcasted_iota(jnp.int32, (2 * LANES, SPREAD * LANES), 1)
-    repeat = one_where(repeat == column // LANES * WIDTH + column % WIDTH)
-    grads = mul(jnp.concatenate(parts_of(grads), axis=1), repeat)
+    grads = mul(jnp.concatenate(parts_of(grads), axis=1), repeat_ref[...])
     modes = modes_ref[pl.ds(extra, modes_z, stride=chunk), :]
-    place = lax.broadcasted_iota(jnp.int32, (2 * LANES, 2 * LANES), 0) % LANES // own_x % 4
-    column = lax.broadcasted_iota(jnp.int32, (2 * LANES, 2 * LANES), 1) // WIDTH
-    spread = one_where(place == column // 4 * 2 + column % 2)
     own = lane // (4 * own_x) * own_x + lane % own_x
     for plane in range(own_x):
         chosen = jnp.concatenate(
             [jnp.where(own == row * own_x + plane, modes, 0.0) for row in range(own_y)], axis=0
         )
-        columns = mul(jnp.concatenate(parts_of(chosen), axis=1), spread)
+        columns = mul(jnp.concatenate(parts_of(chosen), axis=1), spread_ref[...])
         reals, imags = [], []
         for row in range(own_y):
             real = columns[row * modes_z : (row + 1) * modes_z, 0:LANES]
@@ -962,10 +996,23 @@
     for field in range(2):
         both[:, :, field, :, :, field, :] = lines.transpose(2, 3, 4, 0, 1)
     both = both.reshape(4 * total_x, 4 * modes_x)
-    return {
+    index = np.arange(4 * LANES)
+    line = index[: 2 * LANES, None] % LANES
+    group = index[None, : 2 * LANES] // WIDTH
+    same = np.where(group < 4, group, (group + 2) % 4)
+    signs = np.where((group == 2) | (group == 3), -1.0, 1.0)
+    chosen = np.where(line // modes_x == same, signs, 0.0)
+    half = 2 * WIDTH
+    row, column = index[:, None] % (SPREAD * half), index[None, :LANES]
+    gather = row // half * WIDTH + row % WIDTH == column
+    repeat = line == index[None, :] // LANES * WIDTH + index[None, :] % WIDTH
+    spread = line // own_x % 4 == group // 4 * 2 + group % 2
+    masks = {"chosen": chosen, "gather": gather, "repeat": repeat, "spread": spread}
+    masks = {name: mask.astype(ml_dtypes.bfloat16) for name, mask in masks.items()}
+    return masks | {
         "z_plain": left_table(plain_z),
         "z_forth": np.concatenate(halves(weighted_z), axis=0),
-        "z_back": left_table(weighted_z.T),
+        "z_back": left_table(weighted_z.T)[:, : 4 * modes_z],
         "y_first": left_table(order_y),
         "x_first": right_table(both),
         "y_back": left_table(back_y),
@@ -981,6 +1028,7 @@
     return (
         width == WIDTH * WIDTH
         and modes_z == count_x * count_y
+        and 4 * modes_z == LANES
         and 4 * count_x * cells_x == LANES
         and 4 * count_x * own_x == LANES
         and 2 * cells_x * cells_y == LANES
@@ -1035,7 +1083,6 @@
         return jax.ShapeDtypeStruct(dims, real)
 
     far = pl.BlockSpec(memory_space=pltpu.HBM)
-    near = pl.BlockSpec(memory_space=pltpu.VMEM)
     weight_bytes = 8 * own_x * own_y * modes_z * width
     held = jnp.stack([phase, solute, undercool])
     head, tail = call(
@@ -1053,21 +1100,29 @@
     head, tail, lift = lax.optimization_barrier((head, tail, lift_weight.T))
     before, after = ring(tail, "gx", 1), ring(head, "gx", -1)
     planes = 2
-    mixed_weights = call(
+    spread_shape = (cells_x, depth, cells_y * WIDTH)
+    mixed_weights, vectors, mixing, weight = call(
         functools.partial(contract_kernel, planes),
-        like(modes_z * (own_x * own_y + 2), LANES),
-        [
-            pltpu.VMEM(spectral_weight.shape, real),
-            pltpu.SemaphoreType.DMA((own_x // planes,)),
-        ],
+        (
+            like(modes_z * (own_x * own_y + 2), LANES),
+            like(4, cells_y * WIDTH),
+            jax.ShapeDtypeStruct((8 * cells_y, cells_y * WIDTH), NARROW),
+            like(*spread_shape),
+        ),
+        [],
         weight_bytes * LANES,
         weight_bytes,
-        limit=LARGE_VMEM,
-        in_specs=[near, far],
-    )(lift, spectral_weight)
+    )(
+        lift,
+        spectral_weight,
+        local_weight,
+        local_bias.reshape(1, WIDTH),
+        proj_weight.reshape(1, WIDTH),
+        cotangent.reshape(tile, depth),
+    )
     head, tail = call(
         pack_kernel,
-        (like(cells_x + 2, 8, depth), like(cells_x + 2, 8, depth)),
+        (like(6, cells_x, depth), like(6, cells_x, depth)),
         [],
         PACK_COST,
         40 * tile * depth,
@@ -1082,15 +1137,12 @@
         80 * tile * depth,
     )(held, before, after, low, high, table["z_plain"], mixed_weights)
     gathered = exchange(spectra.reshape(-1, 2, LANES)).reshape(spectra.shape)
-    spread_shape = (cells_x, depth, cells_y * WIDTH)
-    modes, fields, vectors, base, weight, lines = call(
+    modes, fields, lines, own_lines = call(
         functools.partial(spectral_kernel, shape),
         (
             like(devices, LANES),
             like(devices * 2 * cells_x * (cells_y // SPREAD), LANES),
-            like(4, cells_y * WIDTH),
-            like(*spread_shape),
-            like(*spread_shape),
+            jax.ShapeDtypeStruct((cells_x, depth, LANES), NARROW),
             jax.ShapeDtypeStruct((cells_x, 4 * cells_y, depth), NARROW),
         ),
         [
@@ -1108,20 +1160,18 @@
         table["y_back"],
         table["x_back"],
         stepped,
-        cotangent.reshape(tile, depth),
-        lift,
-        local_weight,
-        local_bias.reshape(1, WIDTH),
-        proj_weight.reshape(1, WIDTH),
+        table["z_forth"],
+        table["chosen"],
+        table["gather"],
     )
     fields = exchange(fields)
     predicted, spectra = call(
         functools.partial(field_kernel, cells_y),
         (like(tile, depth), like(*fields.shape)),
-        [],
+        [pltpu.VMEM((cells_x, SPREAD * cells_y, LANES), real)],
         1_000_000_000,
         2_000_000,
-    )(fields, base, weight, lines, vectors, table["z_back"], table["z_forth"])
+    )(fields, lines, mixing, weight, own_lines, vectors, table["z_back"], table["z_forth"])
     spectra = exchange(spectra)
     chunk = 2 * own_x * own_y * WIDTH // LANES + 2
     gradients = call(
@@ -1156,7 +1206,7 @@
         weight_bytes * 4 * WIDTH,
         weight_bytes,
         out_specs=(far,) * 6,
-    )(gradients, lift, predicted, stepped)
+    )(gradients, lift, predicted, stepped, table["repeat"], table["spread"])
     return (
         phase_next,
         solute_next,

time: 101 us -> 99.3 us (0.983)
  Pallas kernels: 17.9 us -> 14.6 us
  blocking collectives: 71.4 us -> 72.9 us
    pallas_call x2, Pallas kernels: 4.79 us -> 2.8 us  [the longest x1 2.76 us: per_device_fast(): call(functools.partial(contract_kernel, planes), (like(modes_z * (own_x *...]
    all_to_all x4, blocking collectives: 71.4 us -> 72.9 us  [exchange(): lax.all_to_all(values, ('gx', 'gy'), split_axis=0, concat_axis=0, tiled=T...]
    pallas_call x1, Pallas kernels: 3.56 us -> 2.41 us  [per_device_fast(): call(functools.partial(spectral_kernel, shape), (like(devices, LANES), li...]
  transfers between devices with their start and end apart: 4 -> 4, of which waited for: 2 -> 2; matrix products, arithmetic and copies ran while one was open for 0% -> 0% of each run, Pallas kernels for 5% -> 3%
where the time goes in v4:
time: 99.3 us; the launch traced here: 99.1 us
  blocking collectives  72.9 us (73%)
  Pallas kernels  14.6 us (15%)
  starting transfers between devices  7.7 us (8%)
  waiting for transfers between devices  1.88 us (2%)
    all_to_all x4, blocking collectives, exchange(): lax.all_to_all(values, ('gx', 'gy'), split_axis=0, concat_axis=0, tiled=T...  72.9 us
    ppermute x4, starting transfers between devices, ring(): lax.ppermute(values, axis, [(i, (i + step) % count) for i in range(count)])  7.7 us
    pallas_call x1, Pallas kernels, per_device_fast(): call(functools.partial(outer_kernel, 1.0 / math.sqrt(total_x * total_y *...  4.07 us
    pallas_call x1, Pallas kernels, per_device_fast(): call(functools.partial(field_kernel, cells_y), (like(tile, depth), like(*...  3.14 us
    pallas_call x1, Pallas kernels, per_device_fast(): call(functools.partial(contract_kernel, planes), (like(modes_z * (own_x *...  2.76 us
    pallas_call x1, Pallas kernels, per_device_fast(): call(functools.partial(spectral_kernel, shape), (like(devices, LANES), li...  2.41 us
  transfers between devices with their start and end apart: 4, of which 2 were waited for; matrix products, arithmetic and copies ran while one was open for 0% of the time, Pallas kernels for 3%

profile of v4, /device:TPU:0, one launch (start us, length us, event | category | flops | bytes accessed | tf_op | source)
XLA Modules:
  0.0 99.1 jit_solution(12726711301009041443)
XLA Ops:
  0.6 0.9 pad_maximum_fusion.held_ref
  1.6 0.0 slice-start
  1.6 0.0 slice-start.1
  1.6 0.0 copy-start.4
  1.6 0.0 copy-start.11
  1.6 0.0 copy-start.12
  1.6 0.0 copy-start.13
  1.6 0.0 copy-start.14
  1.7 0.5 collective-permute-start
  2.2 2.0 %collective-permute-start.1 = (f32[5,8,256]{2,1,0:T(8,128)S(1)}, f32[5,8,256]{2,1,0:T(8,128)S(1)}, u32[]{:S(2)}, u32[]{:S(2)}) collective-permute-start(f32[5,8,256]{2,1,0:T(8,128)S(1)} %get-tuple-element.34), channel_id=1, source_target_pairs={{0,24},{8,0},{16,8},{24,16},{1,25},{9,1},{17,9},{25,17},{2,26},{10... | collective-permute-start | bytes 122888 | tf_op jit(solution)/shard_map/ppermute | solution.py:1098
  4.2 1.6 %collective-permute-done.before_ref = f32[5,8,256]{2,1,0:T(8,128)S(1)} collective-permute-done((f32[5,8,256]{2,1,0:T(8,128)S(1)}, f32[5,8,256]{2,1,0:T(8,128)S(1)}, u32[]{:S(2)}, u32[]{:S(2)}) %collective-permute-start) | collective-permute-done | bytes 40992 | tf_op jit(solution)/shard_map/ppermute | solution.py:1098
  5.8 0.3 collective-permute-done.1.after_ref
  6.1 0.0 copy-start.3
  6.1 0.0 copy-start
  6.1 0.0 copy-start.1
  6.1 0.0 copy-start.2
  6.2 0.0 copy-start.5
  6.2 0.0 copy-start.6
  6.2 0.0 copy-start.8
  6.2 0.0 copy-start.10
  6.2 0.0 copy-start.17
  6.2 2.1 %collective-permute-start.2 = (f32[6,8,256]{2,1,0:T(8,128)S(1)}, f32[6,8,256]{2,1,0:T(8,128)S(1)}, u32[]{:S(2)}, u32[]{:S(2)}) collective-permute-start(f32[6,8,256]{2,1,0:T(8,128)S(1)} %get-tuple-element.35), channel_id=1, source_target_pairs={{0,1},{1,2},{2,3},{3,4},{4,5},{5,6},{6,7},{7,0},{8,9},{9,10},{10,1... | collective-permute-start | bytes 147464 | tf_op jit(solution)/shard_map/ppermute | solution.py:1098
  8.3 3.1 %collective-permute-start.3 = (f32[6,8,256]{2,1,0:T(8,128)S(1)}, f32[6,8,256]{2,1,0:T(8,128)S(1)}, u32[]{:S(2)}, u32[]{:S(2)}) collective-permute-start(f32[6,8,256]{2,1,0:T(8,128)S(1)} %get-tuple-element.36), channel_id=1, source_target_pairs={{0,7},{1,0},{2,1},{3,2},{4,3},{5,4},{6,5},{7,6},{8,15},{9,8},{10,9... | collective-permute-start | bytes 147464 | tf_op jit(solution)/shard_map/ppermute | solution.py:1098
  11.4 0.0 slice-done
  11.4 0.0 slice-done.1
  11.4 0.0 copy-done.4
  11.4 0.0 copy-done.11
  11.4 0.0 copy-start.7
  11.5 0.0 copy-start.9
  11.5 0.0 copy-start.15
  11.5 0.0 copy-start.16
  11.5 2.8 %shard_map.255 = (f32[1088,128]{1,0:T(8,128)S(1)}, f32[4,256]{1,0:T(4,128)S(1)}, bf16[64,256]{1,0:T(8,128)(2,1)S(1)}, f32[8,256,256]{2,1,0:T(8,128)S(1)}) custom-call(f32[2,32]{1,0:T(2,128)S(1)} %bitcast.28, f32[2,8,4,32,1024]{4,3,2,1,0:T(8,128)S(1)} %bitcast.18, f32[32,32]{1,0:T(8,128)S(1)} %copy-done.11, f32[1,32]{1,0:T(1,128)S(1)} %bitcast.30, ...), custom_call_target="tpu_custom_call" | custom-call | flops 1073741824 | bytes 8388608 | tf_op jit(solution)/shard_map/pallas_call | solution.py:1104
  14.3 0.0 collective-permute-done.2.low_ref
  14.3 0.0 collective-permute-done.3.high_ref
  14.3 1.2 %shard_map.256 = (f32[2,8,8,256]{3,2,1,0:T(8,128)S(1)}, f32[1088,128]{1,0:T(8,128)S(1)}) custom-call(f32[3,8,8,256]{3,2,1,0:T(8,128)S(1)} %pad_maximum_fusion.held_ref, f32[5,8,256]{2,1,0:T(8,128)S(1)} %collective-permute-done.before_ref, f32[5,8,256]{2,1,0:T(8,128)S(1)} %collective-permute-done.1.after_ref, ...), custom_call_target="tpu_custom_call" | custom-call | flops 6553600 | bytes 1310720 | tf_op jit(solution)/shard_map/pallas_call | solution.py:1132
  15.5 22.6 %all_to_all.32 = f32[544,2,128]{2,1,0:T(2,128)S(1)} all-to-all(f32[544,2,128]{2,1,0:T(2,128)S(1)} %bitcast.22), channel_id=1, replica_groups=mesh['gx'=4,'gy'=8] {'gx','gy'}, dimensions={0} | all-to-all | bytes 1114112 | tf_op jit(solution)/shard_map/all_to_all | solution.py:1057
  38.1 0.0 copy-done.5
  38.1 0.0 copy-done.6
  38.1 0.0 copy-done.8
  38.1 0.0 copy-done.10
  38.1 2.4 %shard_map.257 = (f32[32,128]{1,0:T(8,128)S(1)}, f32[1024,128]{1,0:T(8,128)S(1)}, bf16[8,256,128]{2,1,0:T(8,128)(2,1)S(1)}, bf16[8,32,256]{2,1,0:T(8,128)(2,1)S(1)}) custom-call(f32[1088,128]{1,0:T(8,128)S(1)} %bitcast.19, bf16[64,384]{1,0:T(8,128)(2,1)S(1)} %copy-done.8, bf16[384,128]{1,0:T(8,128)(2,1)S(1)} %copy-done.2, bf16[128,192]{1,0:T(8,128)(2,1)S(1)} %copy-done.6, ...), custom_call_target="tpu_custom_call" | custom-call | flops 100000000 | bytes 2000000 | tf_op jit(solution)/shard_map/pallas_call | solution.py:1140
  40.6 18.4 %all_to_all.33 = f32[32,32,128]{2,1,0:T(8,128)S(1)} all-to-all(f32[32,32,128]{2,1,0:T(8,128)S(1)} %bitcast.23), channel_id=1, replica_groups=mesh['gx'=4,'gy'=8] {'gx','gy'}, dimensions={0} | all-to-all | bytes 1048576 | tf_op jit(solution)/shard_map/all_to_all | solution.py:1057
  59.0 3.1 %shard_map.258 = (f32[64,256]{1,0:T(8,128)S(1)}, f32[1024,128]{1,0:T(8,128)S(1)}) custom-call(f32[1024,128]{1,0:T(8,128)S(1)} %bitcast.24, bf16[8,256,128]{2,1,0:T(8,128)(2,1)S(1)} %get-tuple-element.42.table_ref, bf16[64,256]{1,0:T(8,128)(2,1)S(1)} %get-tuple-element.43.mix_ref, f32[8,256,256]{2,1,0:T(8,128)S(1)} %get-tuple-element.44.weight_ref, ...), custom_call_target="tpu_custom_call" | custom-call | flops 1000000000 | bytes 2000000 | tf_op jit(solution)/shard_map/pallas_call | solution.py:1168
  62.1 18.4 %all_to_all.34 = f32[32,32,128]{2,1,0:T(8,128)S(1)} all-to-all(f32[32,32,128]{2,1,0:T(8,128)S(1)} %bitcast.25), channel_id=1, replica_groups=mesh['gx'=4,'gy'=8] {'gx','gy'}, dimensions={0} | all-to-all | bytes 1048576 | tf_op jit(solution)/shard_map/all_to_all | solution.py:1057
  80.6 0.0 copy-done.9
  80.6 0.9 shard_map.259
  81.5 13.5 %all_to_all.35 = f32[288,2,128]{2,1,0:T(2,128)S(1)} all-to-all(f32[288,2,128]{2,1,0:T(2,128)S(1)} %bitcast.21), channel_id=1, replica_groups=mesh['gx'=4,'gy'=8] {'gx','gy'}, dimensions={0} | all-to-all | bytes 589824 | tf_op jit(solution)/shard_map/all_to_all | solution.py:1057
  95.0 4.1 %shard_map.260 = (f32[32,32]{1,0:T(8,128)}, f32[1,32]{1,0:T(1,128)}, f32[64,256]{1,0:T(8,128)}, f32[8,8,256]{2,1,0:T(8,128)}, f32[8,8,256]{2,1,0:T(8,128)}, /*index=5*/f32[2,8,4,32,1024]{4,3,2,1,0:T(8,128)}) custom-call(f32[576,128]{1,0:T(8,128)S(1)} %bitcast.26, f32[2,32]{1,0:T(2,128)S(1)} %bitcast.29, f32[64,256]{1,0:T(8,128)S(1)} %get-tuple-element.49.predicted_ref, ...), custom_call_target="tpu_custom_call" | custom-call | flops 1073741824 | bytes 8388608 | tf_op jit(solution)/shard_map/pallas_call | solution.py:1188
  (14 shorter events, 0.1 us)
Async XLA Ops:
  1.6 9.8 %slice-start = ((s8[8388608]{0:T(1024)(128)(4,1)}), s8[4194304]{0:T(1024)(128)(4,1)S(1)}, s32[]{:S(2)}) async-start(s8[8388608]{0:T(1024)(128)(4,1)} %bitcast.17), calls=%async_computation.4 | async-start | bytes 8388608
  1.6 9.8 %slice-start.1 = ((s8[8388608]{0:T(1024)(128)(4,1)}), s8[4194304]{0:T(1024)(128)(4,1)S(1)}, s32[]{:S(2)}) async-start(s8[8388608]{0:T(1024)(128)(4,1)} %bitcast.17), calls=%async_computation.5 | async-start | bytes 8388608
  1.6 9.8 %copy-start.4 = (f32[8,8,256]{2,1,0:T(8,128)S(1)}, f32[8,8,256]{2,1,0:T(8,128)}, u32[]{:S(2)}) copy-start(f32[8,8,256]{2,1,0:T(8,128)} %param.30) | copy-start | bytes 196612
  1.6 9.8 %copy-start.11 = (f32[32,32]{1,0:T(8,128)S(1)}, f32[32,32]{1,0:T(8,128)}, u32[]{:S(2)}) copy-start(f32[32,32]{1,0:T(8,128)} %local_ref.1) | copy-start | bytes 12292
  1.6 9.8 %copy-start.12 = (f32[32,2]{0,1:T(2,128)S(1)}, f32[32,2]{0,1:T(2,128)}, u32[]{:S(2)}) copy-start(f32[32,2]{0,1:T(2,128)} %param.25) | copy-start | bytes 772
  1.6 9.8 %copy-start.13 = (f32[32]{0:T(128)S(1)}, f32[32]{0:T(128)}, u32[]{:S(2)}) copy-start(f32[32]{0:T(128)} %param.28) | copy-start | bytes 388
  1.6 9.8 %copy-start.14 = (f32[32]{0:T(128)S(1)}, f32[32]{0:T(128)}, u32[]{:S(2)}) copy-start(f32[32]{0:T(128)} %param.29) | copy-start | bytes 388
  1.7 4.1 %collective-permute-start = (f32[5,8,256]{2,1,0:T(8,128)S(1)}, f32[5,8,256]{2,1,0:T(8,128)S(1)}, u32[]{:S(2)}, u32[]{:S(2)}) collective-permute-start(f32[5,8,256]{2,1,0:T(8,128)S(1)} %get-tuple-element.33), channel_id=1, source_target_pairs={{0,8},{8,16},{16,24},{24,0},{1,9},{9,17},{17,25},{25,1},{2,10},{10... | collective-permute-start | bytes 122888 | tf_op jit(solution)/shard_map/ppermute | solution.py:1098
  2.2 3.9 %collective-permute-start.1 = (f32[5,8,256]{2,1,0:T(8,128)S(1)}, f32[5,8,256]{2,1,0:T(8,128)S(1)}, u32[]{:S(2)}, u32[]{:S(2)}) collective-permute-start(f32[5,8,256]{2,1,0:T(8,128)S(1)} %get-tuple-element.34), channel_id=1, source_target_pairs={{0,24},{8,0},{16,8},{24,16},{1,25},{9,1},{17,9},{25,17},{2,26},{10... | collective-permute-start | bytes 122888 | tf_op jit(solution)/shard_map/ppermute | solution.py:1098
  6.1 8.2 %copy-start.3 = (bf16[64,768]{1,0:T(8,128)(2,1)S(1)}, bf16[64,768]{1,0:T(8,128)(2,1)}, u32[]{:S(2)}) copy-start(bf16[64,768]{1,0:T(8,128)(2,1)} %constant.26.clone.table_ref) | copy-start | bytes 294916
  6.1 32.0 %copy-start = (bf16[512,128]{1,0:T(8,128)(2,1)S(1)}, bf16[512,128]{1,0:T(8,128)(2,1)}, u32[]{:S(2)}) copy-start(bf16[512,128]{1,0:T(8,128)(2,1)} %constant.33.clone.gather_ref) | copy-start | bytes 393220
  6.1 32.0 %copy-start.1 = (bf16[256,256]{1,0:T(8,128)(2,1)S(1)}, bf16[256,256]{1,0:T(8,128)(2,1)}, u32[]{:S(2)}) copy-start(bf16[256,256]{1,0:T(8,128)(2,1)} %constant.32.clone.chosen_ref) | copy-start | bytes 393220
  6.1 32.0 %copy-start.2 = (bf16[384,128]{1,0:T(8,128)(2,1)S(1)}, bf16[384,128]{1,0:T(8,128)(2,1)}, u32[]{:S(2)}) copy-start(bf16[384,128]{1,0:T(8,128)(2,1)} %constant.28.clone.x_in_ref) | copy-start | bytes 294916
  6.2 31.9 %copy-start.5 = (bf16[128,256]{1,0:T(8,128)(2,1)S(1)}, bf16[128,256]{1,0:T(8,128)(2,1)}, u32[]{:S(2)}) copy-start(bf16[128,256]{1,0:T(8,128)(2,1)} %constant.31.clone.forth_ref) | copy-start | bytes 196612
  6.2 31.9 %copy-start.6 = (bf16[128,192]{1,0:T(8,128)(2,1)S(1)}, bf16[128,192]{1,0:T(8,128)(2,1)}, u32[]{:S(2)}) copy-start(bf16[128,192]{1,0:T(8,128)(2,1)} %constant.29.clone.y_out_ref) | copy-start | bytes 147460
  6.2 31.9 %copy-start.8 = (bf16[64,384]{1,0:T(8,128)(2,1)S(1)}, bf16[64,384]{1,0:T(8,128)(2,1)}, u32[]{:S(2)}) copy-start(bf16[64,384]{1,0:T(8,128)(2,1)} %constant.27.clone.y_in_ref) | copy-start | bytes 147460
  6.2 31.9 %copy-start.10 = (bf16[64,192]{1,0:T(8,128)(2,1)S(1)}, bf16[64,192]{1,0:T(8,128)(2,1)}, u32[]{:S(2)}) copy-start(bf16[64,192]{1,0:T(8,128)(2,1)} %constant.30.clone.x_out_ref) | copy-start | bytes 73732
  6.2 52.8 %copy-start.17 = (bf16[256,128]{1,0:T(8,128)(2,1)S(1)}, bf16[256,128]{1,0:T(8,128)(2,1)}, u32[]{:S(2)}) copy-start(bf16[256,128]{1,0:T(8,128)(2,1)} %constant.34.clone.back_ref) | copy-start | bytes 196612
  6.2 8.0 %collective-permute-start.2 = (f32[6,8,256]{2,1,0:T(8,128)S(1)}, f32[6,8,256]{2,1,0:T(8,128)S(1)}, u32[]{:S(2)}, u32[]{:S(2)}) collective-permute-start(f32[6,8,256]{2,1,0:T(8,128)S(1)} %get-tuple-element.35), channel_id=1, source_target_pairs={{0,1},{1,2},{2,3},{3,4},{4,5},{5,6},{6,7},{7,0},{8,9},{9,10},{10,1... | collective-permute-start | bytes 147464 | tf_op jit(solution)/shard_map/ppermute | solution.py:1098
  8.3 6.0 %collective-permute-start.3 = (f32[6,8,256]{2,1,0:T(8,128)S(1)}, f32[6,8,256]{2,1,0:T(8,128)S(1)}, u32[]{:S(2)}, u32[]{:S(2)}) collective-permute-start(f32[6,8,256]{2,1,0:T(8,128)S(1)} %get-tuple-element.36), channel_id=1, source_target_pairs={{0,7},{1,0},{2,1},{3,2},{4,3},{5,4},{6,5},{7,6},{8,15},{9,8},{10,9... | collective-permute-start | bytes 147464 | tf_op jit(solution)/shard_map/ppermute | solution.py:1098
  11.4 69.1 %copy-start.7 = (bf16[64,384]{1,0:T(8,128)(2,1)S(1)}, bf16[64,384]{1,0:T(8,128)(2,1)}, u32[]{:S(2)}) copy-start(bf16[64,384]{1,0:T(8,128)(2,1)} %constant.36.clone.y_in_ref) | copy-start | bytes 147460
  11.5 69.1 %copy-start.9 = (bf16[64,192]{1,0:T(8,128)(2,1)S(1)}, bf16[64,192]{1,0:T(8,128)(2,1)}, u32[]{:S(2)}) copy-start(bf16[64,192]{1,0:T(8,128)(2,1)} %constant.35.clone.x_in_ref) | copy-start | bytes 73732
  11.5 83.5 %copy-start.15 = (bf16[256,512]{1,0:T(8,128)(2,1)S(1)}, bf16[256,512]{1,0:T(8,128)(2,1)}, u32[]{:S(2)}) copy-start(bf16[256,512]{1,0:T(8,128)(2,1)} %constant.37.clone.repeat_ref) | copy-start | bytes 786436
  11.5 83.5 %copy-start.16 = (bf16[256,256]{1,0:T(8,128)(2,1)S(1)}, bf16[256,256]{1,0:T(8,128)(2,1)}, u32[]{:S(2)}) copy-start(bf16[256,256]{1,0:T(8,128)(2,1)} %constant.38.clone.spread_ref) | copy-start | bytes 393220

commit v5 on v4

--- a/solution.py
+++ b/solution.py
@@ -363,6 +363,8 @@
     vector_ref,
     mix_ref,
     spread_ref,
+    outer_ref,
+    wide_ref,
 ):
     _, own_x, own_y, modes_z, width = weight_ref.shape
     chunk = out_ref.shape[0] // modes_z
@@ -418,6 +420,19 @@
         mix_ref,
         spread_ref,
     )
+    for index in range(SPREAD):
+        wide_ref[:, index * WIDTH : (index + 1) * WIDTH] = lift_ref[...]
+    for index in range(1, width // LANES):
+        wide_ref[:, index * LANES : (index + 1) * LANES] = wide_ref[:, 0:LANES]
+    shape = (2 * WIDTH, width)
+    row = lax.broadcasted_iota(jnp.int32, shape, 0)
+    column = lax.broadcasted_iota(jnp.int32, shape, 1)
+    lift = jnp.where(row < WIDTH, wide_ref[0:1, :], wide_ref[1:2, :])
+    head, rest = parts_of(jnp.where(column // WIDTH == row % WIDTH, lift, 0.0))
+    outer_ref[0 : 2 * WIDTH] = head
+    outer_ref[2 * WIDTH : 4 * WIDTH] = head
+    outer_ref[4 * WIDTH : 6 * WIDTH] = rest
+    outer_ref[6 * WIDTH : 8 * WIDTH] = jnp.zeros_like(rest)
 
 
 def edge_kernel(held_ref, head_ref, tail_ref):
@@ -480,6 +495,8 @@
         cool_ext[plane + 2, base - 1 : base] = low_ref[4, line]
         cool_ext[plane + 2, end : end + 1] = high_ref[4, line]
 
+    send_ref[...] = mixed_ref[...]
+
     def sweep(reach):
         diff_ext[...] = diffusivity(phase_ext[...])
 
@@ -537,7 +554,6 @@
         )
     ordered = jnp.concatenate(ordered, axis=1)
     spectra = mul_rows(table_ref[...], thrice(ordered, 1))
-    send_ref[...] = mixed_ref[...]
     modes_z = spectra.shape[0] // 2
     chunk = send_ref.shape[0] // modes_z
     for part in range(2):
@@ -610,6 +626,7 @@
             block = jnp.where(lane // narrow == index, piece, block)
         blocks.append(block)
     along_y = mul(y_in_ref[...], thrice(jnp.concatenate(blocks, axis=0), 0))
+    prepare(fields_ref, forth_ref, table_ref, line_ref)
     half = lax.broadcasted_iota(jnp.int32, (modes_y, LANES), 1) < LANES // 2
     joined = jnp.where(half, along_y[0:modes_y], turn(along_y[modes_y:], LANES // 2))
     modes = mul(thrice(joined, 1), x_in_ref[...])
@@ -621,65 +638,75 @@
     )
     columns = mul(jnp.concatenate(parts_of(chosen), axis=1), chosen_ref[...])
     low = lax.broadcasted_iota(jnp.int32, (modes_y, LANES), 1) < 2 * WIDTH
-    products = [[], []]
-    for quad in range(quads_x):
-        lines = [[], []]
-        for index in range(SPREAD):
-            freq = SPREAD * quad + index
-            start = (freq // own_x) * count_y * own_y * own_x + freq % own_x
-            weights = weight_ref[pl.ds(start, modes_y, stride=own_x), :]
+    def gathered(quads):
+        products = [[], []]
+        for quad in quads:
+            lines = [[], []]
+            for index in range(SPREAD):
+                freq = SPREAD * quad + index
+                start = (freq // own_x) * count_y * own_y * own_x + freq % own_x
+                weights = weight_ref[pl.ds(start, modes_y, stride=own_x), :]
+                for part in range(2):
+                    column = columns[
+                        freq * modes_y : (freq + 1) * modes_y, part * LANES : (part + 1) * LANES
+                    ]
+                    line = weights * column
+                    lines[part].append(line + turn(line, 2 * WIDTH))
             for part in range(2):
-                column = columns[
-                    freq * modes_y : (freq + 1) * modes_y, part * LANES : (part + 1) * LANES
+                pairs = [
+                    jnp.where(low, lines[part][index], lines[part][index + 1])
+                    for index in range(0, SPREAD, 2)
                 ]
-                line = weights * column
-                lines[part].append(line + turn(line, 2 * WIDTH))
-        for part in range(2):
-            pairs = [
-                jnp.where(low, lines[part][index], lines[part][index + 1])
-                for index in range(0, SPREAD, 2)
-            ]
-            products[part].append(jnp.concatenate(pairs, axis=1))
-    products = jnp.concatenate(products[0] + products[1], axis=0)
-    products = mul(jnp.concatenate(parts_of(products), axis=1), gather_ref[...])
-    stacked = [
-        jnp.concatenate(
-            [
-                products[(part * quads_x + quad) * modes_y : (part * quads_x + quad + 1) * modes_y]
-                for part in range(2)
-            ],
-            axis=0,
-        )
-        for quad in range(quads_x)
-    ]
-    back = mul(y_out_ref[...], thrice(jnp.concatenate(stacked, axis=1), 0))
-    for quad in range(quads_x):
-        lines_y[quad] = back[:, quad * LANES : (quad + 1) * LANES]
-    for quad in range(quads_x):
-        for part in range(2):
-            pieces = [
-                lines_y[quad, pl.ds(part * total_y + i, quads_y, stride=SPREAD), :]
-                for i in range(SPREAD)
-            ]
-            for index, piece in enumerate(swap_groups(pieces)):
-                place = part * modes_x + SPREAD * quad + index
-                lines_x[pl.ds(place, quads_y, stride=2 * modes_x), :] = piece
+                products[part].append(jnp.concatenate(pairs, axis=1))
+        products = jnp.concatenate(products[0] + products[1], axis=0)
+        products = mul(jnp.concatenate(parts_of(products), axis=1), gather_ref[...])
+        stacked = []
+        for index in range(len(quads)):
+            places = [(part * len(quads) + index) * modes_y for part in range(2)]
+            stacked.append(
+                jnp.concatenate([products[place : place + modes_y] for place in places], axis=0)
+            )
+        return thrice(jnp.concatenate(stacked, axis=1), 0)
+
+    def along_lines(quads, stacked):
+        back = mul(y_out_ref[...], stacked)
+        for index, quad in enumerate(quads):
+            lines_y[quad] = back[:, index * LANES : (index + 1) * LANES]
+        for quad in quads:
+            for part in range(2):
+                pieces = [
+                    lines_y[quad, pl.ds(part * total_y + i, quads_y, stride=SPREAD), :]
+                    for i in range(SPREAD)
+                ]
+                for index, piece in enumerate(swap_groups(pieces)):
+                    place = part * modes_x + SPREAD * quad + index
+                    lines_x[pl.ds(place, quads_y, stride=2 * modes_x), :] = piece
+
+    batches = [range(first, first + 2) for first in range(0, quads_x, 2)]
+    following = gathered(batches[0])
+    for index, quads in enumerate(batches):
+        stacked = following
+        if index + 1 < len(batches):
+            following = gathered(batches[index + 1])
+        along_lines(quads, stacked)
     per_tile = cells_y // SPREAD
-    blocks = [
-        lines_x[quad * 2 * modes_x : (quad + 1) * 2 * modes_x, :] for quad in range(quads_y)
-    ]
-    back = mul(x_out_ref[...], thrice(jnp.concatenate(blocks, axis=1), 0))
-    for quad in range(quads_y):
-        for part in range(2):
-            for index in range(count_x):
-                device = index * count_y + quad // per_tile
-                place = (device * 2 + part) * per_tile + quad % per_tile
-                first = part * total_x + index * cells_x
-                send_ref[place * cells_x : (place + 1) * cells_x, :] = back[
-                    first : first + cells_x, quad * LANES : (quad + 1) * LANES
-                ]
+    for start in range(0, quads_y, 4):
+        blocks = [
+            lines_x[quad * 2 * modes_x : (quad + 1) * 2 * modes_x, :]
+            for quad in range(start, start + 4)
+        ]
+        back = mul(x_out_ref[...], thrice(jnp.concatenate(blocks, axis=1), 0))
+        for quad in range(start, start + 4):
+            lanes = slice((quad - start) * LANES, (quad - start + 1) * LANES)
+            for part in range(2):
+                for index in range(count_x):
+                    device = index * count_y + quad // per_tile
+                    place = (device * 2 + part) * per_tile + quad % per_tile
+                    first = part * total_x + index * cells_x
+                    send_ref[place * cells_x : (place + 1) * cells_x, :] = back[
+                        first : first + cells_x, lanes
+                    ]
     pack_modes(shape, modes, modes_ref, rows_ref)
-    prepare(fields_ref, forth_ref, table_ref, line_ref)
 
 
 def prepare(fields_ref, forth_ref, table_ref, line_ref):
@@ -751,7 +778,7 @@
     )
     line_sums = jnp.zeros((2 * cells_y, wide), jnp.float32)
     proj_sums = jnp.zeros((8, wide), jnp.float32)
-    for plane in range(planes):
+    def back(plane):
         spectra = jnp.concatenate(
             [
                 field_ref[pl.ds(part * planes + plane, rows, stride=stride), :]
@@ -760,26 +787,30 @@
             axis=1,
         )
         spectra = jnp.concatenate([thrice(spectra, 0), mix_ref[...]], axis=0)
-        back = jnp.concatenate([back_ref[...], table_ref[plane]], axis=1)
-        pre = mul(back, spectra) + bias
+        table = jnp.concatenate([back_ref[...], table_ref[plane]], axis=1)
+        return mul(table, spectra) + bias
+
+    def activate(pre, plane):
         square = pre * pre
         bent = jnp.tanh(pre * (root + (root * curve) * square))
         upper = 0.5 + 0.5 * bent
         active = pre * upper
         slope = upper + (active - active * bent) * (root + (3.0 * root * curve) * square)
         cotangent = weight_ref[plane]
-        weighted = proj * cotangent
-        grad = weighted * slope
-        share = mul_rows(
-            picker, jnp.concatenate(parts_of(fold_channels(proj * active)), axis=1)
+        grad = proj * cotangent * slope
+        sums = jnp.sum((active * cotangent).reshape(depth // 8, 8, wide), axis=0)
+        return sums, parts_of(fold_channels(proj * active)), parts_of(grad)
+
+    def forth(shared, grad, plane):
+        shares_ref[plane, :, 0 : depth // SPREAD] = mul_rows(
+            picker, jnp.concatenate(shared, axis=1)
         )
-        shares_ref[plane, :, 0 : depth // SPREAD] = share
         for index in range(SPREAD):
             predicted_ref[
                 plane * cells_y : (plane + 1) * cells_y,
                 index * (depth // SPREAD) : (index + 1) * (depth // SPREAD),
             ] = shares_ref[plane, pl.ds(index, cells_y, stride=SPREAD), 0 : depth // SPREAD]
-        head, rest = parts_of(grad)
+        head, rest = grad
         lines = line_ref[plane]
         top = jnp.concatenate([forth_ref[0:rows], lines[0 : 2 * cells_y]], axis=0)
         low = jnp.concatenate([forth_ref[rows:], lines[2 * cells_y :]], axis=0)
@@ -789,10 +820,20 @@
             send_ref[pl.ds(part * planes + plane, rows, stride=stride), :] = spectra[
                 0:rows, part * LANES : (part + 1) * LANES
             ]
-        line_sums = line_sums + spectra[rows:]
-        proj_sums = proj_sums + jnp.sum(
-            (active * cotangent).reshape(depth // 8, 8, wide), axis=0
-        )
+        return spectra[rows:]
+
+    following = back(0)
+    previous = None
+    for plane in range(planes + 1):
+        pre = following
+        if plane + 1 < planes:
+            following = back(plane + 1)
+        if plane < planes:
+            sums, *current = activate(pre, plane)
+            proj_sums = proj_sums + sums
+        if plane > 0:
+            line_sums = line_sums + forth(*previous, plane - 1)
+        previous = current
     shape = (cells_y, wide)
     own = lax.broadcasted_iota(jnp.int32, shape, 0) == (
         lax.broadcasted_iota(jnp.int32, shape, 1) // WIDTH
@@ -819,46 +860,26 @@
     chunk = 2 * per_tile * cells_x
     first_device = (lax.axis_index("gx") == 0) & (lax.axis_index("gy") == 0)
     keep = jnp.where(first_device, 0.0, 1.0)
-    blocks = []
-    for quad in range(quads_y):
-        block = []
-        for part in range(2):
-            for index in range(count_x):
-                device = index * count_y + quad // per_tile
-                place = (device * 2 + part) * per_tile + quad % per_tile
-                piece = spectra_ref[place * cells_x : (place + 1) * cells_x, :]
-                block.append(piece * keep if part else piece)
-        blocks.append(jnp.concatenate(block, axis=0))
-    forth = mul(x_in_ref[...], thrice(jnp.concatenate(blocks, axis=1), 0))
-    for quad in range(quads_y):
-        lines_x[quad * 2 * modes_x : (quad + 1) * 2 * modes_x, :] = forth[
-            :, quad * LANES : (quad + 1) * LANES
-        ]
     devices = count_x * count_y
     out_chunk = send_ref.shape[0] // devices
     per_own = own_x // SPREAD
     quads_x = modes_x // SPREAD
-    for quad in range(quads_x):
-        for part in range(2):
-            pieces = [
-                lines_x[
-                    pl.ds(part * modes_x + SPREAD * quad + j, quads_y, stride=2 * modes_x), :
-                ]
-                for j in range(SPREAD)
+    for start in range(0, quads_y, SPREAD):
+        blocks = []
+        for quad in range(start, start + SPREAD):
+            block = []
+            for part in range(2):
+                for index in range(count_x):
+                    device = index * count_y + quad // per_tile
+                    place = (device * 2 + part) * per_tile + quad % per_tile
+                    piece = spectra_ref[place * cells_x : (place + 1) * cells_x, :]
+                    block.append(piece * keep if part else piece)
+            blocks.append(jnp.concatenate(block, axis=0))
+        forth = mul(x_in_ref[...], thrice(jnp.concatenate(blocks, axis=1), 0))
+        for quad in range(start, start + SPREAD):
+            lines_x[quad * 2 * modes_x : (quad + 1) * 2 * modes_x, :] = forth[
+                :, (quad - start) * LANES : (quad - start + 1) * LANES
             ]
-            for index, piece in enumerate(swap_groups(pieces)):
-                lines_y[quad, pl.ds(part * total_y + index, quads_y, stride=SPREAD), :] = piece
-    lines = jnp.concatenate([lines_y[quad] for quad in range(quads_x)], axis=1)
-    modes = mul(y_in_ref[...], thrice(lines, 0))
-    for quad in range(quads_x):
-        for part in range(2):
-            for index in range(count_y):
-                device = (quad // per_own) * count_y + index
-                place = device * out_chunk + (part * per_own + quad % per_own) * own_y
-                first = part * modes_y + index * own_y
-                send_ref[place : place + own_y, :] = modes[
-                    first : first + own_y, quad * LANES : (quad + 1) * LANES
-                ]
     extra = 2 * per_own * own_y
     send_ref[pl.ds(extra, devices, stride=out_chunk), :] = modes_ref[...]
     groups = group_of((1, LANES))
@@ -873,6 +894,28 @@
     send_ref[pl.ds(extra + 1, devices, stride=out_chunk), :] = jnp.broadcast_to(
         total, (devices, LANES)
     )
+    for start in range(0, quads_x, 2):
+        for quad in range(start, start + 2):
+            for part in range(2):
+                pieces = [
+                    lines_x[
+                        pl.ds(part * modes_x + SPREAD * quad + j, quads_y, stride=2 * modes_x), :
+                    ]
+                    for j in range(SPREAD)
+                ]
+                for index, piece in enumerate(swap_groups(pieces)):
+                    lines_y[quad, pl.ds(part * total_y + index, quads_y, stride=SPREAD), :] = piece
+        lines = jnp.concatenate([lines_y[start], lines_y[start + 1]], axis=1)
+        modes = mul(y_in_ref[...], thrice(lines, 0))
+        for quad in range(start, start + 2):
+            for part in range(2):
+                for index in range(count_y):
+                    device = (quad // per_own) * count_y + index
+                    place = device * out_chunk + (part * per_own + quad % per_own) * own_y
+                    first = part * modes_y + index * own_y
+                    send_ref[place : place + own_y, :] = modes[
+                        first : first + own_y, (quad - start) * LANES : (quad - start + 1) * LANES
+                    ]
 
 
 def outer_kernel(
@@ -881,6 +924,7 @@
     narrow_ref,
     predicted_ref,
     fields_ref,
+    mix_ref,
     repeat_ref,
     spread_ref,
     local_out,
@@ -889,10 +933,8 @@
     phase_out,
     solute_out,
     grad_ref,
-    mix_ref,
     local_ref,
     proj_ref,
-    lift_ref,
     held,
     sent,
 ):
@@ -907,19 +949,6 @@
     ]
     for copy in copies:
         copy.start()
-    for index in range(SPREAD):
-        lift_ref[:, index * WIDTH : (index + 1) * WIDTH] = narrow_ref[...]
-    for index in range(1, width // LANES):
-        lift_ref[:, index * LANES : (index + 1) * LANES] = lift_ref[:, 0:LANES]
-    shape = (2 * WIDTH, width)
-    row = lax.broadcasted_iota(jnp.int32, shape, 0)
-    column = lax.broadcasted_iota(jnp.int32, shape, 1)
-    lift = jnp.where(row < WIDTH, lift_ref[0:1, :], lift_ref[1:2, :])
-    head, rest = parts_of(jnp.where(column // WIDTH == row % WIDTH, lift, 0.0))
-    mix_ref[0 : 2 * WIDTH] = head
-    mix_ref[2 * WIDTH : 4 * WIDTH] = head
-    mix_ref[4 * WIDTH : 6 * WIDTH] = rest
-    mix_ref[6 * WIDTH : 8 * WIDTH] = jnp.zeros_like(rest)
     lane = lax.broadcasted_iota(jnp.int32, (modes_z, LANES), 1)
     low = lane < 2 * WIDTH
 
@@ -928,29 +957,20 @@
         both = jnp.where(low, head.astype(jnp.float32), rest.astype(jnp.float32)).astype(NARROW)
         return jnp.concatenate([both, head], axis=1)
 
-    line = modes_ref[extra + 1 : extra + 2, :]
-    square = (WIDTH, WIDTH)
-    diagonal = lax.broadcasted_iota(jnp.int32, square, 0) == lax.broadcasted_iota(
-        jnp.int32, square, 1
-    )
-    local = jnp.zeros(square, jnp.float32)
-    for k in range(2):
-        sums = jnp.broadcast_to(line[:, k * WIDTH : (k + 1) * WIDTH], square)
-        sums = jnp.sum(jnp.where(diagonal, sums, 0.0), axis=1, keepdims=True)
-        local = local + sums * narrow_ref[k : k + 1, :]
-    local_ref[...] = scale * local
-    proj_ref[...] = scale * line[:, 2 * WIDTH : 3 * WIDTH]
-    copies.append(pltpu.make_async_copy(local_ref, local_out, sent.at[own_x + 3]))
-    copies.append(pltpu.make_async_copy(proj_ref, proj_out, sent.at[own_x + 4]))
-    copies[3].start()
-    copies[4].start()
-    grads = jnp.concatenate(
-        [modes_ref[pl.ds(place, modes_z, stride=chunk), :] for place in range(extra)], axis=0
-    )
-    grads = mul(jnp.concatenate(parts_of(grads), axis=1), repeat_ref[...])
+    def repeated(half):
+        grads = [
+            modes_ref[pl.ds((part * per_own + half) * own_y + row, modes_z, stride=chunk), :]
+            for part in range(2)
+            for row in range(own_y)
+        ]
+        grads = jnp.concatenate(grads, axis=0)
+        return mul(jnp.concatenate(parts_of(grads), axis=1), repeat_ref[...])
+
     modes = modes_ref[pl.ds(extra, modes_z, stride=chunk), :]
     own = lane // (4 * own_x) * own_x + lane % own_x
     for plane in range(own_x):
+        if plane % SPREAD == 0:
+            grads = repeated(plane // SPREAD)
         chosen = jnp.concatenate(
             [jnp.where(own == row * own_x + plane, modes, 0.0) for row in range(own_y)], axis=0
         )
@@ -961,7 +981,7 @@
             imag = columns[row * modes_z : (row + 1) * modes_z, LANES:]
             pair = []
             for part in range(2):
-                first = ((part * per_own + plane // SPREAD) * own_y + row) * modes_z
+                first = (part * own_y + row) * modes_z
                 group = plane % SPREAD * LANES
                 pair.append(grads[first : first + modes_z, group : group + LANES])
             reals.append(rows_of(pair[0] * real + pair[1] * imag))
@@ -972,6 +992,22 @@
             pltpu.make_async_copy(held.at[:, plane], grad_ref.at[:, plane], sent.at[plane])
         )
         copies[-1].start()
+    line = modes_ref[extra + 1 : extra + 2, :]
+    square = (WIDTH, WIDTH)
+    diagonal = lax.broadcasted_iota(jnp.int32, square, 0) == lax.broadcasted_iota(
+        jnp.int32, square, 1
+    )
+    local = jnp.zeros(square, jnp.float32)
+    for k in range(2):
+        sums = jnp.broadcast_to(line[:, k * WIDTH : (k + 1) * WIDTH], square)
+        sums = jnp.sum(jnp.where(diagonal, sums, 0.0), axis=1, keepdims=True)
+        local = local + sums * narrow_ref[k : k + 1, :]
+    local_ref[...] = scale * local
+    proj_ref[...] = scale * line[:, 2 * WIDTH : 3 * WIDTH]
+    copies.append(pltpu.make_async_copy(local_ref, local_out, sent.at[own_x + 3]))
+    copies.append(pltpu.make_async_copy(proj_ref, proj_out, sent.at[own_x + 4]))
+    copies[-2].start()
+    copies[-1].start()
     for copy in copies:
         copy.wait()
 
@@ -1101,15 +1137,16 @@
     before, after = ring(tail, "gx", 1), ring(head, "gx", -1)
     planes = 2
     spread_shape = (cells_x, depth, cells_y * WIDTH)
-    mixed_weights, vectors, mixing, weight = call(
+    mixed_weights, vectors, mixing, weight, outer_mix = call(
         functools.partial(contract_kernel, planes),
         (
             like(modes_z * (own_x * own_y + 2), LANES),
             like(4, cells_y * WIDTH),
             jax.ShapeDtypeStruct((8 * cells_y, cells_y * WIDTH), NARROW),
             like(*spread_shape),
+            jax.ShapeDtypeStruct((8 * WIDTH, width), NARROW),
         ),
-        [],
+        [pltpu.VMEM((2, width), real)],
         weight_bytes * LANES,
         weight_bytes,
     )(
@@ -1196,17 +1233,15 @@
             like(*spectral_weight.shape),
         ),
         [
-            pltpu.VMEM((8 * WIDTH, width), NARROW),
             pltpu.VMEM((WIDTH, WIDTH), real),
             pltpu.VMEM((1, WIDTH), real),
-            pltpu.VMEM((2, width), real),
             pltpu.VMEM(spectral_weight.shape, real),
             pltpu.SemaphoreType.DMA((own_x + 5,)),
         ],
         weight_bytes * 4 * WIDTH,
         weight_bytes,
         out_specs=(far,) * 6,
-    )(gradients, lift, predicted, stepped, table["repeat"], table["spread"])
+    )(gradients, lift, predicted, stepped, outer_mix, table["repeat"], table["spread"])
     return (
         phase_next,
         solute_next,

time: 99.3 us -> 98.2 us (0.989)
  Pallas kernels: 14.6 us -> 13.4 us
where the time goes in v5:
time: 98.2 us; the launch traced here: 97.9 us
  blocking collectives  72.9 us (74%)
  Pallas kernels  13.4 us (14%)
  starting transfers between devices  7.7 us (8%)
  waiting for transfers between devices  1.88 us (2%)
    all_to_all x4, blocking collectives, exchange(): lax.all_to_all(values, ('gx', 'gy'), split_axis=0, concat_axis=0, tiled=T...  72.9 us
    ppermute x4, starting transfers between devices, ring(): lax.ppermute(values, axis, [(i, (i + step) % count) for i in range(count)])  7.7 us
    pallas_call x1, Pallas kernels, per_device_fast(): call(functools.partial(outer_kernel, 1.0 / math.sqrt(total_x * total_y *...  3.92 us
    pallas_call x1, Pallas kernels, per_device_fast(): call(functools.partial(contract_kernel, planes), (like(modes_z * (own_x *...  2.76 us
    pallas_call x1, Pallas kernels, per_device_fast(): call(functools.partial(field_kernel, cells_y), (like(tile, depth), like(*...  2.66 us
  transfers between devices with their start and end apart: 4, of which 2 were waited for; matrix products, arithmetic and copies ran while one was open for 0% of the time, Pallas kernels for 3%

profile of v5, /device:TPU:0, one launch (start us, length us, event | category | flops | bytes accessed | tf_op | source)
XLA Modules:
  0.0 97.9 jit_solution(5620861281131242767)
XLA Ops:
  0.6 0.9 pad_maximum_fusion.held_ref
  1.6 0.0 slice-start
  1.6 0.0 slice-start.1
  1.6 0.0 copy-start.4
  1.6 0.0 copy-start.11
  1.6 0.0 copy-start.12
  1.6 0.0 copy-start.13
  1.6 0.0 copy-start.14
  1.7 0.5 collective-permute-start
  2.2 2.0 %collective-permute-start.1 = (f32[5,8,256]{2,1,0:T(8,128)S(1)}, f32[5,8,256]{2,1,0:T(8,128)S(1)}, u32[]{:S(2)}, u32[]{:S(2)}) collective-permute-start(f32[5,8,256]{2,1,0:T(8,128)S(1)} %get-tuple-element.35), channel_id=1, source_target_pairs={{0,24},{8,0},{16,8},{24,16},{1,25},{9,1},{17,9},{25,17},{2,26},{10... | collective-permute-start | bytes 122888 | tf_op jit(solution)/shard_map/ppermute | solution.py:1134
  4.2 1.6 %collective-permute-done.before_ref = f32[5,8,256]{2,1,0:T(8,128)S(1)} collective-permute-done((f32[5,8,256]{2,1,0:T(8,128)S(1)}, f32[5,8,256]{2,1,0:T(8,128)S(1)}, u32[]{:S(2)}, u32[]{:S(2)}) %collective-permute-start) | collective-permute-done | bytes 40992 | tf_op jit(solution)/shard_map/ppermute | solution.py:1134
  5.8 0.3 collective-permute-done.1.after_ref
  6.1 0.0 copy-start.3
  6.1 0.0 copy-start
  6.1 0.0 copy-start.1
  6.1 0.0 copy-start.2
  6.2 0.0 copy-start.5
  6.2 0.0 copy-start.6
  6.2 0.0 copy-start.8
  6.2 0.0 copy-start.10
  6.2 0.0 copy-start.17
  6.2 2.1 %collective-permute-start.2 = (f32[6,8,256]{2,1,0:T(8,128)S(1)}, f32[6,8,256]{2,1,0:T(8,128)S(1)}, u32[]{:S(2)}, u32[]{:S(2)}) collective-permute-start(f32[6,8,256]{2,1,0:T(8,128)S(1)} %get-tuple-element.36), channel_id=1, source_target_pairs={{0,1},{1,2},{2,3},{3,4},{4,5},{5,6},{6,7},{7,0},{8,9},{9,10},{10,1... | collective-permute-start | bytes 147464 | tf_op jit(solution)/shard_map/ppermute | solution.py:1134
  8.3 3.1 %collective-permute-start.3 = (f32[6,8,256]{2,1,0:T(8,128)S(1)}, f32[6,8,256]{2,1,0:T(8,128)S(1)}, u32[]{:S(2)}, u32[]{:S(2)}) collective-permute-start(f32[6,8,256]{2,1,0:T(8,128)S(1)} %get-tuple-element.37), channel_id=1, source_target_pairs={{0,7},{1,0},{2,1},{3,2},{4,3},{5,4},{6,5},{7,6},{8,15},{9,8},{10,9... | collective-permute-start | bytes 147464 | tf_op jit(solution)/shard_map/ppermute | solution.py:1134
  11.4 0.0 slice-done
  11.4 0.0 slice-done.1
  11.4 0.0 copy-done.4
  11.4 0.0 copy-done.11
  11.4 0.0 copy-done.12
  11.4 0.0 copy-done.13
  11.4 0.0 copy-done.14
  11.4 0.0 copy-start.7
  11.5 0.0 copy-start.9
  11.5 0.0 copy-start.15
  11.5 0.0 copy-start.16
  11.5 2.8 %shard_map.255 = (f32[1088,128]{1,0:T(8,128)S(1)}, f32[4,256]{1,0:T(4,128)S(1)}, bf16[64,256]{1,0:T(8,128)(2,1)S(1)}, f32[8,256,256]{2,1,0:T(8,128)S(1)}, bf16[256,1024]{1,0:T(8,128)(2,1)S(1)}) custom-call(f32[2,32]{1,0:T(2,128)S(1)} %bitcast.28, f32[2,8,4,32,1024]{4,3,2,1,0:T(8,128)S(1)} %bitcast.18, f32[32,32]{1,0:T(8,128)S(1)} %copy-done.11, ...), custom_call_target="tpu_custom_call" | custom-call | flops 1073741824 | bytes 8388608 | tf_op jit(solution)/shard_map/pallas_call | solution.py:1140
  14.3 0.0 collective-permute-done.2.low_ref
  14.3 0.0 collective-permute-done.3.high_ref
  14.3 1.2 %shard_map.256 = (f32[2,8,8,256]{3,2,1,0:T(8,128)S(1)}, f32[1088,128]{1,0:T(8,128)S(1)}) custom-call(f32[3,8,8,256]{3,2,1,0:T(8,128)S(1)} %pad_maximum_fusion.held_ref, f32[5,8,256]{2,1,0:T(8,128)S(1)} %collective-permute-done.before_ref, f32[5,8,256]{2,1,0:T(8,128)S(1)} %collective-permute-done.1.after_ref, ...), custom_call_target="tpu_custom_call" | custom-call | flops 6553600 | bytes 1310720 | tf_op jit(solution)/shard_map/pallas_call | solution.py:1169
  15.5 22.6 %all_to_all.32 = f32[544,2,128]{2,1,0:T(2,128)S(1)} all-to-all(f32[544,2,128]{2,1,0:T(2,128)S(1)} %bitcast.22), channel_id=1, replica_groups=mesh['gx'=4,'gy'=8] {'gx','gy'}, dimensions={0} | all-to-all | bytes 1114112 | tf_op jit(solution)/shard_map/all_to_all | solution.py:1093
  38.1 0.0 copy-done.1
  38.1 1.9 %shard_map.257 = (f32[32,128]{1,0:T(8,128)S(1)}, f32[1024,128]{1,0:T(8,128)S(1)}, bf16[8,256,128]{2,1,0:T(8,128)(2,1)S(1)}, bf16[8,32,256]{2,1,0:T(8,128)(2,1)S(1)}) custom-call(f32[1088,128]{1,0:T(8,128)S(1)} %bitcast.19, bf16[64,384]{1,0:T(8,128)(2,1)S(1)} %copy-done.8, bf16[384,128]{1,0:T(8,128)(2,1)S(1)} %copy-done.2, bf16[128,192]{1,0:T(8,128)(2,1)S(1)} %copy-done.6, ...), custom_call_target="tpu_custom_call" | custom-call | flops 100000000 | bytes 2000000 | tf_op jit(solution)/shard_map/pallas_call | solution.py:1177
  40.0 18.4 %all_to_all.33 = f32[32,32,128]{2,1,0:T(8,128)S(1)} all-to-all(f32[32,32,128]{2,1,0:T(8,128)S(1)} %bitcast.23), channel_id=1, replica_groups=mesh['gx'=4,'gy'=8] {'gx','gy'}, dimensions={0} | all-to-all | bytes 1048576 | tf_op jit(solution)/shard_map/all_to_all | solution.py:1093
  58.4 2.7 %shard_map.258 = (f32[64,256]{1,0:T(8,128)S(1)}, f32[1024,128]{1,0:T(8,128)S(1)}) custom-call(f32[1024,128]{1,0:T(8,128)S(1)} %bitcast.24, bf16[8,256,128]{2,1,0:T(8,128)(2,1)S(1)} %get-tuple-element.43.table_ref, bf16[64,256]{1,0:T(8,128)(2,1)S(1)} %get-tuple-element.44.mix_ref, f32[8,256,256]{2,1,0:T(8,128)S(1)} %get-tuple-element.45.weight_ref, ...), custom_call_target="tpu_custom_call" | custom-call | flops 1000000000 | bytes 2000000 | tf_op jit(solution)/shard_map/pallas_call | solution.py:1205
  61.1 18.4 %all_to_all.34 = f32[32,32,128]{2,1,0:T(8,128)S(1)} all-to-all(f32[32,32,128]{2,1,0:T(8,128)S(1)} %bitcast.25), channel_id=1, replica_groups=mesh['gx'=4,'gy'=8] {'gx','gy'}, dimensions={0} | all-to-all | bytes 1048576 | tf_op jit(solution)/shard_map/all_to_all | solution.py:1093
  79.5 0.9 shard_map.259
  80.5 13.5 %all_to_all.35 = f32[288,2,128]{2,1,0:T(2,128)S(1)} all-to-all(f32[288,2,128]{2,1,0:T(2,128)S(1)} %bitcast.21), channel_id=1, replica_groups=mesh['gx'=4,'gy'=8] {'gx','gy'}, dimensions={0} | all-to-all | bytes 589824 | tf_op jit(solution)/shard_map/all_to_all | solution.py:1093
  94.0 0.0 copy-done.16
  94.0 3.9 %shard_map.260 = (f32[32,32]{1,0:T(8,128)}, f32[1,32]{1,0:T(1,128)}, f32[64,256]{1,0:T(8,128)}, f32[8,8,256]{2,1,0:T(8,128)}, f32[8,8,256]{2,1,0:T(8,128)}, /*index=5*/f32[2,8,4,32,1024]{4,3,2,1,0:T(8,128)}) custom-call(f32[576,128]{1,0:T(8,128)S(1)} %bitcast.26, f32[2,32]{1,0:T(2,128)S(1)} %bitcast.29, f32[64,256]{1,0:T(8,128)S(1)} %get-tuple-element.50.predicted_ref, ...), custom_call_target="tpu_custom_call" | custom-call | flops 1073741824 | bytes 8388608 | tf_op jit(solution)/shard_map/pallas_call | solution.py:1225
  (14 shorter events, 0.1 us)
Async XLA Ops:
  1.6 9.8 %slice-start = ((s8[8388608]{0:T(1024)(128)(4,1)}), s8[4194304]{0:T(1024)(128)(4,1)S(1)}, s32[]{:S(2)}) async-start(s8[8388608]{0:T(1024)(128)(4,1)} %bitcast.17), calls=%async_computation.4 | async-start | bytes 8388608
  1.6 9.8 %slice-start.1 = ((s8[8388608]{0:T(1024)(128)(4,1)}), s8[4194304]{0:T(1024)(128)(4,1)S(1)}, s32[]{:S(2)}) async-start(s8[8388608]{0:T(1024)(128)(4,1)} %bitcast.17), calls=%async_computation.5 | async-start | bytes 8388608
  1.6 9.8 %copy-start.4 = (f32[8,8,256]{2,1,0:T(8,128)S(1)}, f32[8,8,256]{2,1,0:T(8,128)}, u32[]{:S(2)}) copy-start(f32[8,8,256]{2,1,0:T(8,128)} %param.30) | copy-start | bytes 196612
  1.6 9.8 %copy-start.11 = (f32[32,32]{1,0:T(8,128)S(1)}, f32[32,32]{1,0:T(8,128)}, u32[]{:S(2)}) copy-start(f32[32,32]{1,0:T(8,128)} %local_ref.1) | copy-start | bytes 12292
  1.6 9.8 %copy-start.12 = (f32[32,2]{0,1:T(2,128)S(1)}, f32[32,2]{0,1:T(2,128)}, u32[]{:S(2)}) copy-start(f32[32,2]{0,1:T(2,128)} %param.25) | copy-start | bytes 772
  1.6 9.8 %copy-start.13 = (f32[32]{0:T(128)S(1)}, f32[32]{0:T(128)}, u32[]{:S(2)}) copy-start(f32[32]{0:T(128)} %param.28) | copy-start | bytes 388
  1.6 9.8 %copy-start.14 = (f32[32]{0:T(128)S(1)}, f32[32]{0:T(128)}, u32[]{:S(2)}) copy-start(f32[32]{0:T(128)} %param.29) | copy-start | bytes 388
  1.7 4.1 %collective-permute-start = (f32[5,8,256]{2,1,0:T(8,128)S(1)}, f32[5,8,256]{2,1,0:T(8,128)S(1)}, u32[]{:S(2)}, u32[]{:S(2)}) collective-permute-start(f32[5,8,256]{2,1,0:T(8,128)S(1)} %get-tuple-element.34), channel_id=1, source_target_pairs={{0,8},{8,16},{16,24},{24,0},{1,9},{9,17},{17,25},{25,1},{2,10},{10... | collective-permute-start | bytes 122888 | tf_op jit(solution)/shard_map/ppermute | solution.py:1134
  2.2 3.9 %collective-permute-start.1 = (f32[5,8,256]{2,1,0:T(8,128)S(1)}, f32[5,8,256]{2,1,0:T(8,128)S(1)}, u32[]{:S(2)}, u32[]{:S(2)}) collective-permute-start(f32[5,8,256]{2,1,0:T(8,128)S(1)} %get-tuple-element.35), channel_id=1, source_target_pairs={{0,24},{8,0},{16,8},{24,16},{1,25},{9,1},{17,9},{25,17},{2,26},{10... | collective-permute-start | bytes 122888 | tf_op jit(solution)/shard_map/ppermute | solution.py:1134
  6.1 8.2 %copy-start.3 = (bf16[64,768]{1,0:T(8,128)(2,1)S(1)}, bf16[64,768]{1,0:T(8,128)(2,1)}, u32[]{:S(2)}) copy-start(bf16[64,768]{1,0:T(8,128)(2,1)} %constant.26.clone.table_ref) | copy-start | bytes 294916
  6.1 32.0 %copy-start = (bf16[512,128]{1,0:T(8,128)(2,1)S(1)}, bf16[512,128]{1,0:T(8,128)(2,1)}, u32[]{:S(2)}) copy-start(bf16[512,128]{1,0:T(8,128)(2,1)} %constant.33.clone.gather_ref) | copy-start | bytes 393220
  6.1 32.0 %copy-start.1 = (bf16[256,256]{1,0:T(8,128)(2,1)S(1)}, bf16[256,256]{1,0:T(8,128)(2,1)}, u32[]{:S(2)}) copy-start(bf16[256,256]{1,0:T(8,128)(2,1)} %constant.32.clone.chosen_ref) | copy-start | bytes 393220
  6.1 32.0 %copy-start.2 = (bf16[384,128]{1,0:T(8,128)(2,1)S(1)}, bf16[384,128]{1,0:T(8,128)(2,1)}, u32[]{:S(2)}) copy-start(bf16[384,128]{1,0:T(8,128)(2,1)} %constant.28.clone.x_in_ref) | copy-start | bytes 294916
  6.2 31.9 %copy-start.5 = (bf16[128,256]{1,0:T(8,128)(2,1)S(1)}, bf16[128,256]{1,0:T(8,128)(2,1)}, u32[]{:S(2)}) copy-start(bf16[128,256]{1,0:T(8,128)(2,1)} %constant.31.clone.forth_ref) | copy-start | bytes 196612
  6.2 31.9 %copy-start.6 = (bf16[128,192]{1,0:T(8,128)(2,1)S(1)}, bf16[128,192]{1,0:T(8,128)(2,1)}, u32[]{:S(2)}) copy-start(bf16[128,192]{1,0:T(8,128)(2,1)} %constant.29.clone.y_out_ref) | copy-start | bytes 147460
  6.2 31.9 %copy-start.8 = (bf16[64,384]{1,0:T(8,128)(2,1)S(1)}, bf16[64,384]{1,0:T(8,128)(2,1)}, u32[]{:S(2)}) copy-start(bf16[64,384]{1,0:T(8,128)(2,1)} %constant.27.clone.y_in_ref) | copy-start | bytes 147460
  6.2 31.9 %copy-start.10 = (bf16[64,192]{1,0:T(8,128)(2,1)S(1)}, bf16[64,192]{1,0:T(8,128)(2,1)}, u32[]{:S(2)}) copy-start(bf16[64,192]{1,0:T(8,128)(2,1)} %constant.30.clone.x_out_ref) | copy-start | bytes 73732
  6.2 52.2 %copy-start.17 = (bf16[256,128]{1,0:T(8,128)(2,1)S(1)}, bf16[256,128]{1,0:T(8,128)(2,1)}, u32[]{:S(2)}) copy-start(bf16[256,128]{1,0:T(8,128)(2,1)} %constant.34.clone.back_ref) | copy-start | bytes 196612
  6.2 8.0 %collective-permute-start.2 = (f32[6,8,256]{2,1,0:T(8,128)S(1)}, f32[6,8,256]{2,1,0:T(8,128)S(1)}, u32[]{:S(2)}, u32[]{:S(2)}) collective-permute-start(f32[6,8,256]{2,1,0:T(8,128)S(1)} %get-tuple-element.36), channel_id=1, source_target_pairs={{0,1},{1,2},{2,3},{3,4},{4,5},{5,6},{6,7},{7,0},{8,9},{9,10},{10,1... | collective-permute-start | bytes 147464 | tf_op jit(solution)/shard_map/ppermute | solution.py:1134
  8.3 6.0 %collective-permute-start.3 = (f32[6,8,256]{2,1,0:T(8,128)S(1)}, f32[6,8,256]{2,1,0:T(8,128)S(1)}, u32[]{:S(2)}, u32[]{:S(2)}) collective-permute-start(f32[6,8,256]{2,1,0:T(8,128)S(1)} %get-tuple-element.37), channel_id=1, source_target_pairs={{0,7},{1,0},{2,1},{3,2},{4,3},{5,4},{6,5},{7,6},{8,15},{9,8},{10,9... | collective-permute-start | bytes 147464 | tf_op jit(solution)/shard_map/ppermute | solution.py:1134
  11.4 68.1 %copy-start.7 = (bf16[64,384]{1,0:T(8,128)(2,1)S(1)}, bf16[64,384]{1,0:T(8,128)(2,1)}, u32[]{:S(2)}) copy-start(bf16[64,384]{1,0:T(8,128)(2,1)} %constant.36.clone.y_in_ref) | copy-start | bytes 147460
  11.5 68.1 %copy-start.9 = (bf16[64,192]{1,0:T(8,128)(2,1)S(1)}, bf16[64,192]{1,0:T(8,128)(2,1)}, u32[]{:S(2)}) copy-start(bf16[64,192]{1,0:T(8,128)(2,1)} %constant.35.clone.x_in_ref) | copy-start | bytes 73732
  11.5 82.5 %copy-start.15 = (bf16[256,512]{1,0:T(8,128)(2,1)S(1)}, bf16[256,512]{1,0:T(8,128)(2,1)}, u32[]{:S(2)}) copy-start(bf16[256,512]{1,0:T(8,128)(2,1)} %constant.37.clone.repeat_ref) | copy-start | bytes 786436
  11.5 82.5 %copy-start.16 = (bf16[256,256]{1,0:T(8,128)(2,1)S(1)}, bf16[256,256]{1,0:T(8,128)(2,1)}, u32[]{:S(2)}) copy-start(bf16[256,256]{1,0:T(8,128)(2,1)} %constant.38.clone.spread_ref) | copy-start | bytes 393220

commit v6 on v5

--- a/solution.py
+++ b/solution.py
@@ -480,20 +480,14 @@
         ext[2 : cells_x + 2, base:end] = held_ref[index]
         ext[0:2, base:end] = before_ref[first : first + 2]
         ext[cells_x + 2 : cells_x + 4, base:end] = after_ref[first : first + 2]
-        for source, near, far in ((low_ref, base - 1, base - 2), (high_ref, end, end + 1)):
+        for source, near in ((low_ref, base - 1), (high_ref, end)):
             for plane in range(cells_x):
-                line = slice(plane, plane + 1)
-                ext[plane + 2, near : near + 1] = source[first, line]
-                ext[plane + 2, far : far + 1] = source[first + 1, line]
+                ext[plane + 2, near : near + 1] = source[first, plane : plane + 1]
             ext[1, near : near + 1] = source[5, first : first + 1]
             ext[cells_x + 2, near : near + 1] = source[5, first + 1 : first + 2]
     cool_ext[2 : cells_x + 2, base:end] = held_ref[2]
     cool_ext[1:2, base:end] = before_ref[4:5]
     cool_ext[cells_x + 2 : cells_x + 3, base:end] = after_ref[4:5]
-    for plane in range(cells_x):
-        line = slice(plane, plane + 1)
-        cool_ext[plane + 2, base - 1 : base] = low_ref[4, line]
-        cool_ext[plane + 2, end : end + 1] = high_ref[4, line]
 
     send_ref[...] = mixed_ref[...]
 
@@ -502,8 +496,7 @@
 
         def window(ext, move_x, move_y):
             return ext[
-                2 - reach + move_x : cells_x + 2 + reach + move_x,
-                base - reach + move_y : end + reach + move_y,
+                2 - reach + move_x : cells_x + 2 + reach + move_x, base + move_y : end + move_y
             ]
 
         def around(ext, now):
@@ -529,9 +522,36 @@
             around(diff_ext, diff_now),
         )
 
+    def edge(source, row, sign):
+        values, sides = [], []
+        for index in range(2):
+            near, far = source[2 * index], source[2 * index + 1]
+            inner = jnp.concatenate(
+                [held_ref[index, plane, row : row + 1] for plane in range(cells_x)], axis=0
+            )
+            before = source[5, 2 * index : 2 * index + 1]
+            after = source[5, 2 * index + 1 : 2 * index + 2]
+            values.append(near)
+            sides.append(
+                [
+                    jnp.concatenate([near[1:], after], axis=0),
+                    jnp.concatenate([before, near[:-1]], axis=0),
+                    *((inner, far) if sign < 0 else (far, inner)),
+                    pltpu.roll(near, depth - 1, 1),
+                    pltpu.roll(near, 1, 1),
+                ]
+            )
+        diffs = [diffusivity(side) for side in sides[0]]
+        return update(*values, source[4], *sides, diffusivity(values[0]), diffs)
+
     phase_mid, solute_mid = sweep(1)
-    phase_ext[1 : cells_x + 3, base - 1 : end + 1] = phase_mid
-    solute_ext[1 : cells_x + 3, base - 1 : end + 1] = solute_mid
+    edges = (edge(low_ref, 0, -1), edge(high_ref, cells_y - 1, 1))
+    phase_ext[1 : cells_x + 3, base:end] = phase_mid
+    solute_ext[1 : cells_x + 3, base:end] = solute_mid
+    for place, moved in zip((base - 1, end), edges):
+        for ext, line in zip((phase_ext, solute_ext), moved):
+            for plane in range(cells_x):
+                ext[plane + 2, place : place + 1] = line[plane : plane + 1]
     phase_next, solute_next = sweep(0)
     fields_ref[0] = phase_next
     fields_ref[1] = solute_next

time: 98.2 us -> 97.8 us (level)
  no operation moved by 1% of the time
where the time goes in v6:
time: 97.8 us; the launch traced here: 97.5 us
  blocking collectives  72.9 us (75%)
  Pallas kernels  13.1 us (13%)
  starting transfers between devices  7.7 us (8%)
  waiting for transfers between devices  1.88 us (2%)
    all_to_all x4, blocking collectives, exchange(): lax.all_to_all(values, ('gx', 'gy'), split_axis=0, concat_axis=0, tiled=T...  72.9 us
    ppermute x4, starting transfers between devices, ring(): lax.ppermute(values, axis, [(i, (i + step) % count) for i in range(count)])  7.7 us
    pallas_call x1, Pallas kernels, per_device_fast(): call(functools.partial(outer_kernel, 1.0 / math.sqrt(total_x * total_y *...  3.92 us
    pallas_call x1, Pallas kernels, per_device_fast(): call(functools.partial(contract_kernel, planes), (like(modes_z * (own_x *...  2.76 us
    pallas_call x1, Pallas kernels, per_device_fast(): call(functools.partial(field_kernel, cells_y), (like(tile, depth), like(*...  2.66 us
  transfers between devices with their start and end apart: 4, of which 2 were waited for; matrix products, arithmetic and copies ran while one was open for 0% of the time, Pallas kernels for 3%

profile of v6, /device:TPU:0, one launch (start us, length us, event | category | flops | bytes accessed | tf_op | source)
XLA Modules:
  0.0 97.5 jit_solution(18170756924493846323)
XLA Ops:
  0.6 0.9 pad_maximum_fusion.held_ref
  1.6 0.0 slice-start
  1.6 0.0 slice-start.1
  1.6 0.0 copy-start.4
  1.6 0.0 copy-start.11
  1.6 0.0 copy-start.12
  1.6 0.0 copy-start.13
  1.6 0.0 copy-start.14
  1.7 0.5 collective-permute-start
  2.2 2.0 %collective-permute-start.1 = (f32[5,8,256]{2,1,0:T(8,128)S(1)}, f32[5,8,256]{2,1,0:T(8,128)S(1)}, u32[]{:S(2)}, u32[]{:S(2)}) collective-permute-start(f32[5,8,256]{2,1,0:T(8,128)S(1)} %get-tuple-element.35), channel_id=1, source_target_pairs={{0,24},{8,0},{16,8},{24,16},{1,25},{9,1},{17,9},{25,17},{2,26},{10... | collective-permute-start | bytes 122888 | tf_op jit(solution)/shard_map/ppermute | solution.py:1154
  4.2 1.6 %collective-permute-done.before_ref = f32[5,8,256]{2,1,0:T(8,128)S(1)} collective-permute-done((f32[5,8,256]{2,1,0:T(8,128)S(1)}, f32[5,8,256]{2,1,0:T(8,128)S(1)}, u32[]{:S(2)}, u32[]{:S(2)}) %collective-permute-start) | collective-permute-done | bytes 40992 | tf_op jit(solution)/shard_map/ppermute | solution.py:1154
  5.8 0.3 collective-permute-done.1.after_ref
  6.1 0.0 copy-start.3
  6.1 0.0 copy-start
  6.1 0.0 copy-start.1
  6.1 0.0 copy-start.2
  6.2 0.0 copy-start.5
  6.2 0.0 copy-start.6
  6.2 0.0 copy-start.8
  6.2 0.0 copy-start.10
  6.2 0.0 copy-start.17
  6.2 2.1 %collective-permute-start.2 = (f32[6,8,256]{2,1,0:T(8,128)S(1)}, f32[6,8,256]{2,1,0:T(8,128)S(1)}, u32[]{:S(2)}, u32[]{:S(2)}) collective-permute-start(f32[6,8,256]{2,1,0:T(8,128)S(1)} %get-tuple-element.36), channel_id=1, source_target_pairs={{0,1},{1,2},{2,3},{3,4},{4,5},{5,6},{6,7},{7,0},{8,9},{9,10},{10,1... | collective-permute-start | bytes 147464 | tf_op jit(solution)/shard_map/ppermute | solution.py:1154
  8.3 3.1 %collective-permute-start.3 = (f32[6,8,256]{2,1,0:T(8,128)S(1)}, f32[6,8,256]{2,1,0:T(8,128)S(1)}, u32[]{:S(2)}, u32[]{:S(2)}) collective-permute-start(f32[6,8,256]{2,1,0:T(8,128)S(1)} %get-tuple-element.37), channel_id=1, source_target_pairs={{0,7},{1,0},{2,1},{3,2},{4,3},{5,4},{6,5},{7,6},{8,15},{9,8},{10,9... | collective-permute-start | bytes 147464 | tf_op jit(solution)/shard_map/ppermute | solution.py:1154
  11.4 0.0 slice-done
  11.4 0.0 slice-done.1
  11.4 0.0 copy-done.4
  11.4 0.0 copy-done.11
  11.4 0.0 copy-done.12
  11.4 0.0 copy-done.13
  11.4 0.0 copy-done.14
  11.4 0.0 copy-start.7
  11.5 0.0 copy-start.9
  11.5 0.0 copy-start.15
  11.5 0.0 copy-start.16
  11.5 2.8 %shard_map.255 = (f32[1088,128]{1,0:T(8,128)S(1)}, f32[4,256]{1,0:T(4,128)S(1)}, bf16[64,256]{1,0:T(8,128)(2,1)S(1)}, f32[8,256,256]{2,1,0:T(8,128)S(1)}, bf16[256,1024]{1,0:T(8,128)(2,1)S(1)}) custom-call(f32[2,32]{1,0:T(2,128)S(1)} %bitcast.28, f32[2,8,4,32,1024]{4,3,2,1,0:T(8,128)S(1)} %bitcast.18, f32[32,32]{1,0:T(8,128)S(1)} %copy-done.11, ...), custom_call_target="tpu_custom_call" | custom-call | flops 1073741824 | bytes 8388608 | tf_op jit(solution)/shard_map/pallas_call | solution.py:1160
  14.3 0.0 collective-permute-done.2.low_ref
  14.3 0.0 collective-permute-done.3.high_ref
  14.3 0.8 shard_map.256
  15.1 22.6 %all_to_all.32 = f32[544,2,128]{2,1,0:T(2,128)S(1)} all-to-all(f32[544,2,128]{2,1,0:T(2,128)S(1)} %bitcast.22), channel_id=1, replica_groups=mesh['gx'=4,'gy'=8] {'gx','gy'}, dimensions={0} | all-to-all | bytes 1114112 | tf_op jit(solution)/shard_map/all_to_all | solution.py:1113
  37.7 0.0 copy-done.1
  37.8 1.9 %shard_map.257 = (f32[32,128]{1,0:T(8,128)S(1)}, f32[1024,128]{1,0:T(8,128)S(1)}, bf16[8,256,128]{2,1,0:T(8,128)(2,1)S(1)}, bf16[8,32,256]{2,1,0:T(8,128)(2,1)S(1)}) custom-call(f32[1088,128]{1,0:T(8,128)S(1)} %bitcast.19, bf16[64,384]{1,0:T(8,128)(2,1)S(1)} %copy-done.8, bf16[384,128]{1,0:T(8,128)(2,1)S(1)} %copy-done.2, bf16[128,192]{1,0:T(8,128)(2,1)S(1)} %copy-done.6, ...), custom_call_target="tpu_custom_call" | custom-call | flops 100000000 | bytes 2000000 | tf_op jit(solution)/shard_map/pallas_call | solution.py:1197
  39.6 18.4 %all_to_all.33 = f32[32,32,128]{2,1,0:T(8,128)S(1)} all-to-all(f32[32,32,128]{2,1,0:T(8,128)S(1)} %bitcast.23), channel_id=1, replica_groups=mesh['gx'=4,'gy'=8] {'gx','gy'}, dimensions={0} | all-to-all | bytes 1048576 | tf_op jit(solution)/shard_map/all_to_all | solution.py:1113
  58.1 2.7 %shard_map.258 = (f32[64,256]{1,0:T(8,128)S(1)}, f32[1024,128]{1,0:T(8,128)S(1)}) custom-call(f32[1024,128]{1,0:T(8,128)S(1)} %bitcast.24, bf16[8,256,128]{2,1,0:T(8,128)(2,1)S(1)} %get-tuple-element.43.table_ref, bf16[64,256]{1,0:T(8,128)(2,1)S(1)} %get-tuple-element.44.mix_ref, f32[8,256,256]{2,1,0:T(8,128)S(1)} %get-tuple-element.45.weight_ref, ...), custom_call_target="tpu_custom_call" | custom-call | flops 1000000000 | bytes 2000000 | tf_op jit(solution)/shard_map/pallas_call | solution.py:1225
  60.7 18.4 %all_to_all.34 = f32[32,32,128]{2,1,0:T(8,128)S(1)} all-to-all(f32[32,32,128]{2,1,0:T(8,128)S(1)} %bitcast.25), channel_id=1, replica_groups=mesh['gx'=4,'gy'=8] {'gx','gy'}, dimensions={0} | all-to-all | bytes 1048576 | tf_op jit(solution)/shard_map/all_to_all | solution.py:1113
  79.1 0.9 shard_map.259
  80.1 13.5 %all_to_all.35 = f32[288,2,128]{2,1,0:T(2,128)S(1)} all-to-all(f32[288,2,128]{2,1,0:T(2,128)S(1)} %bitcast.21), channel_id=1, replica_groups=mesh['gx'=4,'gy'=8] {'gx','gy'}, dimensions={0} | all-to-all | bytes 589824 | tf_op jit(solution)/shard_map/all_to_all | solution.py:1113
  93.6 0.0 copy-done.16
  93.6 3.9 %shard_map.260 = (f32[32,32]{1,0:T(8,128)}, f32[1,32]{1,0:T(1,128)}, f32[64,256]{1,0:T(8,128)}, f32[8,8,256]{2,1,0:T(8,128)}, f32[8,8,256]{2,1,0:T(8,128)}, /*index=5*/f32[2,8,4,32,1024]{4,3,2,1,0:T(8,128)}) custom-call(f32[576,128]{1,0:T(8,128)S(1)} %bitcast.26, f32[2,32]{1,0:T(2,128)S(1)} %bitcast.29, f32[64,256]{1,0:T(8,128)S(1)} %get-tuple-element.50.predicted_ref, ...), custom_call_target="tpu_custom_call" | custom-call | flops 1073741824 | bytes 8388608 | tf_op jit(solution)/shard_map/pallas_call | solution.py:1245
  (14 shorter events, 0.1 us)
Async XLA Ops:
  1.6 9.8 %slice-start = ((s8[8388608]{0:T(1024)(128)(4,1)}), s8[4194304]{0:T(1024)(128)(4,1)S(1)}, s32[]{:S(2)}) async-start(s8[8388608]{0:T(1024)(128)(4,1)} %bitcast.17), calls=%async_computation.4 | async-start | bytes 8388608
  1.6 9.8 %slice-start.1 = ((s8[8388608]{0:T(1024)(128)(4,1)}), s8[4194304]{0:T(1024)(128)(4,1)S(1)}, s32[]{:S(2)}) async-start(s8[8388608]{0:T(1024)(128)(4,1)} %bitcast.17), calls=%async_computation.5 | async-start | bytes 8388608
  1.6 9.8 %copy-start.4 = (f32[8,8,256]{2,1,0:T(8,128)S(1)}, f32[8,8,256]{2,1,0:T(8,128)}, u32[]{:S(2)}) copy-start(f32[8,8,256]{2,1,0:T(8,128)} %param.30) | copy-start | bytes 196612
  1.6 9.8 %copy-start.11 = (f32[32,32]{1,0:T(8,128)S(1)}, f32[32,32]{1,0:T(8,128)}, u32[]{:S(2)}) copy-start(f32[32,32]{1,0:T(8,128)} %local_ref.1) | copy-start | bytes 12292
  1.6 9.8 %copy-start.12 = (f32[32,2]{0,1:T(2,128)S(1)}, f32[32,2]{0,1:T(2,128)}, u32[]{:S(2)}) copy-start(f32[32,2]{0,1:T(2,128)} %param.25) | copy-start | bytes 772
  1.6 9.8 %copy-start.13 = (f32[32]{0:T(128)S(1)}, f32[32]{0:T(128)}, u32[]{:S(2)}) copy-start(f32[32]{0:T(128)} %param.28) | copy-start | bytes 388
  1.6 9.8 %copy-start.14 = (f32[32]{0:T(128)S(1)}, f32[32]{0:T(128)}, u32[]{:S(2)}) copy-start(f32[32]{0:T(128)} %param.29) | copy-start | bytes 388
  1.7 4.1 %collective-permute-start = (f32[5,8,256]{2,1,0:T(8,128)S(1)}, f32[5,8,256]{2,1,0:T(8,128)S(1)}, u32[]{:S(2)}, u32[]{:S(2)}) collective-permute-start(f32[5,8,256]{2,1,0:T(8,128)S(1)} %get-tuple-element.34), channel_id=1, source_target_pairs={{0,8},{8,16},{16,24},{24,0},{1,9},{9,17},{17,25},{25,1},{2,10},{10... | collective-permute-start | bytes 122888 | tf_op jit(solution)/shard_map/ppermute | solution.py:1154
  2.2 3.9 %collective-permute-start.1 = (f32[5,8,256]{2,1,0:T(8,128)S(1)}, f32[5,8,256]{2,1,0:T(8,128)S(1)}, u32[]{:S(2)}, u32[]{:S(2)}) collective-permute-start(f32[5,8,256]{2,1,0:T(8,128)S(1)} %get-tuple-element.35), channel_id=1, source_target_pairs={{0,24},{8,0},{16,8},{24,16},{1,25},{9,1},{17,9},{25,17},{2,26},{10... | collective-permute-start | bytes 122888 | tf_op jit(solution)/shard_map/ppermute | solution.py:1154
  6.1 8.2 %copy-start.3 = (bf16[64,768]{1,0:T(8,128)(2,1)S(1)}, bf16[64,768]{1,0:T(8,128)(2,1)}, u32[]{:S(2)}) copy-start(bf16[64,768]{1,0:T(8,128)(2,1)} %constant.26.clone.table_ref) | copy-start | bytes 294916
  6.1 31.6 %copy-start = (bf16[512,128]{1,0:T(8,128)(2,1)S(1)}, bf16[512,128]{1,0:T(8,128)(2,1)}, u32[]{:S(2)}) copy-start(bf16[512,128]{1,0:T(8,128)(2,1)} %constant.33.clone.gather_ref) | copy-start | bytes 393220
  6.1 31.6 %copy-start.1 = (bf16[256,256]{1,0:T(8,128)(2,1)S(1)}, bf16[256,256]{1,0:T(8,128)(2,1)}, u32[]{:S(2)}) copy-start(bf16[256,256]{1,0:T(8,128)(2,1)} %constant.32.clone.chosen_ref) | copy-start | bytes 393220
  6.1 31.6 %copy-start.2 = (bf16[384,128]{1,0:T(8,128)(2,1)S(1)}, bf16[384,128]{1,0:T(8,128)(2,1)}, u32[]{:S(2)}) copy-start(bf16[384,128]{1,0:T(8,128)(2,1)} %constant.28.clone.x_in_ref) | copy-start | bytes 294916
  6.2 31.6 %copy-start.5 = (bf16[128,256]{1,0:T(8,128)(2,1)S(1)}, bf16[128,256]{1,0:T(8,128)(2,1)}, u32[]{:S(2)}) copy-start(bf16[128,256]{1,0:T(8,128)(2,1)} %constant.31.clone.forth_ref) | copy-start | bytes 196612
  6.2 31.6 %copy-start.6 = (bf16[128,192]{1,0:T(8,128)(2,1)S(1)}, bf16[128,192]{1,0:T(8,128)(2,1)}, u32[]{:S(2)}) copy-start(bf16[128,192]{1,0:T(8,128)(2,1)} %constant.29.clone.y_out_ref) | copy-start | bytes 147460
  6.2 31.6 %copy-start.8 = (bf16[64,384]{1,0:T(8,128)(2,1)S(1)}, bf16[64,384]{1,0:T(8,128)(2,1)}, u32[]{:S(2)}) copy-start(bf16[64,384]{1,0:T(8,128)(2,1)} %constant.27.clone.y_in_ref) | copy-start | bytes 147460
  6.2 31.6 %copy-start.10 = (bf16[64,192]{1,0:T(8,128)(2,1)S(1)}, bf16[64,192]{1,0:T(8,128)(2,1)}, u32[]{:S(2)}) copy-start(bf16[64,192]{1,0:T(8,128)(2,1)} %constant.30.clone.x_out_ref) | copy-start | bytes 73732
  6.2 51.9 %copy-start.17 = (bf16[256,128]{1,0:T(8,128)(2,1)S(1)}, bf16[256,128]{1,0:T(8,128)(2,1)}, u32[]{:S(2)}) copy-start(bf16[256,128]{1,0:T(8,128)(2,1)} %constant.34.clone.back_ref) | copy-start | bytes 196612
  6.2 8.0 %collective-permute-start.2 = (f32[6,8,256]{2,1,0:T(8,128)S(1)}, f32[6,8,256]{2,1,0:T(8,128)S(1)}, u32[]{:S(2)}, u32[]{:S(2)}) collective-permute-start(f32[6,8,256]{2,1,0:T(8,128)S(1)} %get-tuple-element.36), channel_id=1, source_target_pairs={{0,1},{1,2},{2,3},{3,4},{4,5},{5,6},{6,7},{7,0},{8,9},{9,10},{10,1... | collective-permute-start | bytes 147464 | tf_op jit(solution)/shard_map/ppermute | solution.py:1154
  8.3 6.0 %collective-permute-start.3 = (f32[6,8,256]{2,1,0:T(8,128)S(1)}, f32[6,8,256]{2,1,0:T(8,128)S(1)}, u32[]{:S(2)}, u32[]{:S(2)}) collective-permute-start(f32[6,8,256]{2,1,0:T(8,128)S(1)} %get-tuple-element.37), channel_id=1, source_target_pairs={{0,7},{1,0},{2,1},{3,2},{4,3},{5,4},{6,5},{7,6},{8,15},{9,8},{10,9... | collective-permute-start | bytes 147464 | tf_op jit(solution)/shard_map/ppermute | solution.py:1154
  11.4 67.7 %copy-start.7 = (bf16[64,384]{1,0:T(8,128)(2,1)S(1)}, bf16[64,384]{1,0:T(8,128)(2,1)}, u32[]{:S(2)}) copy-start(bf16[64,384]{1,0:T(8,128)(2,1)} %constant.36.clone.y_in_ref) | copy-start | bytes 147460
  11.5 67.7 %copy-start.9 = (bf16[64,192]{1,0:T(8,128)(2,1)S(1)}, bf16[64,192]{1,0:T(8,128)(2,1)}, u32[]{:S(2)}) copy-start(bf16[64,192]{1,0:T(8,128)(2,1)} %constant.35.clone.x_in_ref) | copy-start | bytes 73732
  11.5 82.1 %copy-start.15 = (bf16[256,512]{1,0:T(8,128)(2,1)S(1)}, bf16[256,512]{1,0:T(8,128)(2,1)}, u32[]{:S(2)}) copy-start(bf16[256,512]{1,0:T(8,128)(2,1)} %constant.37.clone.repeat_ref) | copy-start | bytes 786436
  11.5 82.1 %copy-start.16 = (bf16[256,256]{1,0:T(8,128)(2,1)S(1)}, bf16[256,256]{1,0:T(8,128)(2,1)}, u32[]{:S(2)}) copy-start(bf16[256,256]{1,0:T(8,128)(2,1)} %constant.38.clone.spread_ref) | copy-start | bytes 393220

commit v7 on v6

--- a/solution.py
+++ b/solution.py
@@ -342,8 +342,9 @@
         return jnp.where(own, line.astype(jnp.float32), 0.0)
 
     mixing = [diagonal(part[k : k + 1]) for k in range(2) for part in (head, head, rest)]
-    blank = jnp.zeros((2 * cells_y, wide), jnp.float32)
-    mix_ref[...] = jnp.concatenate(mixing + [blank], axis=0).astype(NARROW)
+    mixing += [part[2:3].astype(jnp.float32) for part in (head, rest)]
+    mixing.append(jnp.zeros((2 * cells_y - 2, wide), jnp.float32))
+    mix_ref[...] = jnp.concatenate(mixing, axis=0).astype(NARROW)
     spread = jnp.concatenate(parts_of(cotangent_ref[...].T), axis=1)
     cell = lax.broadcasted_iota(jnp.int32, (2 * tile, wide), 0) % tile
     row = lax.broadcasted_iota(jnp.int32, (2 * tile, wide), 1) // WIDTH
@@ -735,13 +736,13 @@
     tile = planes * cells_y
     rows = forth_ref.shape[0] // 2
     fields = (fields_ref[0].reshape(tile, depth), fields_ref[1].reshape(tile, depth) - SOLUTE_MEAN)
-    blank = jnp.zeros((2 * cells_y, depth), jnp.float32)
+    ones = jnp.where(lax.broadcasted_iota(jnp.int32, (2 * cells_y, depth), 0) < 2, 1.0, 0.0)
     table = forth_ref[rows:].astype(jnp.float32)
     for plane in range(planes):
         lines = [values[plane * cells_y : (plane + 1) * cells_y] for values in fields]
         pieces = [[part.astype(jnp.float32) for part in parts_of(values)] for values in lines]
         both = [piece for head, rest in pieces for piece in (head, rest, head)]
-        both = jnp.concatenate([table] + both + [blank], axis=0)
+        both = jnp.concatenate([table] + both + [ones], axis=0)
         table_ref[plane] = both.T.astype(NARROW)
         pieces = [piece for pair in zip(*pieces) for piece in pair]
         line_ref[plane] = jnp.concatenate(pieces, axis=0).astype(NARROW)
@@ -786,8 +787,7 @@
     rows = forth_ref.shape[0] // 2
     halves_y = cells_y // SPREAD
     stride = halves_y * planes
-    bias = vector_ref[2:3, :]
-    proj = vector_ref[3:4, :]
+    proj = 0.5 * vector_ref[3:4, :]
     root = math.sqrt(2.0 / math.pi)
     curve = 0.044715
     picker = one_where(
@@ -808,16 +808,16 @@
         )
         spectra = jnp.concatenate([thrice(spectra, 0), mix_ref[...]], axis=0)
         table = jnp.concatenate([back_ref[...], table_ref[plane]], axis=1)
-        return mul(table, spectra) + bias
+        return mul(table, spectra)
 
     def activate(pre, plane):
         square = pre * pre
         bent = jnp.tanh(pre * (root + (root * curve) * square))
-        upper = 0.5 + 0.5 * bent
+        upper = 1.0 + bent
         active = pre * upper
         slope = upper + (active - active * bent) * (root + (3.0 * root * curve) * square)
         cotangent = weight_ref[plane]
-        grad = proj * cotangent * slope
+        grad = cotangent * slope
         sums = jnp.sum((active * cotangent).reshape(depth // 8, 8, wide), axis=0)
         return sums, parts_of(fold_channels(proj * active)), parts_of(grad)
 
@@ -836,6 +836,7 @@
         low = jnp.concatenate([forth_ref[rows:], lines[2 * cells_y :]], axis=0)
         spectra = mul(jnp.concatenate([top, low], axis=0), head)
         spectra = spectra[0 : rows + 2 * cells_y] + spectra[rows + 2 * cells_y :] + mul(top, rest)
+        spectra = spectra * proj
         for part in range(halves_y):
             send_ref[pl.ds(part * planes + plane, rows, stride=stride), :] = spectra[
                 0:rows, part * LANES : (part + 1) * LANES
@@ -861,7 +862,7 @@
     sums = [
         jnp.where(own, line_sums[0:cells_y], 0.0),
         jnp.where(own, line_sums[cells_y:], 0.0),
-        proj_sums,
+        0.5 * proj_sums,
     ]
     for index, values in enumerate(sums):
         line = jnp.sum(values, axis=0, keepdims=True)

time: 97.8 us -> 97.8 us (level)
  no operation moved by 1% of the time
where the time goes in v7:
time: 97.8 us; the launch traced here: 97.5 us
  blocking collectives  72.9 us (75%)
  Pallas kernels  13 us (13%)
  starting transfers between devices  7.7 us (8%)
  waiting for transfers between devices  1.88 us (2%)
    all_to_all x4, blocking collectives, exchange(): lax.all_to_all(values, ('gx', 'gy'), split_axis=0, concat_axis=0, tiled=T...  72.9 us
    ppermute x4, starting transfers between devices, ring(): lax.ppermute(values, axis, [(i, (i + step) % count) for i in range(count)])  7.7 us
    pallas_call x1, Pallas kernels, per_device_fast(): call(functools.partial(outer_kernel, 1.0 / math.sqrt(total_x * total_y *...  3.92 us
    pallas_call x1, Pallas kernels, per_device_fast(): call(functools.partial(contract_kernel, planes), (like(modes_z * (own_x *...  2.76 us
    pallas_call x1, Pallas kernels, per_device_fast(): call(functools.partial(field_kernel, cells_y), (like(tile, depth), like(*...  2.6 us
  transfers between devices with their start and end apart: 4, of which 2 were waited for; matrix products, arithmetic and copies ran while one was open for 0% of the time, Pallas kernels for 3%

profile of v7, /device:TPU:0, one launch (start us, length us, event | category | flops | bytes accessed | tf_op | source)
XLA Modules:
  0.0 97.5 jit_solution(3234899494946084422)
XLA Ops:
  0.6 0.9 pad_maximum_fusion.held_ref
  1.6 0.0 slice-start
  1.6 0.0 slice-start.1
  1.6 0.0 copy-start.4
  1.6 0.0 copy-start.11
  1.6 0.0 copy-start.12
  1.6 0.0 copy-start.13
  1.6 0.0 copy-start.14
  1.7 0.5 collective-permute-start
  2.2 2.0 %collective-permute-start.1 = (f32[5,8,256]{2,1,0:T(8,128)S(1)}, f32[5,8,256]{2,1,0:T(8,128)S(1)}, u32[]{:S(2)}, u32[]{:S(2)}) collective-permute-start(f32[5,8,256]{2,1,0:T(8,128)S(1)} %get-tuple-element.35), channel_id=1, source_target_pairs={{0,24},{8,0},{16,8},{24,16},{1,25},{9,1},{17,9},{25,17},{2,26},{10... | collective-permute-start | bytes 122888 | tf_op jit(solution)/shard_map/ppermute | solution.py:1155
  4.2 1.6 %collective-permute-done.before_ref = f32[5,8,256]{2,1,0:T(8,128)S(1)} collective-permute-done((f32[5,8,256]{2,1,0:T(8,128)S(1)}, f32[5,8,256]{2,1,0:T(8,128)S(1)}, u32[]{:S(2)}, u32[]{:S(2)}) %collective-permute-start) | collective-permute-done | bytes 40992 | tf_op jit(solution)/shard_map/ppermute | solution.py:1155
  5.8 0.3 collective-permute-done.1.after_ref
  6.1 0.0 copy-start.3
  6.1 0.0 copy-start
  6.1 0.0 copy-start.1
  6.1 0.0 copy-start.2
  6.2 0.0 copy-start.5
  6.2 0.0 copy-start.6
  6.2 0.0 copy-start.8
  6.2 0.0 copy-start.10
  6.2 0.0 copy-start.17
  6.2 2.1 %collective-permute-start.2 = (f32[6,8,256]{2,1,0:T(8,128)S(1)}, f32[6,8,256]{2,1,0:T(8,128)S(1)}, u32[]{:S(2)}, u32[]{:S(2)}) collective-permute-start(f32[6,8,256]{2,1,0:T(8,128)S(1)} %get-tuple-element.36), channel_id=1, source_target_pairs={{0,1},{1,2},{2,3},{3,4},{4,5},{5,6},{6,7},{7,0},{8,9},{9,10},{10,1... | collective-permute-start | bytes 147464 | tf_op jit(solution)/shard_map/ppermute | solution.py:1155
  8.3 3.1 %collective-permute-start.3 = (f32[6,8,256]{2,1,0:T(8,128)S(1)}, f32[6,8,256]{2,1,0:T(8,128)S(1)}, u32[]{:S(2)}, u32[]{:S(2)}) collective-permute-start(f32[6,8,256]{2,1,0:T(8,128)S(1)} %get-tuple-element.37), channel_id=1, source_target_pairs={{0,7},{1,0},{2,1},{3,2},{4,3},{5,4},{6,5},{7,6},{8,15},{9,8},{10,9... | collective-permute-start | bytes 147464 | tf_op jit(solution)/shard_map/ppermute | solution.py:1155
  11.4 0.0 slice-done
  11.4 0.0 slice-done.1
  11.4 0.0 copy-done.4
  11.4 0.0 copy-done.11
  11.4 0.0 copy-done.12
  11.4 0.0 copy-done.13
  11.4 0.0 copy-start.7
  11.5 0.0 copy-start.9
  11.5 0.0 copy-start.15
  11.5 0.0 copy-start.16
  11.5 2.8 %shard_map.255 = (f32[1088,128]{1,0:T(8,128)S(1)}, f32[4,256]{1,0:T(4,128)S(1)}, bf16[64,256]{1,0:T(8,128)(2,1)S(1)}, f32[8,256,256]{2,1,0:T(8,128)S(1)}, bf16[256,1024]{1,0:T(8,128)(2,1)S(1)}) custom-call(f32[2,32]{1,0:T(2,128)S(1)} %bitcast.28, f32[2,8,4,32,1024]{4,3,2,1,0:T(8,128)S(1)} %bitcast.18, f32[32,32]{1,0:T(8,128)S(1)} %copy-done.11, ...), custom_call_target="tpu_custom_call" | custom-call | flops 1073741824 | bytes 8388608 | tf_op jit(solution)/shard_map/pallas_call | solution.py:1161
  14.3 0.0 collective-permute-done.2.low_ref
  14.3 0.0 collective-permute-done.3.high_ref
  14.3 0.8 shard_map.256
  15.1 22.6 %all_to_all.32 = f32[544,2,128]{2,1,0:T(2,128)S(1)} all-to-all(f32[544,2,128]{2,1,0:T(2,128)S(1)} %bitcast.22), channel_id=1, replica_groups=mesh['gx'=4,'gy'=8] {'gx','gy'}, dimensions={0} | all-to-all | bytes 1114112 | tf_op jit(solution)/shard_map/all_to_all | solution.py:1114
  37.7 0.0 copy-done.1
  37.8 1.9 %shard_map.257 = (f32[32,128]{1,0:T(8,128)S(1)}, f32[1024,128]{1,0:T(8,128)S(1)}, bf16[8,256,128]{2,1,0:T(8,128)(2,1)S(1)}, bf16[8,32,256]{2,1,0:T(8,128)(2,1)S(1)}) custom-call(f32[1088,128]{1,0:T(8,128)S(1)} %bitcast.19, bf16[64,384]{1,0:T(8,128)(2,1)S(1)} %copy-done.8, bf16[384,128]{1,0:T(8,128)(2,1)S(1)} %copy-done.2, bf16[128,192]{1,0:T(8,128)(2,1)S(1)} %copy-done.6, ...), custom_call_target="tpu_custom_call" | custom-call | flops 100000000 | bytes 2000000 | tf_op jit(solution)/shard_map/pallas_call | solution.py:1198
  39.6 18.4 %all_to_all.33 = f32[32,32,128]{2,1,0:T(8,128)S(1)} all-to-all(f32[32,32,128]{2,1,0:T(8,128)S(1)} %bitcast.23), channel_id=1, replica_groups=mesh['gx'=4,'gy'=8] {'gx','gy'}, dimensions={0} | all-to-all | bytes 1048576 | tf_op jit(solution)/shard_map/all_to_all | solution.py:1114
  58.1 0.0 copy-done.17
  58.1 2.6 %shard_map.258 = (f32[64,256]{1,0:T(8,128)S(1)}, f32[1024,128]{1,0:T(8,128)S(1)}) custom-call(f32[1024,128]{1,0:T(8,128)S(1)} %bitcast.24, bf16[8,256,128]{2,1,0:T(8,128)(2,1)S(1)} %get-tuple-element.43.table_ref, bf16[64,256]{1,0:T(8,128)(2,1)S(1)} %get-tuple-element.44.mix_ref, f32[8,256,256]{2,1,0:T(8,128)S(1)} %get-tuple-element.45.weight_ref, ...), custom_call_target="tpu_custom_call" | custom-call | flops 1000000000 | bytes 2000000 | tf_op jit(solution)/shard_map/pallas_call | solution.py:1226
  60.7 18.4 %all_to_all.34 = f32[32,32,128]{2,1,0:T(8,128)S(1)} all-to-all(f32[32,32,128]{2,1,0:T(8,128)S(1)} %bitcast.25), channel_id=1, replica_groups=mesh['gx'=4,'gy'=8] {'gx','gy'}, dimensions={0} | all-to-all | bytes 1048576 | tf_op jit(solution)/shard_map/all_to_all | solution.py:1114
  79.1 0.9 shard_map.259
  80.1 13.5 %all_to_all.35 = f32[288,2,128]{2,1,0:T(2,128)S(1)} all-to-all(f32[288,2,128]{2,1,0:T(2,128)S(1)} %bitcast.21), channel_id=1, replica_groups=mesh['gx'=4,'gy'=8] {'gx','gy'}, dimensions={0} | all-to-all | bytes 589824 | tf_op jit(solution)/shard_map/all_to_all | solution.py:1114
  93.6 0.0 copy-done.16
  93.6 3.9 %shard_map.260 = (f32[32,32]{1,0:T(8,128)}, f32[1,32]{1,0:T(1,128)}, f32[64,256]{1,0:T(8,128)}, f32[8,8,256]{2,1,0:T(8,128)}, f32[8,8,256]{2,1,0:T(8,128)}, /*index=5*/f32[2,8,4,32,1024]{4,3,2,1,0:T(8,128)}) custom-call(f32[576,128]{1,0:T(8,128)S(1)} %bitcast.26, f32[2,32]{1,0:T(2,128)S(1)} %bitcast.29, f32[64,256]{1,0:T(8,128)S(1)} %get-tuple-element.50.predicted_ref, ...), custom_call_target="tpu_custom_call" | custom-call | flops 1073741824 | bytes 8388608 | tf_op jit(solution)/shard_map/pallas_call | solution.py:1246
  (14 shorter events, 0.1 us)
Async XLA Ops:
  1.6 9.8 %slice-start = ((s8[8388608]{0:T(1024)(128)(4,1)}), s8[4194304]{0:T(1024)(128)(4,1)S(1)}, s32[]{:S(2)}) async-start(s8[8388608]{0:T(1024)(128)(4,1)} %bitcast.17), calls=%async_computation.4 | async-start | bytes 8388608
  1.6 9.8 %slice-start.1 = ((s8[8388608]{0:T(1024)(128)(4,1)}), s8[4194304]{0:T(1024)(128)(4,1)S(1)}, s32[]{:S(2)}) async-start(s8[8388608]{0:T(1024)(128)(4,1)} %bitcast.17), calls=%async_computation.5 | async-start | bytes 8388608
  1.6 9.8 %copy-start.4 = (f32[8,8,256]{2,1,0:T(8,128)S(1)}, f32[8,8,256]{2,1,0:T(8,128)}, u32[]{:S(2)}) copy-start(f32[8,8,256]{2,1,0:T(8,128)} %param.30) | copy-start | bytes 196612
  1.6 9.8 %copy-start.11 = (f32[32,32]{1,0:T(8,128)S(1)}, f32[32,32]{1,0:T(8,128)}, u32[]{:S(2)}) copy-start(f32[32,32]{1,0:T(8,128)} %local_ref.1) | copy-start | bytes 12292
  1.6 9.8 %copy-start.12 = (f32[32,2]{0,1:T(2,128)S(1)}, f32[32,2]{0,1:T(2,128)}, u32[]{:S(2)}) copy-start(f32[32,2]{0,1:T(2,128)} %param.25) | copy-start | bytes 772
  1.6 9.8 %copy-start.13 = (f32[32]{0:T(128)S(1)}, f32[32]{0:T(128)}, u32[]{:S(2)}) copy-start(f32[32]{0:T(128)} %param.28) | copy-start | bytes 388
  1.6 9.8 %copy-start.14 = (f32[32]{0:T(128)S(1)}, f32[32]{0:T(128)}, u32[]{:S(2)}) copy-start(f32[32]{0:T(128)} %param.29) | copy-start | bytes 388
  1.7 4.1 %collective-permute-start = (f32[5,8,256]{2,1,0:T(8,128)S(1)}, f32[5,8,256]{2,1,0:T(8,128)S(1)}, u32[]{:S(2)}, u32[]{:S(2)}) collective-permute-start(f32[5,8,256]{2,1,0:T(8,128)S(1)} %get-tuple-element.34), channel_id=1, source_target_pairs={{0,8},{8,16},{16,24},{24,0},{1,9},{9,17},{17,25},{25,1},{2,10},{10... | collective-permute-start | bytes 122888 | tf_op jit(solution)/shard_map/ppermute | solution.py:1155
  2.2 3.9 %collective-permute-start.1 = (f32[5,8,256]{2,1,0:T(8,128)S(1)}, f32[5,8,256]{2,1,0:T(8,128)S(1)}, u32[]{:S(2)}, u32[]{:S(2)}) collective-permute-start(f32[5,8,256]{2,1,0:T(8,128)S(1)} %get-tuple-element.35), channel_id=1, source_target_pairs={{0,24},{8,0},{16,8},{24,16},{1,25},{9,1},{17,9},{25,17},{2,26},{10... | collective-permute-start | bytes 122888 | tf_op jit(solution)/shard_map/ppermute | solution.py:1155
  6.1 8.2 %copy-start.3 = (bf16[64,768]{1,0:T(8,128)(2,1)S(1)}, bf16[64,768]{1,0:T(8,128)(2,1)}, u32[]{:S(2)}) copy-start(bf16[64,768]{1,0:T(8,128)(2,1)} %constant.26.clone.table_ref) | copy-start | bytes 294916
  6.1 31.6 %copy-start = (bf16[512,128]{1,0:T(8,128)(2,1)S(1)}, bf16[512,128]{1,0:T(8,128)(2,1)}, u32[]{:S(2)}) copy-start(bf16[512,128]{1,0:T(8,128)(2,1)} %constant.33.clone.gather_ref) | copy-start | bytes 393220
  6.1 31.6 %copy-start.1 = (bf16[256,256]{1,0:T(8,128)(2,1)S(1)}, bf16[256,256]{1,0:T(8,128)(2,1)}, u32[]{:S(2)}) copy-start(bf16[256,256]{1,0:T(8,128)(2,1)} %constant.32.clone.chosen_ref) | copy-start | bytes 393220
  6.1 31.6 %copy-start.2 = (bf16[384,128]{1,0:T(8,128)(2,1)S(1)}, bf16[384,128]{1,0:T(8,128)(2,1)}, u32[]{:S(2)}) copy-start(bf16[384,128]{1,0:T(8,128)(2,1)} %constant.28.clone.x_in_ref) | copy-start | bytes 294916
  6.2 31.6 %copy-start.5 = (bf16[128,256]{1,0:T(8,128)(2,1)S(1)}, bf16[128,256]{1,0:T(8,128)(2,1)}, u32[]{:S(2)}) copy-start(bf16[128,256]{1,0:T(8,128)(2,1)} %constant.31.clone.forth_ref) | copy-start | bytes 196612
  6.2 31.6 %copy-start.6 = (bf16[128,192]{1,0:T(8,128)(2,1)S(1)}, bf16[128,192]{1,0:T(8,128)(2,1)}, u32[]{:S(2)}) copy-start(bf16[128,192]{1,0:T(8,128)(2,1)} %constant.29.clone.y_out_ref) | copy-start | bytes 147460
  6.2 31.6 %copy-start.8 = (bf16[64,384]{1,0:T(8,128)(2,1)S(1)}, bf16[64,384]{1,0:T(8,128)(2,1)}, u32[]{:S(2)}) copy-start(bf16[64,384]{1,0:T(8,128)(2,1)} %constant.27.clone.y_in_ref) | copy-start | bytes 147460
  6.2 31.6 %copy-start.10 = (bf16[64,192]{1,0:T(8,128)(2,1)S(1)}, bf16[64,192]{1,0:T(8,128)(2,1)}, u32[]{:S(2)}) copy-start(bf16[64,192]{1,0:T(8,128)(2,1)} %constant.30.clone.x_out_ref) | copy-start | bytes 73732
  6.2 51.9 %copy-start.17 = (bf16[256,128]{1,0:T(8,128)(2,1)S(1)}, bf16[256,128]{1,0:T(8,128)(2,1)}, u32[]{:S(2)}) copy-start(bf16[256,128]{1,0:T(8,128)(2,1)} %constant.34.clone.back_ref) | copy-start | bytes 196612
  6.2 8.0 %collective-permute-start.2 = (f32[6,8,256]{2,1,0:T(8,128)S(1)}, f32[6,8,256]{2,1,0:T(8,128)S(1)}, u32[]{:S(2)}, u32[]{:S(2)}) collective-permute-start(f32[6,8,256]{2,1,0:T(8,128)S(1)} %get-tuple-element.36), channel_id=1, source_target_pairs={{0,1},{1,2},{2,3},{3,4},{4,5},{5,6},{6,7},{7,0},{8,9},{9,10},{10,1... | collective-permute-start | bytes 147464 | tf_op jit(solution)/shard_map/ppermute | solution.py:1155
  8.3 6.0 %collective-permute-start.3 = (f32[6,8,256]{2,1,0:T(8,128)S(1)}, f32[6,8,256]{2,1,0:T(8,128)S(1)}, u32[]{:S(2)}, u32[]{:S(2)}) collective-permute-start(f32[6,8,256]{2,1,0:T(8,128)S(1)} %get-tuple-element.37), channel_id=1, source_target_pairs={{0,7},{1,0},{2,1},{3,2},{4,3},{5,4},{6,5},{7,6},{8,15},{9,8},{10,9... | collective-permute-start | bytes 147464 | tf_op jit(solution)/shard_map/ppermute | solution.py:1155
  11.4 67.7 %copy-start.7 = (bf16[64,384]{1,0:T(8,128)(2,1)S(1)}, bf16[64,384]{1,0:T(8,128)(2,1)}, u32[]{:S(2)}) copy-start(bf16[64,384]{1,0:T(8,128)(2,1)} %constant.36.clone.y_in_ref) | copy-start | bytes 147460
  11.5 67.7 %copy-start.9 = (bf16[64,192]{1,0:T(8,128)(2,1)S(1)}, bf16[64,192]{1,0:T(8,128)(2,1)}, u32[]{:S(2)}) copy-start(bf16[64,192]{1,0:T(8,128)(2,1)} %constant.35.clone.x_in_ref) | copy-start | bytes 73732
  11.5 82.1 %copy-start.15 = (bf16[256,512]{1,0:T(8,128)(2,1)S(1)}, bf16[256,512]{1,0:T(8,128)(2,1)}, u32[]{:S(2)}) copy-start(bf16[256,512]{1,0:T(8,128)(2,1)} %constant.37.clone.repeat_ref) | copy-start | bytes 786436
  11.5 82.1 %copy-start.16 = (bf16[256,256]{1,0:T(8,128)(2,1)S(1)}, bf16[256,256]{1,0:T(8,128)(2,1)}, u32[]{:S(2)}) copy-start(bf16[256,256]{1,0:T(8,128)(2,1)} %constant.38.clone.spread_ref) | copy-start | bytes 393220

commit v8 on v6

--- a/solution.py
+++ b/solution.py
@@ -597,7 +597,7 @@
         for row in range(1, own_y):
             piece = rows_ref[index, pl.ds(row, count_y, stride=own_y), :]
             line = jnp.where(groups == row, turn(piece, row * WIDTH), line)
-        modes_ref[index * count_y : (index + 1) * count_y] = line
+        modes_ref[pl.ds(index, count_y, stride=count_x), :] = line
 
 
 def spectral_kernel(
@@ -629,20 +629,27 @@
     devices = count_x * count_y
     own = own_x * own_y
     chunk = mixed_ref.shape[0] // devices
-    spectra = [mixed_ref[pl.ds(own + part, devices, stride=chunk), :] for part in range(2)]
-    for index in range(devices):
-        weight_ref[index * own : (index + 1) * own, :] = mixed_ref[
-            index * chunk : index * chunk + own, :
-        ]
+    for index_x in range(count_x):
+        for index_y in range(count_y):
+            place = (index_x * count_y + index_y) * own
+            start = (index_y * count_x + index_x) * chunk
+            weight_ref[place : place + own, :] = mixed_ref[start : start + own, :]
+    pieces = [
+        jnp.concatenate(
+            [
+                mixed_ref[pl.ds(index * chunk + own + part, count_y, stride=count_x * chunk), :]
+                for part in range(2)
+            ],
+            axis=0,
+        )
+        for index in range(count_x)
+    ]
     lane = lax.broadcasted_iota(jnp.int32, (rows, LANES), 1)
     blocks = []
     for row in range(cells_y):
         block = jnp.zeros((rows, LANES), jnp.float32)
         for index in range(count_x):
-            piece = jnp.concatenate(
-                [values[index * count_y : (index + 1) * count_y] for values in spectra], axis=0
-            )
-            piece = turn(piece, narrow * (index - row))
+            piece = turn(pieces[index], narrow * (index - row))
             block = jnp.where(lane // narrow == index, piece, block)
         blocks.append(block)
     along_y = mul(y_in_ref[...], thrice(jnp.concatenate(blocks, axis=0), 0))
@@ -720,7 +727,7 @@
             lanes = slice((quad - start) * LANES, (quad - start + 1) * LANES)
             for part in range(2):
                 for index in range(count_x):
-                    device = index * count_y + quad // per_tile
+                    device = quad // per_tile * count_x + index
                     place = (device * 2 + part) * per_tile + quad % per_tile
                     first = part * total_x + index * cells_x
                     send_ref[place * cells_x : (place + 1) * cells_x, :] = back[
@@ -890,7 +897,7 @@
             block = []
             for part in range(2):
                 for index in range(count_x):
-                    device = index * count_y + quad // per_tile
+                    device = quad // per_tile * count_x + index
                     place = (device * 2 + part) * per_tile + quad % per_tile
                     piece = spectra_ref[place * cells_x : (place + 1) * cells_x, :]
                     block.append(piece * keep if part else piece)
@@ -930,7 +937,7 @@
         for quad in range(start, start + 2):
             for part in range(2):
                 for index in range(count_y):
-                    device = (quad // per_own) * count_y + index
+                    device = index * count_x + quad // per_own
                     place = device * out_chunk + (part * per_own + quad % per_own) * own_y
                     first = part * modes_y + index * own_y
                     send_ref[place : place + own_y, :] = modes[
@@ -963,9 +970,9 @@
     per_own = own_x // SPREAD
     extra = 2 * per_own * own_y
     copies = [
-        pltpu.make_async_copy(predicted_ref, predicted_out, sent.at[own_x]),
-        pltpu.make_async_copy(fields_ref.at[0], phase_out, sent.at[own_x + 1]),
-        pltpu.make_async_copy(fields_ref.at[1], solute_out, sent.at[own_x + 2]),
+        pltpu.make_async_copy(predicted_ref, predicted_out, sent.at[2 * own_x]),
+        pltpu.make_async_copy(fields_ref.at[0], phase_out, sent.at[2 * own_x + 1]),
+        pltpu.make_async_copy(fields_ref.at[1], solute_out, sent.at[2 * own_x + 2]),
     ]
     for copy in copies:
         copy.start()
@@ -1006,12 +1013,15 @@
                 pair.append(grads[first : first + modes_z, group : group + LANES])
             reals.append(rows_of(pair[0] * real + pair[1] * imag))
             imags.append(rows_of(pair[1] * real - pair[0] * imag))
-        result = mul(jnp.concatenate(reals + imags, axis=0), mix_ref[...])
-        held[:, plane] = result.reshape(2, own_y, modes_z, width)
-        copies.append(
-            pltpu.make_async_copy(held.at[:, plane], grad_ref.at[:, plane], sent.at[plane])
-        )
-        copies[-1].start()
+        for part, factors in enumerate((reals, imags)):
+            result = mul(jnp.concatenate(factors, axis=0), mix_ref[...])
+            held[part, plane] = result.reshape(own_y, modes_z, width)
+            copies.append(
+                pltpu.make_async_copy(
+                    held.at[part, plane], grad_ref.at[part, plane], sent.at[2 * plane + part]
+                )
+            )
+            copies[-1].start()
     line = modes_ref[extra + 1 : extra + 2, :]
     square = (WIDTH, WIDTH)
     diagonal = lax.broadcasted_iota(jnp.int32, square, 0) == lax.broadcasted_iota(
@@ -1024,8 +1034,8 @@
         local = local + sums * narrow_ref[k : k + 1, :]
     local_ref[...] = scale * local
     proj_ref[...] = scale * line[:, 2 * WIDTH : 3 * WIDTH]
-    copies.append(pltpu.make_async_copy(local_ref, local_out, sent.at[own_x + 3]))
-    copies.append(pltpu.make_async_copy(proj_ref, proj_out, sent.at[own_x + 4]))
+    copies.append(pltpu.make_async_copy(local_ref, local_out, sent.at[2 * own_x + 3]))
+    copies.append(pltpu.make_async_copy(proj_ref, proj_out, sent.at[2 * own_x + 4]))
     copies[-2].start()
     copies[-1].start()
     for copy in copies:
@@ -1110,7 +1120,7 @@
 
 
 def exchange(values):
-    return lax.all_to_all(values, ("gx", "gy"), split_axis=0, concat_axis=0, tiled=True)
+    return lax.all_to_all(values, ("gy", "gx"), split_axis=0, concat_axis=0, tiled=True)
 
 
 def per_device_fast(
@@ -1256,7 +1266,7 @@
             pltpu.VMEM((WIDTH, WIDTH), real),
             pltpu.VMEM((1, WIDTH), real),
             pltpu.VMEM(spectral_weight.shape, real),
-            pltpu.SemaphoreType.DMA((own_x + 5,)),
+            pltpu.SemaphoreType.DMA((2 * own_x + 5,)),
         ],
         weight_bytes * 4 * WIDTH,
         weight_bytes,

time: 97.8 us -> 97.8 us (level)
  no operation moved by 1% of the time
where the time goes in v8:
time: 97.8 us; the launch traced here: 97.5 us
  blocking collectives  72.9 us (75%)
  Pallas kernels  13.1 us (13%)
  starting transfers between devices  7.7 us (8%)
  waiting for transfers between devices  1.88 us (2%)
    all_to_all x4, blocking collectives, exchange(): lax.all_to_all(values, ('gy', 'gx'), split_axis=0, concat_axis=0, tiled=T...  72.9 us
    ppermute x4, starting transfers between devices, ring(): lax.ppermute(values, axis, [(i, (i + step) % count) for i in range(count)])  7.7 us
    pallas_call x1, Pallas kernels, per_device_fast(): call(functools.partial(outer_kernel, 1.0 / math.sqrt(total_x * total_y *...  3.92 us
    pallas_call x1, Pallas kernels, per_device_fast(): call(functools.partial(contract_kernel, planes), (like(modes_z * (own_x *...  2.76 us
    pallas_call x1, Pallas kernels, per_device_fast(): call(functools.partial(field_kernel, cells_y), (like(tile, depth), like(*...  2.66 us
  transfers between devices with their start and end apart: 4, of which 2 were waited for; matrix products, arithmetic and copies ran while one was open for 0% of the time, Pallas kernels for 3%

profile of v8, /device:TPU:0, one launch (start us, length us, event | category | flops | bytes accessed | tf_op | source)
XLA Modules:
  0.0 97.5 jit_solution(2881236804469769148)
XLA Ops:
  0.6 0.9 pad_maximum_fusion.held_ref
  1.6 0.0 slice-start
  1.6 0.0 slice-start.1
  1.6 0.0 copy-start.4
  1.6 0.0 copy-start.11
  1.6 0.0 copy-start.12
  1.6 0.0 copy-start.13
  1.6 0.0 copy-start.14
  1.7 0.5 collective-permute-start
  2.2 2.0 %collective-permute-start.1 = (f32[5,8,256]{2,1,0:T(8,128)S(1)}, f32[5,8,256]{2,1,0:T(8,128)S(1)}, u32[]{:S(2)}, u32[]{:S(2)}) collective-permute-start(f32[5,8,256]{2,1,0:T(8,128)S(1)} %get-tuple-element.35), channel_id=1, source_target_pairs={{0,24},{8,0},{16,8},{24,16},{1,25},{9,1},{17,9},{25,17},{2,26},{10... | collective-permute-start | bytes 122888 | tf_op jit(solution)/shard_map/ppermute | solution.py:1164
  4.2 1.6 %collective-permute-done.before_ref = f32[5,8,256]{2,1,0:T(8,128)S(1)} collective-permute-done((f32[5,8,256]{2,1,0:T(8,128)S(1)}, f32[5,8,256]{2,1,0:T(8,128)S(1)}, u32[]{:S(2)}, u32[]{:S(2)}) %collective-permute-start) | collective-permute-done | bytes 40992 | tf_op jit(solution)/shard_map/ppermute | solution.py:1164
  5.8 0.3 collective-permute-done.1.after_ref
  6.1 0.0 copy-start.3
  6.1 0.0 copy-start
  6.1 0.0 copy-start.1
  6.1 0.0 copy-start.2
  6.2 0.0 copy-start.5
  6.2 0.0 copy-start.6
  6.2 0.0 copy-start.8
  6.2 0.0 copy-start.10
  6.2 0.0 copy-start.17
  6.2 2.1 %collective-permute-start.2 = (f32[6,8,256]{2,1,0:T(8,128)S(1)}, f32[6,8,256]{2,1,0:T(8,128)S(1)}, u32[]{:S(2)}, u32[]{:S(2)}) collective-permute-start(f32[6,8,256]{2,1,0:T(8,128)S(1)} %get-tuple-element.36), channel_id=1, source_target_pairs={{0,1},{1,2},{2,3},{3,4},{4,5},{5,6},{6,7},{7,0},{8,9},{9,10},{10,1... | collective-permute-start | bytes 147464 | tf_op jit(solution)/shard_map/ppermute | solution.py:1164
  8.3 3.1 %collective-permute-start.3 = (f32[6,8,256]{2,1,0:T(8,128)S(1)}, f32[6,8,256]{2,1,0:T(8,128)S(1)}, u32[]{:S(2)}, u32[]{:S(2)}) collective-permute-start(f32[6,8,256]{2,1,0:T(8,128)S(1)} %get-tuple-element.37), channel_id=1, source_target_pairs={{0,7},{1,0},{2,1},{3,2},{4,3},{5,4},{6,5},{7,6},{8,15},{9,8},{10,9... | collective-permute-start | bytes 147464 | tf_op jit(solution)/shard_map/ppermute | solution.py:1164
  11.4 0.0 slice-done
  11.4 0.0 slice-done.1
  11.4 0.0 copy-done.4
  11.4 0.0 copy-done.11
  11.4 0.0 copy-done.12
  11.4 0.0 copy-done.13
  11.4 0.0 copy-start.7
  11.5 0.0 copy-start.9
  11.5 0.0 copy-start.15
  11.5 0.0 copy-start.16
  11.5 2.8 %shard_map.255 = (f32[1088,128]{1,0:T(8,128)S(1)}, f32[4,256]{1,0:T(4,128)S(1)}, bf16[64,256]{1,0:T(8,128)(2,1)S(1)}, f32[8,256,256]{2,1,0:T(8,128)S(1)}, bf16[256,1024]{1,0:T(8,128)(2,1)S(1)}) custom-call(f32[2,32]{1,0:T(2,128)S(1)} %bitcast.28, f32[2,8,4,32,1024]{4,3,2,1,0:T(8,128)S(1)} %bitcast.18, f32[32,32]{1,0:T(8,128)S(1)} %copy-done.11, ...), custom_call_target="tpu_custom_call" | custom-call | flops 1073741824 | bytes 8388608 | tf_op jit(solution)/shard_map/pallas_call | solution.py:1170
  14.3 0.0 collective-permute-done.2.low_ref
  14.3 0.0 collective-permute-done.3.high_ref
  14.3 0.8 shard_map.256
  15.1 21.6 %all_to_all.32 = f32[544,2,128]{2,1,0:T(2,128)S(1)} all-to-all(f32[544,2,128]{2,1,0:T(2,128)S(1)} %bitcast.22), channel_id=1, replica_groups=mesh['gx'=4,'gy'=8] {'gy','gx'}, dimensions={0} | all-to-all | bytes 1114112 | tf_op jit(solution)/shard_map/all_to_all | solution.py:1123
  36.8 0.0 copy-done
  36.8 1.9 %shard_map.257 = (f32[32,128]{1,0:T(8,128)S(1)}, f32[1024,128]{1,0:T(8,128)S(1)}, bf16[8,256,128]{2,1,0:T(8,128)(2,1)S(1)}, bf16[8,32,256]{2,1,0:T(8,128)(2,1)S(1)}) custom-call(f32[1088,128]{1,0:T(8,128)S(1)} %bitcast.19, bf16[64,384]{1,0:T(8,128)(2,1)S(1)} %copy-done.8, bf16[384,128]{1,0:T(8,128)(2,1)S(1)} %copy-done.2, bf16[128,192]{1,0:T(8,128)(2,1)S(1)} %copy-done.6, ...), custom_call_target="tpu_custom_call" | custom-call | flops 100000000 | bytes 2000000 | tf_op jit(solution)/shard_map/pallas_call | solution.py:1207
  38.7 18.5 %all_to_all.33 = f32[32,32,128]{2,1,0:T(8,128)S(1)} all-to-all(f32[32,32,128]{2,1,0:T(8,128)S(1)} %bitcast.23), channel_id=1, replica_groups=mesh['gx'=4,'gy'=8] {'gy','gx'}, dimensions={0} | all-to-all | bytes 1048576 | tf_op jit(solution)/shard_map/all_to_all | solution.py:1123
  57.3 2.7 %shard_map.258 = (f32[64,256]{1,0:T(8,128)S(1)}, f32[1024,128]{1,0:T(8,128)S(1)}) custom-call(f32[1024,128]{1,0:T(8,128)S(1)} %bitcast.24, bf16[8,256,128]{2,1,0:T(8,128)(2,1)S(1)} %get-tuple-element.43.table_ref, bf16[64,256]{1,0:T(8,128)(2,1)S(1)} %get-tuple-element.44.mix_ref, f32[8,256,256]{2,1,0:T(8,128)S(1)} %get-tuple-element.45.weight_ref, ...), custom_call_target="tpu_custom_call" | custom-call | flops 1000000000 | bytes 2000000 | tf_op jit(solution)/shard_map/pallas_call | solution.py:1235
  59.9 18.4 %all_to_all.34 = f32[32,32,128]{2,1,0:T(8,128)S(1)} all-to-all(f32[32,32,128]{2,1,0:T(8,128)S(1)} %bitcast.25), channel_id=1, replica_groups=mesh['gx'=4,'gy'=8] {'gy','gx'}, dimensions={0} | all-to-all | bytes 1048576 | tf_op jit(solution)/shard_map/all_to_all | solution.py:1123
  78.4 0.0 copy-done.7
  78.4 0.9 shard_map.259
  79.3 14.3 %all_to_all.35 = f32[288,2,128]{2,1,0:T(2,128)S(1)} all-to-all(f32[288,2,128]{2,1,0:T(2,128)S(1)} %bitcast.21), channel_id=1, replica_groups=mesh['gx'=4,'gy'=8] {'gy','gx'}, dimensions={0} | all-to-all | bytes 589824 | tf_op jit(solution)/shard_map/all_to_all | solution.py:1123
  93.6 0.0 copy-done.15
  93.6 3.9 %shard_map.260 = (f32[32,32]{1,0:T(8,128)}, f32[1,32]{1,0:T(1,128)}, f32[64,256]{1,0:T(8,128)}, f32[8,8,256]{2,1,0:T(8,128)}, f32[8,8,256]{2,1,0:T(8,128)}, /*index=5*/f32[2,8,4,32,1024]{4,3,2,1,0:T(8,128)}) custom-call(f32[576,128]{1,0:T(8,128)S(1)} %bitcast.26, f32[2,32]{1,0:T(2,128)S(1)} %bitcast.29, f32[64,256]{1,0:T(8,128)S(1)} %get-tuple-element.50.predicted_ref, ...), custom_call_target="tpu_custom_call" | custom-call | flops 1073741824 | bytes 8388608 | tf_op jit(solution)/shard_map/pallas_call | solution.py:1255
  (14 shorter events, 0.1 us)
Async XLA Ops:
  1.6 9.8 %slice-start = ((s8[8388608]{0:T(1024)(128)(4,1)}), s8[4194304]{0:T(1024)(128)(4,1)S(1)}, s32[]{:S(2)}) async-start(s8[8388608]{0:T(1024)(128)(4,1)} %bitcast.17), calls=%async_computation.4 | async-start | bytes 8388608
  1.6 9.8 %slice-start.1 = ((s8[8388608]{0:T(1024)(128)(4,1)}), s8[4194304]{0:T(1024)(128)(4,1)S(1)}, s32[]{:S(2)}) async-start(s8[8388608]{0:T(1024)(128)(4,1)} %bitcast.17), calls=%async_computation.5 | async-start | bytes 8388608
  1.6 9.8 %copy-start.4 = (f32[8,8,256]{2,1,0:T(8,128)S(1)}, f32[8,8,256]{2,1,0:T(8,128)}, u32[]{:S(2)}) copy-start(f32[8,8,256]{2,1,0:T(8,128)} %param.30) | copy-start | bytes 196612
  1.6 9.8 %copy-start.11 = (f32[32,32]{1,0:T(8,128)S(1)}, f32[32,32]{1,0:T(8,128)}, u32[]{:S(2)}) copy-start(f32[32,32]{1,0:T(8,128)} %local_ref.1) | copy-start | bytes 12292
  1.6 9.8 %copy-start.12 = (f32[32,2]{0,1:T(2,128)S(1)}, f32[32,2]{0,1:T(2,128)}, u32[]{:S(2)}) copy-start(f32[32,2]{0,1:T(2,128)} %param.25) | copy-start | bytes 772
  1.6 9.8 %copy-start.13 = (f32[32]{0:T(128)S(1)}, f32[32]{0:T(128)}, u32[]{:S(2)}) copy-start(f32[32]{0:T(128)} %param.28) | copy-start | bytes 388
  1.6 9.8 %copy-start.14 = (f32[32]{0:T(128)S(1)}, f32[32]{0:T(128)}, u32[]{:S(2)}) copy-start(f32[32]{0:T(128)} %param.29) | copy-start | bytes 388
  1.7 4.1 %collective-permute-start = (f32[5,8,256]{2,1,0:T(8,128)S(1)}, f32[5,8,256]{2,1,0:T(8,128)S(1)}, u32[]{:S(2)}, u32[]{:S(2)}) collective-permute-start(f32[5,8,256]{2,1,0:T(8,128)S(1)} %get-tuple-element.34), channel_id=1, source_target_pairs={{0,8},{8,16},{16,24},{24,0},{1,9},{9,17},{17,25},{25,1},{2,10},{10... | collective-permute-start | bytes 122888 | tf_op jit(solution)/shard_map/ppermute | solution.py:1164
  2.2 3.9 %collective-permute-start.1 = (f32[5,8,256]{2,1,0:T(8,128)S(1)}, f32[5,8,256]{2,1,0:T(8,128)S(1)}, u32[]{:S(2)}, u32[]{:S(2)}) collective-permute-start(f32[5,8,256]{2,1,0:T(8,128)S(1)} %get-tuple-element.35), channel_id=1, source_target_pairs={{0,24},{8,0},{16,8},{24,16},{1,25},{9,1},{17,9},{25,17},{2,26},{10... | collective-permute-start | bytes 122888 | tf_op jit(solution)/shard_map/ppermute | solution.py:1164
  6.1 8.2 %copy-start.3 = (bf16[64,768]{1,0:T(8,128)(2,1)S(1)}, bf16[64,768]{1,0:T(8,128)(2,1)}, u32[]{:S(2)}) copy-start(bf16[64,768]{1,0:T(8,128)(2,1)} %constant.26.clone.table_ref) | copy-start | bytes 294916
  6.1 30.7 %copy-start = (bf16[512,128]{1,0:T(8,128)(2,1)S(1)}, bf16[512,128]{1,0:T(8,128)(2,1)}, u32[]{:S(2)}) copy-start(bf16[512,128]{1,0:T(8,128)(2,1)} %constant.33.clone.gather_ref) | copy-start | bytes 393220
  6.1 30.7 %copy-start.1 = (bf16[256,256]{1,0:T(8,128)(2,1)S(1)}, bf16[256,256]{1,0:T(8,128)(2,1)}, u32[]{:S(2)}) copy-start(bf16[256,256]{1,0:T(8,128)(2,1)} %constant.32.clone.chosen_ref) | copy-start | bytes 393220
  6.1 30.7 %copy-start.2 = (bf16[384,128]{1,0:T(8,128)(2,1)S(1)}, bf16[384,128]{1,0:T(8,128)(2,1)}, u32[]{:S(2)}) copy-start(bf16[384,128]{1,0:T(8,128)(2,1)} %constant.28.clone.x_in_ref) | copy-start | bytes 294916
  6.2 30.6 %copy-start.5 = (bf16[128,256]{1,0:T(8,128)(2,1)S(1)}, bf16[128,256]{1,0:T(8,128)(2,1)}, u32[]{:S(2)}) copy-start(bf16[128,256]{1,0:T(8,128)(2,1)} %constant.31.clone.forth_ref) | copy-start | bytes 196612
  6.2 30.6 %copy-start.6 = (bf16[128,192]{1,0:T(8,128)(2,1)S(1)}, bf16[128,192]{1,0:T(8,128)(2,1)}, u32[]{:S(2)}) copy-start(bf16[128,192]{1,0:T(8,128)(2,1)} %constant.29.clone.y_out_ref) | copy-start | bytes 147460
  6.2 30.6 %copy-start.8 = (bf16[64,384]{1,0:T(8,128)(2,1)S(1)}, bf16[64,384]{1,0:T(8,128)(2,1)}, u32[]{:S(2)}) copy-start(bf16[64,384]{1,0:T(8,128)(2,1)} %constant.27.clone.y_in_ref) | copy-start | bytes 147460
  6.2 30.6 %copy-start.10 = (bf16[64,192]{1,0:T(8,128)(2,1)S(1)}, bf16[64,192]{1,0:T(8,128)(2,1)}, u32[]{:S(2)}) copy-start(bf16[64,192]{1,0:T(8,128)(2,1)} %constant.30.clone.x_out_ref) | copy-start | bytes 73732
  6.2 51.1 %copy-start.17 = (bf16[256,128]{1,0:T(8,128)(2,1)S(1)}, bf16[256,128]{1,0:T(8,128)(2,1)}, u32[]{:S(2)}) copy-start(bf16[256,128]{1,0:T(8,128)(2,1)} %constant.34.clone.back_ref) | copy-start | bytes 196612
  6.2 8.0 %collective-permute-start.2 = (f32[6,8,256]{2,1,0:T(8,128)S(1)}, f32[6,8,256]{2,1,0:T(8,128)S(1)}, u32[]{:S(2)}, u32[]{:S(2)}) collective-permute-start(f32[6,8,256]{2,1,0:T(8,128)S(1)} %get-tuple-element.36), channel_id=1, source_target_pairs={{0,1},{1,2},{2,3},{3,4},{4,5},{5,6},{6,7},{7,0},{8,9},{9,10},{10,1... | collective-permute-start | bytes 147464 | tf_op jit(solution)/shard_map/ppermute | solution.py:1164
  8.3 6.0 %collective-permute-start.3 = (f32[6,8,256]{2,1,0:T(8,128)S(1)}, f32[6,8,256]{2,1,0:T(8,128)S(1)}, u32[]{:S(2)}, u32[]{:S(2)}) collective-permute-start(f32[6,8,256]{2,1,0:T(8,128)S(1)} %get-tuple-element.37), channel_id=1, source_target_pairs={{0,7},{1,0},{2,1},{3,2},{4,3},{5,4},{6,5},{7,6},{8,15},{9,8},{10,9... | collective-permute-start | bytes 147464 | tf_op jit(solution)/shard_map/ppermute | solution.py:1164
  11.4 66.9 %copy-start.7 = (bf16[64,384]{1,0:T(8,128)(2,1)S(1)}, bf16[64,384]{1,0:T(8,128)(2,1)}, u32[]{:S(2)}) copy-start(bf16[64,384]{1,0:T(8,128)(2,1)} %constant.36.clone.y_in_ref) | copy-start | bytes 147460
  11.5 66.9 %copy-start.9 = (bf16[64,192]{1,0:T(8,128)(2,1)S(1)}, bf16[64,192]{1,0:T(8,128)(2,1)}, u32[]{:S(2)}) copy-start(bf16[64,192]{1,0:T(8,128)(2,1)} %constant.35.clone.x_in_ref) | copy-start | bytes 73732
  11.5 82.1 %copy-start.15 = (bf16[256,512]{1,0:T(8,128)(2,1)S(1)}, bf16[256,512]{1,0:T(8,128)(2,1)}, u32[]{:S(2)}) copy-start(bf16[256,512]{1,0:T(8,128)(2,1)} %constant.37.clone.repeat_ref) | copy-start | bytes 786436
  11.5 82.1 %copy-start.16 = (bf16[256,256]{1,0:T(8,128)(2,1)S(1)}, bf16[256,256]{1,0:T(8,128)(2,1)}, u32[]{:S(2)}) copy-start(bf16[256,256]{1,0:T(8,128)(2,1)} %constant.38.clone.spread_ref) | copy-start | bytes 393220

commit v9 on v7

--- a/solution.py
+++ b/solution.py
@@ -598,7 +598,7 @@
         for row in range(1, own_y):
             piece = rows_ref[index, pl.ds(row, count_y, stride=own_y), :]
             line = jnp.where(groups == row, turn(piece, row * WIDTH), line)
-        modes_ref[index * count_y : (index + 1) * count_y] = line
+        modes_ref[pl.ds(index, count_y, stride=count_x), :] = line
 
 
 def spectral_kernel(
@@ -630,20 +630,27 @@
     devices = count_x * count_y
     own = own_x * own_y
     chunk = mixed_ref.shape[0] // devices
-    spectra = [mixed_ref[pl.ds(own + part, devices, stride=chunk), :] for part in range(2)]
-    for index in range(devices):
-        weight_ref[index * own : (index + 1) * own, :] = mixed_ref[
-            index * chunk : index * chunk + own, :
-        ]
+    for index_x in range(count_x):
+        for index_y in range(count_y):
+            place = (index_x * count_y + index_y) * own
+            start = (index_y * count_x + index_x) * chunk
+            weight_ref[place : place + own, :] = mixed_ref[start : start + own, :]
+    pieces = [
+        jnp.concatenate(
+            [
+                mixed_ref[pl.ds(index * chunk + own + part, count_y, stride=count_x * chunk), :]
+                for part in range(2)
+            ],
+            axis=0,
+        )
+        for index in range(count_x)
+    ]
     lane = lax.broadcasted_iota(jnp.int32, (rows, LANES), 1)
     blocks = []
     for row in range(cells_y):
         block = jnp.zeros((rows, LANES), jnp.float32)
         for index in range(count_x):
-            piece = jnp.concatenate(
-                [values[index * count_y : (index + 1) * count_y] for values in spectra], axis=0
-            )
-            piece = turn(piece, narrow * (index - row))
+            piece = turn(pieces[index], narrow * (index - row))
             block = jnp.where(lane // narrow == index, piece, block)
         blocks.append(block)
     along_y = mul(y_in_ref[...], thrice(jnp.concatenate(blocks, axis=0), 0))
@@ -721,7 +728,7 @@
             lanes = slice((quad - start) * LANES, (quad - start + 1) * LANES)
             for part in range(2):
                 for index in range(count_x):
-                    device = index * count_y + quad // per_tile
+                    device = quad // per_tile * count_x + index
                     place = (device * 2 + part) * per_tile + quad % per_tile
                     first = part * total_x + index * cells_x
                     send_ref[place * cells_x : (place + 1) * cells_x, :] = back[
@@ -891,7 +898,7 @@
             block = []
             for part in range(2):
                 for index in range(count_x):
-                    device = index * count_y + quad // per_tile
+                    device = quad // per_tile * count_x + index
                     place = (device * 2 + part) * per_tile + quad % per_tile
                     piece = spectra_ref[place * cells_x : (place + 1) * cells_x, :]
                     block.append(piece * keep if part else piece)
@@ -931,7 +938,7 @@
         for quad in range(start, start + 2):
             for part in range(2):
                 for index in range(count_y):
-                    device = (quad // per_own) * count_y + index
+                    device = index * count_x + quad // per_own
                     place = device * out_chunk + (part * per_own + quad % per_own) * own_y
                     first = part * modes_y + index * own_y
                     send_ref[place : place + own_y, :] = modes[
@@ -1111,7 +1118,7 @@
 
 
 def exchange(values):
-    return lax.all_to_all(values, ("gx", "gy"), split_axis=0, concat_axis=0, tiled=True)
+    return lax.all_to_all(values, ("gy", "gx"), split_axis=0, concat_axis=0, tiled=True)
 
 
 def per_device_fast(

time: 97.8 us -> 97.7 us (level)
  no operation moved by 1% of the time
where the time goes in v9:
time: 97.7 us; the launch traced here: 97.5 us
  blocking collectives  72.9 us (75%)
  Pallas kernels  13 us (13%)
  starting transfers between devices  7.7 us (8%)
  waiting for transfers between devices  1.88 us (2%)
    all_to_all x4, blocking collectives, exchange(): lax.all_to_all(values, ('gy', 'gx'), split_axis=0, concat_axis=0, tiled=T...  72.9 us
    ppermute x4, starting transfers between devices, ring(): lax.ppermute(values, axis, [(i, (i + step) % count) for i in range(count)])  7.7 us
    pallas_call x1, Pallas kernels, per_device_fast(): call(functools.partial(outer_kernel, 1.0 / math.sqrt(total_x * total_y *...  3.92 us
    pallas_call x1, Pallas kernels, per_device_fast(): call(functools.partial(contract_kernel, planes), (like(modes_z * (own_x *...  2.76 us
    pallas_call x1, Pallas kernels, per_device_fast(): call(functools.partial(field_kernel, cells_y), (like(tile, depth), like(*...  2.6 us
  transfers between devices with their start and end apart: 4, of which 2 were waited for; matrix products, arithmetic and copies ran while one was open for 0% of the time, Pallas kernels for 3%

profile of v9, /device:TPU:0, one launch (start us, length us, event | category | flops | bytes accessed | tf_op | source)
XLA Modules:
  0.0 97.5 jit_solution(17605324508960849826)
XLA Ops:
  0.6 0.9 pad_maximum_fusion.held_ref
  1.6 0.0 slice-start
  1.6 0.0 slice-start.1
  1.6 0.0 copy-start.4
  1.6 0.0 copy-start.11
  1.6 0.0 copy-start.12
  1.6 0.0 copy-start.13
  1.6 0.0 copy-start.14
  1.7 0.5 collective-permute-start
  2.2 2.0 %collective-permute-start.1 = (f32[5,8,256]{2,1,0:T(8,128)S(1)}, f32[5,8,256]{2,1,0:T(8,128)S(1)}, u32[]{:S(2)}, u32[]{:S(2)}) collective-permute-start(f32[5,8,256]{2,1,0:T(8,128)S(1)} %get-tuple-element.35), channel_id=1, source_target_pairs={{0,24},{8,0},{16,8},{24,16},{1,25},{9,1},{17,9},{25,17},{2,26},{10... | collective-permute-start | bytes 122888 | tf_op jit(solution)/shard_map/ppermute | solution.py:1162
  4.2 1.6 %collective-permute-done.before_ref = f32[5,8,256]{2,1,0:T(8,128)S(1)} collective-permute-done((f32[5,8,256]{2,1,0:T(8,128)S(1)}, f32[5,8,256]{2,1,0:T(8,128)S(1)}, u32[]{:S(2)}, u32[]{:S(2)}) %collective-permute-start) | collective-permute-done | bytes 40992 | tf_op jit(solution)/shard_map/ppermute | solution.py:1162
  5.8 0.3 collective-permute-done.1.after_ref
  6.1 0.0 copy-start.3
  6.1 0.0 copy-start
  6.1 0.0 copy-start.1
  6.1 0.0 copy-start.2
  6.2 0.0 copy-start.5
  6.2 0.0 copy-start.6
  6.2 0.0 copy-start.8
  6.2 0.0 copy-start.10
  6.2 0.0 copy-start.17
  6.2 2.1 %collective-permute-start.2 = (f32[6,8,256]{2,1,0:T(8,128)S(1)}, f32[6,8,256]{2,1,0:T(8,128)S(1)}, u32[]{:S(2)}, u32[]{:S(2)}) collective-permute-start(f32[6,8,256]{2,1,0:T(8,128)S(1)} %get-tuple-element.36), channel_id=1, source_target_pairs={{0,1},{1,2},{2,3},{3,4},{4,5},{5,6},{6,7},{7,0},{8,9},{9,10},{10,1... | collective-permute-start | bytes 147464 | tf_op jit(solution)/shard_map/ppermute | solution.py:1162
  8.3 3.1 %collective-permute-start.3 = (f32[6,8,256]{2,1,0:T(8,128)S(1)}, f32[6,8,256]{2,1,0:T(8,128)S(1)}, u32[]{:S(2)}, u32[]{:S(2)}) collective-permute-start(f32[6,8,256]{2,1,0:T(8,128)S(1)} %get-tuple-element.37), channel_id=1, source_target_pairs={{0,7},{1,0},{2,1},{3,2},{4,3},{5,4},{6,5},{7,6},{8,15},{9,8},{10,9... | collective-permute-start | bytes 147464 | tf_op jit(solution)/shard_map/ppermute | solution.py:1162
  11.4 0.0 slice-done
  11.4 0.0 slice-done.1
  11.4 0.0 copy-done.4
  11.4 0.0 copy-done.11
  11.4 0.0 copy-done.12
  11.4 0.0 copy-done.13
  11.4 0.0 copy-done.14
  11.4 0.0 copy-start.7
  11.5 0.0 copy-start.9
  11.5 0.0 copy-start.15
  11.5 0.0 copy-start.16
  11.5 2.8 %shard_map.255 = (f32[1088,128]{1,0:T(8,128)S(1)}, f32[4,256]{1,0:T(4,128)S(1)}, bf16[64,256]{1,0:T(8,128)(2,1)S(1)}, f32[8,256,256]{2,1,0:T(8,128)S(1)}, bf16[256,1024]{1,0:T(8,128)(2,1)S(1)}) custom-call(f32[2,32]{1,0:T(2,128)S(1)} %bitcast.28, f32[2,8,4,32,1024]{4,3,2,1,0:T(8,128)S(1)} %bitcast.18, f32[32,32]{1,0:T(8,128)S(1)} %copy-done.11, ...), custom_call_target="tpu_custom_call" | custom-call | flops 1073741824 | bytes 8388608 | tf_op jit(solution)/shard_map/pallas_call | solution.py:1168
  14.3 0.0 collective-permute-done.2.low_ref
  14.3 0.0 collective-permute-done.3.high_ref
  14.3 0.8 shard_map.256
  15.1 21.6 %all_to_all.32 = f32[544,2,128]{2,1,0:T(2,128)S(1)} all-to-all(f32[544,2,128]{2,1,0:T(2,128)S(1)} %bitcast.22), channel_id=1, replica_groups=mesh['gx'=4,'gy'=8] {'gy','gx'}, dimensions={0} | all-to-all | bytes 1114112 | tf_op jit(solution)/shard_map/all_to_all | solution.py:1121
  36.8 0.0 copy-done
  36.8 1.9 %shard_map.257 = (f32[32,128]{1,0:T(8,128)S(1)}, f32[1024,128]{1,0:T(8,128)S(1)}, bf16[8,256,128]{2,1,0:T(8,128)(2,1)S(1)}, bf16[8,32,256]{2,1,0:T(8,128)(2,1)S(1)}) custom-call(f32[1088,128]{1,0:T(8,128)S(1)} %bitcast.19, bf16[64,384]{1,0:T(8,128)(2,1)S(1)} %copy-done.8, bf16[384,128]{1,0:T(8,128)(2,1)S(1)} %copy-done.2, bf16[128,192]{1,0:T(8,128)(2,1)S(1)} %copy-done.6, ...), custom_call_target="tpu_custom_call" | custom-call | flops 100000000 | bytes 2000000 | tf_op jit(solution)/shard_map/pallas_call | solution.py:1205
  38.7 18.5 %all_to_all.33 = f32[32,32,128]{2,1,0:T(8,128)S(1)} all-to-all(f32[32,32,128]{2,1,0:T(8,128)S(1)} %bitcast.23), channel_id=1, replica_groups=mesh['gx'=4,'gy'=8] {'gy','gx'}, dimensions={0} | all-to-all | bytes 1048576 | tf_op jit(solution)/shard_map/all_to_all | solution.py:1121
  57.3 2.6 %shard_map.258 = (f32[64,256]{1,0:T(8,128)S(1)}, f32[1024,128]{1,0:T(8,128)S(1)}) custom-call(f32[1024,128]{1,0:T(8,128)S(1)} %bitcast.24, bf16[8,256,128]{2,1,0:T(8,128)(2,1)S(1)} %get-tuple-element.43.table_ref, bf16[64,256]{1,0:T(8,128)(2,1)S(1)} %get-tuple-element.44.mix_ref, f32[8,256,256]{2,1,0:T(8,128)S(1)} %get-tuple-element.45.weight_ref, ...), custom_call_target="tpu_custom_call" | custom-call | flops 1000000000 | bytes 2000000 | tf_op jit(solution)/shard_map/pallas_call | solution.py:1233
  59.9 18.4 %all_to_all.34 = f32[32,32,128]{2,1,0:T(8,128)S(1)} all-to-all(f32[32,32,128]{2,1,0:T(8,128)S(1)} %bitcast.25), channel_id=1, replica_groups=mesh['gx'=4,'gy'=8] {'gy','gx'}, dimensions={0} | all-to-all | bytes 1048576 | tf_op jit(solution)/shard_map/all_to_all | solution.py:1121
  78.3 0.0 copy-done.7
  78.3 0.9 shard_map.259
  79.3 14.3 %all_to_all.35 = f32[288,2,128]{2,1,0:T(2,128)S(1)} all-to-all(f32[288,2,128]{2,1,0:T(2,128)S(1)} %bitcast.21), channel_id=1, replica_groups=mesh['gx'=4,'gy'=8] {'gy','gx'}, dimensions={0} | all-to-all | bytes 589824 | tf_op jit(solution)/shard_map/all_to_all | solution.py:1121
  93.6 3.9 %shard_map.260 = (f32[32,32]{1,0:T(8,128)}, f32[1,32]{1,0:T(1,128)}, f32[64,256]{1,0:T(8,128)}, f32[8,8,256]{2,1,0:T(8,128)}, f32[8,8,256]{2,1,0:T(8,128)}, /*index=5*/f32[2,8,4,32,1024]{4,3,2,1,0:T(8,128)}) custom-call(f32[576,128]{1,0:T(8,128)S(1)} %bitcast.26, f32[2,32]{1,0:T(2,128)S(1)} %bitcast.29, f32[64,256]{1,0:T(8,128)S(1)} %get-tuple-element.50.predicted_ref, ...), custom_call_target="tpu_custom_call" | custom-call | flops 1073741824 | bytes 8388608 | tf_op jit(solution)/shard_map/pallas_call | solution.py:1253
  (14 shorter events, 0.1 us)
Async XLA Ops:
  1.6 9.8 %slice-start = ((s8[8388608]{0:T(1024)(128)(4,1)}), s8[4194304]{0:T(1024)(128)(4,1)S(1)}, s32[]{:S(2)}) async-start(s8[8388608]{0:T(1024)(128)(4,1)} %bitcast.17), calls=%async_computation.4 | async-start | bytes 8388608
  1.6 9.8 %slice-start.1 = ((s8[8388608]{0:T(1024)(128)(4,1)}), s8[4194304]{0:T(1024)(128)(4,1)S(1)}, s32[]{:S(2)}) async-start(s8[8388608]{0:T(1024)(128)(4,1)} %bitcast.17), calls=%async_computation.5 | async-start | bytes 8388608
  1.6 9.8 %copy-start.4 = (f32[8,8,256]{2,1,0:T(8,128)S(1)}, f32[8,8,256]{2,1,0:T(8,128)}, u32[]{:S(2)}) copy-start(f32[8,8,256]{2,1,0:T(8,128)} %param.30) | copy-start | bytes 196612
  1.6 9.8 %copy-start.11 = (f32[32,32]{1,0:T(8,128)S(1)}, f32[32,32]{1,0:T(8,128)}, u32[]{:S(2)}) copy-start(f32[32,32]{1,0:T(8,128)} %local_ref.1) | copy-start | bytes 12292
  1.6 9.8 %copy-start.12 = (f32[32,2]{0,1:T(2,128)S(1)}, f32[32,2]{0,1:T(2,128)}, u32[]{:S(2)}) copy-start(f32[32,2]{0,1:T(2,128)} %param.25) | copy-start | bytes 772
  1.6 9.8 %copy-start.13 = (f32[32]{0:T(128)S(1)}, f32[32]{0:T(128)}, u32[]{:S(2)}) copy-start(f32[32]{0:T(128)} %param.28) | copy-start | bytes 388
  1.6 9.8 %copy-start.14 = (f32[32]{0:T(128)S(1)}, f32[32]{0:T(128)}, u32[]{:S(2)}) copy-start(f32[32]{0:T(128)} %param.29) | copy-start | bytes 388
  1.7 4.1 %collective-permute-start = (f32[5,8,256]{2,1,0:T(8,128)S(1)}, f32[5,8,256]{2,1,0:T(8,128)S(1)}, u32[]{:S(2)}, u32[]{:S(2)}) collective-permute-start(f32[5,8,256]{2,1,0:T(8,128)S(1)} %get-tuple-element.34), channel_id=1, source_target_pairs={{0,8},{8,16},{16,24},{24,0},{1,9},{9,17},{17,25},{25,1},{2,10},{10... | collective-permute-start | bytes 122888 | tf_op jit(solution)/shard_map/ppermute | solution.py:1162
  2.2 3.9 %collective-permute-start.1 = (f32[5,8,256]{2,1,0:T(8,128)S(1)}, f32[5,8,256]{2,1,0:T(8,128)S(1)}, u32[]{:S(2)}, u32[]{:S(2)}) collective-permute-start(f32[5,8,256]{2,1,0:T(8,128)S(1)} %get-tuple-element.35), channel_id=1, source_target_pairs={{0,24},{8,0},{16,8},{24,16},{1,25},{9,1},{17,9},{25,17},{2,26},{10... | collective-permute-start | bytes 122888 | tf_op jit(solution)/shard_map/ppermute | solution.py:1162
  6.1 8.2 %copy-start.3 = (bf16[64,768]{1,0:T(8,128)(2,1)S(1)}, bf16[64,768]{1,0:T(8,128)(2,1)}, u32[]{:S(2)}) copy-start(bf16[64,768]{1,0:T(8,128)(2,1)} %constant.26.clone.table_ref) | copy-start | bytes 294916
  6.1 30.7 %copy-start = (bf16[512,128]{1,0:T(8,128)(2,1)S(1)}, bf16[512,128]{1,0:T(8,128)(2,1)}, u32[]{:S(2)}) copy-start(bf16[512,128]{1,0:T(8,128)(2,1)} %constant.33.clone.gather_ref) | copy-start | bytes 393220
  6.1 30.7 %copy-start.1 = (bf16[256,256]{1,0:T(8,128)(2,1)S(1)}, bf16[256,256]{1,0:T(8,128)(2,1)}, u32[]{:S(2)}) copy-start(bf16[256,256]{1,0:T(8,128)(2,1)} %constant.32.clone.chosen_ref) | copy-start | bytes 393220
  6.1 30.7 %copy-start.2 = (bf16[384,128]{1,0:T(8,128)(2,1)S(1)}, bf16[384,128]{1,0:T(8,128)(2,1)}, u32[]{:S(2)}) copy-start(bf16[384,128]{1,0:T(8,128)(2,1)} %constant.28.clone.x_in_ref) | copy-start | bytes 294916
  6.2 30.6 %copy-start.5 = (bf16[128,256]{1,0:T(8,128)(2,1)S(1)}, bf16[128,256]{1,0:T(8,128)(2,1)}, u32[]{:S(2)}) copy-start(bf16[128,256]{1,0:T(8,128)(2,1)} %constant.31.clone.forth_ref) | copy-start | bytes 196612
  6.2 30.6 %copy-start.6 = (bf16[128,192]{1,0:T(8,128)(2,1)S(1)}, bf16[128,192]{1,0:T(8,128)(2,1)}, u32[]{:S(2)}) copy-start(bf16[128,192]{1,0:T(8,128)(2,1)} %constant.29.clone.y_out_ref) | copy-start | bytes 147460
  6.2 30.6 %copy-start.8 = (bf16[64,384]{1,0:T(8,128)(2,1)S(1)}, bf16[64,384]{1,0:T(8,128)(2,1)}, u32[]{:S(2)}) copy-start(bf16[64,384]{1,0:T(8,128)(2,1)} %constant.27.clone.y_in_ref) | copy-start | bytes 147460
  6.2 30.6 %copy-start.10 = (bf16[64,192]{1,0:T(8,128)(2,1)S(1)}, bf16[64,192]{1,0:T(8,128)(2,1)}, u32[]{:S(2)}) copy-start(bf16[64,192]{1,0:T(8,128)(2,1)} %constant.30.clone.x_out_ref) | copy-start | bytes 73732
  6.2 51.1 %copy-start.17 = (bf16[256,128]{1,0:T(8,128)(2,1)S(1)}, bf16[256,128]{1,0:T(8,128)(2,1)}, u32[]{:S(2)}) copy-start(bf16[256,128]{1,0:T(8,128)(2,1)} %constant.34.clone.back_ref) | copy-start | bytes 196612
  6.2 8.0 %collective-permute-start.2 = (f32[6,8,256]{2,1,0:T(8,128)S(1)}, f32[6,8,256]{2,1,0:T(8,128)S(1)}, u32[]{:S(2)}, u32[]{:S(2)}) collective-permute-start(f32[6,8,256]{2,1,0:T(8,128)S(1)} %get-tuple-element.36), channel_id=1, source_target_pairs={{0,1},{1,2},{2,3},{3,4},{4,5},{5,6},{6,7},{7,0},{8,9},{9,10},{10,1... | collective-permute-start | bytes 147464 | tf_op jit(solution)/shard_map/ppermute | solution.py:1162
  8.3 6.0 %collective-permute-start.3 = (f32[6,8,256]{2,1,0:T(8,128)S(1)}, f32[6,8,256]{2,1,0:T(8,128)S(1)}, u32[]{:S(2)}, u32[]{:S(2)}) collective-permute-start(f32[6,8,256]{2,1,0:T(8,128)S(1)} %get-tuple-element.37), channel_id=1, source_target_pairs={{0,7},{1,0},{2,1},{3,2},{4,3},{5,4},{6,5},{7,6},{8,15},{9,8},{10,9... | collective-permute-start | bytes 147464 | tf_op jit(solution)/shard_map/ppermute | solution.py:1162
  11.4 66.9 %copy-start.7 = (bf16[64,384]{1,0:T(8,128)(2,1)S(1)}, bf16[64,384]{1,0:T(8,128)(2,1)}, u32[]{:S(2)}) copy-start(bf16[64,384]{1,0:T(8,128)(2,1)} %constant.36.clone.y_in_ref) | copy-start | bytes 147460
  11.5 66.9 %copy-start.9 = (bf16[64,192]{1,0:T(8,128)(2,1)S(1)}, bf16[64,192]{1,0:T(8,128)(2,1)}, u32[]{:S(2)}) copy-start(bf16[64,192]{1,0:T(8,128)(2,1)} %constant.35.clone.x_in_ref) | copy-start | bytes 73732
  11.5 82.1 %copy-start.15 = (bf16[256,512]{1,0:T(8,128)(2,1)S(1)}, bf16[256,512]{1,0:T(8,128)(2,1)}, u32[]{:S(2)}) copy-start(bf16[256,512]{1,0:T(8,128)(2,1)} %constant.37.clone.repeat_ref) | copy-start | bytes 786436
  11.5 82.1 %copy-start.16 = (bf16[256,256]{1,0:T(8,128)(2,1)S(1)}, bf16[256,256]{1,0:T(8,128)(2,1)}, u32[]{:S(2)}) copy-start(bf16[256,256]{1,0:T(8,128)(2,1)} %constant.38.clone.spread_ref) | copy-start | bytes 393220
